TPU v7x, 32 devices: a whole 2x2x4 slice. The times are simulated.
32 devices in a mesh: hour: 2 (over x), rcpt: 16 (over z, y, core).
Axes of the slice: x: 2, y: 2, z: 4, core: 2. Of those that a mesh axis runs over, the one named last changes fastest.
Arguments:
- flux: float32 [192, 4096], P('hour', 'rcpt'), may hold values from -6 to 6
- footprint: bfloat16 [4096, 8, 4096], P(('hour', 'rcpt')), may hold values from -0.0625 to 0.0625
- tile_mask: int32 [256, 8, 32], P(('hour', 'rcpt')), may hold values 0 or 1
- rec_hour: int32 [4096], P(('hour', 'rcpt')), may hold values from 0 to 95
- observed: float32 [4096], P(('hour', 'rcpt')), may hold values from -6 to 6
- obs_weight: float32 [4096], P(('hour', 'rcpt')), may hold values from 0.2 to 5
- site_count: int32 [32], P(('hour', 'rcpt')), may hold values from 1 to 128, 2560 in all
Outputs:
- gradient: float32 [192, 4096], P('hour', 'rcpt')
- mismatch: float32 [4096], P(('hour', 'rcpt'))
Inputs may be any that keep to these rules, and one draw needn't show every extreme that they name: `site_count`: at most 128 live receptors in a shard; some shard has exactly 128.
All inputs are finite; a program needn't handle non-finite values. No bound on the sum of `tile_mask` on one device may be relied on, other than what follows from the above.
Results may differ from a plain program's by a relative error of at most 0.0036.
Values may be sent and summed in bfloat16 or wider, within the bound.
No kernel may reach another device: no remote copies, remote signals or barrier semaphores. Data moves between devices by JAX's collectives and lax.ppermute only.
A program may use at most 64 MiB of HBM per device.

v0:
```python
import jax
import jax.numpy as jnp
from jax import lax
from jax.sharding import PartitionSpec as P

TILE = 128


def from_behind(block, axis, distance):
    devices = range(lax.axis_size(axis))
    route = [(i - distance, i) for i in devices if i - distance in devices]
    return lax.ppermute(block, axis, route)


def per_device(flux, footprint, tile_mask, rec_hour, observed, obs_weight, site_count):
    hours_block, own_cells = flux.shape
    rows, lags, cells = footprint.shape
    width = hours_block + lags - 1
    blocks = tile_mask.shape[0]
    block_rows = rows // blocks
    tiles = cells // TILE
    low = flux.astype(jnp.bfloat16)
    full = lax.all_gather(low, "rcpt", axis=1, tiled=True)
    rim = from_behind(full[hours_block - (lags - 1) :], "hour", 1)
    window = jnp.concatenate([rim, full], axis=0)
    shaped = footprint.reshape(blocks, block_rows, lags, tiles, TILE)
    shaped = shaped * tile_mask.astype(jnp.bfloat16)[:, None, :, :, None]
    masked = shaped.reshape(rows, lags, cells)
    lag_index = jnp.arange(lags, dtype=jnp.int32)
    slots = rec_hour[:, None] - lag_index[None, :] + lags - 1
    live = (jnp.arange(rows, dtype=jnp.int32) < site_count[0]).astype(jnp.float32)
    columns = jnp.arange(width, dtype=jnp.int32)
    select = (slots[:, :, None] == columns[None, None, :]).astype(jnp.bfloat16)
    picked = jnp.einsum("rlw,wc->rlc", select, window, preferred_element_type=jnp.float32).astype(
        jnp.bfloat16
    )
    model = jnp.einsum("rlc,rlc->r", masked, picked, preferred_element_type=jnp.float32)
    mism = live * obs_weight * (model - observed)
    spread = select * mism.astype(jnp.bfloat16)[:, None, None]
    part = jnp.einsum("rlw,rlc->wc", spread, masked, preferred_element_type=jnp.float32)
    owned = lax.psum_scatter(part, "rcpt", scatter_dimension=1, tiled=True)
    back = from_behind(owned[: lags - 1], "hour", -1)
    gradient = owned[lags - 1 :] + jnp.pad(back, ((hours_block - (lags - 1), 0), (0, 0)))
    return (gradient, mism)


def solution(mesh):
    placed = (
        P("hour", "rcpt"),
        P(("hour", "rcpt"), None, None),
        P(("hour", "rcpt"), None, None),
        P(("hour", "rcpt")),
        P(("hour", "rcpt")),
        P(("hour", "rcpt")),
        P(("hour", "rcpt")),
    )
    return jax.shard_map(
        per_device,
        mesh=mesh,
        in_specs=placed,
        out_specs=(P("hour", "rcpt"), P(("hour", "rcpt"))),
        check_vma=False,
    )
```

profile of v0, /device:TPU:0, one launch (start us, length us, event | category | flops | bytes accessed | tf_op | source)
XLA Modules:
  0.0 135.7 jit_solution(17550529824297311136)
XLA Ops:
  7.2 0.0 reduce-scatter.2.cloned.1.call-start
  7.2 0.9 convert_element_type.17
  8.1 25.4 %all_gather.3 = bf16[96,4096]{1,0:T(8,128)(2,1)S(1)} all-gather(bf16[96,256]{1,0:T(8,128)(2,1)S(1)} %convert_element_type.17), channel_id=1, replica_groups=mesh['hour'=2,'rcpt'=16] {'rcpt'}, dimensions={1}, use_global_device_ids=true | all-gather | bytes 835584 | tf_op jit(solution)/shard_map/all_gather | solution.py:23
  33.6 3.4 %collective-permute-start = (bf16[7,4096]{1,0:T(8,128)(2,1)S(1)}, bf16[7,4096]{1,0:T(8,128)(2,1)S(1)}, u32[]{:S(2)}, u32[]{:S(2)}) collective-permute-start(bf16[7,4096]{1,0:T(8,128)(2,1)S(1)} %slice.12), channel_id=1, source_target_pairs={{0,16},{1,17},{2,18},{3,19},{4,20},{5,21},{6,22},{7,23},{8,24},{9,... | collective-permute-start | bytes 172040 | tf_op jit(solution)/shard_map/ppermute | solution.py:12
  37.0 0.7 subtract_add_fusion
  37.6 0.1 iota_compare_fusion
  37.7 0.8 convert_element_type.16
  38.5 0.1 copy.9
  38.6 0.3 copy.11
  38.9 0.0 copy-start
  39.7 2.1 %mul.26 = bf16[8,16,8,32,128]{4,2,3,1,0:T(8,128)(2,1)S(1)} broadcast(bf16[8,8,32]{1,2,0:T(8,128)(2,1)S(1)} %copy.9), dimensions={0,2,3} | broadcast | bytes 8392704 | tf_op jit(solution)/shard_map/mul | solution.py:27
  41.8 0.4 copy-done
  42.3 5.0 %mul.28 = bf16[128,8,4096]{2,1,0:T(8,128)(2,1)} multiply(bf16[128,8,4096]{2,1,0:T(8,128)(2,1)S(1)} %copy-done, bf16[128,8,4096]{2,1,0:T(8,128)(2,1)S(1)} %bitcast.13) | non-fusion elementwise | flops 4194304 | bytes 25165824 | tf_op jit(solution)/shard_map/mul | solution.py:27
  47.3 0.0 copy-start.2
  47.3 0.0 copy-start.3
  47.3 0.0 copy-start.1
  47.3 0.0 collective-permute-done
  47.3 6.5 %fusion = f32[128]{0:T(128)S(1)} fusion(bf16[128,8,4096]{2,1,0:T(8,128)(2,1)} %mul.28, pred[128,8,103]{2,1,0:T(8,128)(4,1)S(1)} %copy.11, bf16[96,4096]{1,0:T(8,128)(2,1)S(1)} %all_gather.3, bf16[7,4096]{1,0:T(8,128)(2,1)S(1)} %collective-permute-done), kind=kOutput, calls=%fused_computation.1 | convolution fusion | flops 886685568 | bytes 9338368 | tf_op jit(solution)/shard_map/rlw,wc->rlc/dot_general | solution.py:34
  53.8 0.0 copy-done.2
  53.8 0.0 copy-done.3
  53.8 0.5 fusion.14
  54.3 0.0 copy-done.1
  54.3 10.6 %fusion.3 = f32[103,4096]{1,0:T(8,128)} fusion(bf16[128,8,4096]{2,1,0:T(8,128)(2,1)S(1)} %copy-done.1, bf16[128]{0:T(256)(128)(2,1)S(1)} %get-tuple-element.2, s32[128,8]{0,1:T(8,128)S(1)} %subtract_add_fusion), kind=kOutput, calls=%fused_computation.4 | convolution fusion | flops 864237568 | bytes 10080512 | tf_op jit(solution)/shard_map/rlw,rlc->wc/dot_general | solution.py:40
  65.0 0.0 reduce-scatter.2.cloned.1.call-update
  65.0 56.1 %reduce-scatter.2.cloned.1.call-done = f32[103,256]{1,0:T(8,128)} async-done(((f32[103,4096]{1,0:T(8,128)}), f32[103,256]{1,0:T(8,128)}) %reduce-scatter.2.cloned.1.call-update) | async-done | bytes 105488 | tf_op jit(solution)/shard_map/reduce_scatter | solution.py:41
  121.1 0.7 slice.14
  121.8 1.3 collective-permute-start.1
  123.1 4.2 %collective-permute-done.1 = f32[7,256]{1,0:T(8,128)S(1)} collective-permute-done((f32[7,256]{1,0:T(8,128)S(1)}, f32[7,256]{1,0:T(8,128)S(1)}, u32[]{:S(2)}, u32[]{:S(2)}) %collective-permute-start.1) | collective-permute-done | bytes 7200 | tf_op jit(solution)/shard_map/ppermute | solution.py:12
  127.3 1.5 %slice_add_fusion = f32[96,256]{1,0:T(8,128)} fusion(f32[103,256]{1,0:T(8,128)} %reduce-scatter.2.cloned.1.call-done, f32[7,256]{1,0:T(8,128)S(1)} %collective-permute-done.1), kind=kLoop, calls=%fused_computation.12 | loop fusion | flops 24576 | bytes 203776 | tf_op jit(solution)/shard_map/add | solution.py:43
  (1 shorter events, 0.0 us)
Async XLA Ops:
  7.2 113.9 %reduce-scatter.2.cloned.1.call-start = ((), (), s32[]{:S(2)}) async-start(), calls=%async_computation.1 | async-start | bytes 1810432 | tf_op jit(solution)/shard_map/reduce_scatter | solution.py:41
  33.6 13.7 %collective-permute-start = (bf16[7,4096]{1,0:T(8,128)(2,1)S(1)}, bf16[7,4096]{1,0:T(8,128)(2,1)S(1)}, u32[]{:S(2)}, u32[]{:S(2)}) collective-permute-start(bf16[7,4096]{1,0:T(8,128)(2,1)S(1)} %slice.12), channel_id=1, source_target_pairs={{0,16},{1,17},{2,18},{3,19},{4,20},{5,21},{6,22},{7,23},{8,24},{9,... | collective-permute-start | bytes 172040 | tf_op jit(solution)/shard_map/ppermute | solution.py:12
  38.9 3.4 %copy-start = (bf16[128,8,4096]{2,1,0:T(8,128)(2,1)S(1)}, bf16[128,8,4096]{2,1,0:T(8,128)(2,1)}, u32[]{:S(2)}) copy-start(bf16[128,8,4096]{2,1,0:T(8,128)(2,1)} %param.8) | copy-start | bytes 25165828
  47.3 6.5 %copy-start.2 = (f32[128]{0:T(128)S(1)}, f32[128]{0:T(128)}, u32[]{:S(2)}) copy-start(f32[128]{0:T(128)} %param.11) | copy-start | bytes 1540
  47.3 6.5 %copy-start.3 = (f32[128]{0:T(128)S(1)}, f32[128]{0:T(128)}, u32[]{:S(2)}) copy-start(f32[128]{0:T(128)} %param.12) | copy-start | bytes 1540
  47.3 7.0 %copy-start.1 = (bf16[128,8,4096]{2,1,0:T(8,128)(2,1)S(1)}, bf16[128,8,4096]{2,1,0:T(8,128)(2,1)}, u32[]{:S(2)}) copy-start(bf16[128,8,4096]{2,1,0:T(8,128)(2,1)} %mul.28) | copy-start | bytes 25165828
  121.8 5.5 %collective-permute-start.1 = (f32[7,256]{1,0:T(8,128)S(1)}, f32[7,256]{1,0:T(8,128)S(1)}, u32[]{:S(2)}, u32[]{:S(2)}) collective-permute-start(f32[7,256]{1,0:T(8,128)S(1)} %slice.14), channel_id=1, source_target_pairs={{16,0},{17,1},{18,2},{19,3},{20,4},{21,5},{22,6},{23,7},{24,8},{25... | collective-permute-start | bytes 21512 | tf_op jit(solution)/shard_map/ppermute | solution.py:12
Sparse Core Ops, SparseCore 0:
  65.1 55.9 reduce-scatter.1
where the time goes:
time: 136 us
  waiting for transfers between devices  60.4 us (44%)
  blocking collectives  25.4 us (19%)
  matrix products  17.1 us (13%)
  between operations  14.9 us (11%)
  other arithmetic  9.5 us (7%)
  starting transfers between devices  4.72 us (3%)
  local copies, waits for them, and re-layouts  3.69 us (3%)
    reduce_scatter x1, waiting for transfers between devices, per_device(): owned = lax.psum_scatter(part, 'rcpt', scatter_dimension=1, tiled=True)  56.1 us
    all_gather x1, blocking collectives, per_device(): full = lax.all_gather(low, 'rcpt', axis=1, tiled=True)  25.4 us
    dot_general x1, matrix products, per_device(): jnp.einsum('rlw,rlc->wc', spread, masked, preferred_element_type=jnp.floa...  10.6 us
    dot_general x1, matrix products, per_device(): jnp.einsum('rlw,wc->rlc', select, window, preferred_element_type=jnp.floa...  6.48 us
    mul x1, other arithmetic, per_device(): shaped = shaped * tile_mask.astype(jnp.bfloat16)[:, None, :, :, None]  5.04 us
    ppermute x2, starting transfers between devices, from_behind(): return lax.ppermute(block, axis, route)  4.68 us
    ppermute x2, waiting for transfers between devices, from_behind(): return lax.ppermute(block, axis, route)  4.25 us
  transfers between devices with their start and end apart: 3, of which 2 were waited for; matrix products, arithmetic and copies ran while one was open for 7% of the time, Pallas kernels for 0%

commit v1 on v0

v1 whole, which is shorter than its diff:
```python
import functools

import jax
import jax.numpy as jnp
from jax import lax
from jax.experimental import pallas as pl
from jax.experimental.pallas import tpu as pltpu
from jax.sharding import PartitionSpec as P

RIM = 8
F32 = jnp.float32
BF16 = jnp.bfloat16
VMEM_LIMIT = 40 * 1024 * 1024


def swap(block, bit):
    devices = range(lax.axis_size("rcpt"))
    return lax.ppermute(block, "rcpt", [(i, i ^ bit) for i in devices])


def turn(block, distance):
    size = lax.axis_size("hour")
    return lax.ppermute(block, "hour", [(i, (i + distance) % size) for i in range(size)])


def expander(rows, lags, dtype):
    shape = (rows, rows * lags)
    row = lax.broadcasted_iota(jnp.int32, shape, 0)
    column = lax.broadcasted_iota(jnp.int32, shape, 1)
    first = row * lags
    return ((column >= first) & (column < first + lags)).astype(dtype)


def prepare_kernel(me_ref, foot_ref, mask_ref, hour_ref, masked_ref, select_ref):
    step = pl.program_id(0)
    blocks, lags, tiles = mask_ref.shape
    depth, own = foot_ref.shape
    width = select_ref.shape[0]
    rows = depth // lags
    group = 2 * lags
    tile = own * pl.num_programs(0) // tiles

    @pl.when(step == 0)
    def _():
        hours = jnp.broadcast_to(hour_ref[...].astype(F32), (8, rows)).astype(BF16)
        spread = jnp.dot(hours, expander(rows, lags, BF16), preferred_element_type=F32)
        column = lax.broadcasted_iota(jnp.int32, (1, depth), 1)
        slot = spread[:1].astype(jnp.int32) - lax.rem(column, lags) + RIM
        line = lax.broadcasted_iota(jnp.int32, (width, depth), 0)
        select_ref[...] = (line == slot).astype(F32).astype(BF16)

    device = me_ref[0] ^ step
    mask = mask_ref[...].astype(F32)
    twice = jnp.broadcast_to(mask[:, None], (blocks, 2, lags, tiles)).reshape(blocks * group, tiles)
    per = own // tile
    shape = (tiles, own)
    wanted = device * per + lax.broadcasted_iota(jnp.int32, shape, 1) // tile
    widen = (lax.broadcasted_iota(jnp.int32, shape, 0) == wanted).astype(F32).astype(BF16)
    wide = jnp.dot(twice.astype(BF16), widen, preferred_element_type=F32).astype(BF16)
    part = depth // blocks
    for b in range(blocks):
        line = wide[b * group : (b + 1) * group]
        for j in range(part // group):
            at = pl.ds(b * part + j * group, group)
            masked_ref[0, at, :] = foot_ref[at, :] * line


def prepare(me, foot, mask, hour, devices, width):
    depth, cells = foot.shape
    own = cells // devices
    grid_spec = pltpu.PrefetchScalarGridSpec(
        num_scalar_prefetch=1,
        grid=(devices,),
        in_specs=[
            pl.BlockSpec((depth, own), lambda k, me: (0, me[0] ^ k)),
            pl.BlockSpec(mask.shape, lambda k, me: (0, 0, 0)),
            pl.BlockSpec(hour.shape, lambda k, me: (0, 0)),
        ],
        out_specs=[
            pl.BlockSpec((1, depth, own), lambda k, me: (k, 0, 0)),
            pl.BlockSpec((width, depth), lambda k, me: (0, 0)),
        ],
    )
    return pl.pallas_call(
        prepare_kernel,
        grid_spec=grid_spec,
        out_shape=[
            jax.ShapeDtypeStruct((devices, depth, own), BF16),
            jax.ShapeDtypeStruct((width, depth), BF16),
        ],
        cost_estimate=pl.CostEstimate(
            flops=depth * cells, bytes_accessed=4 * depth * cells, transcendentals=0
        ),
        name="prepare",
    )(me, foot, mask, hour)


def adjoint_kernel(devices, lags, *refs):
    chunks = refs[:devices]
    masked_ref, select_ref, obs_ref, weight_ref, count_ref = refs[devices : devices + 5]
    mism_ref, own_ref, other_ref = refs[devices + 5 : devices + 8]
    score_ref, spread_ref = refs[devices + 8 :]
    width, depth = score_ref.shape
    rows = depth // lags
    for k in range(devices):
        dims = (((1,), (1,)), ((), ()))
        term = lax.dot_general(chunks[k][...], masked_ref[k], dims, preferred_element_type=F32)
        if k == 0:
            score_ref[...] = term
        else:
            score_ref[...] += term
    chosen = score_ref[...] * select_ref[...].astype(F32)
    line = jnp.sum(chosen, axis=0, keepdims=True)
    belongs = expander(rows, lags, F32)
    model = lax.dot_general(
        jnp.broadcast_to(line, (8, depth)),
        belongs,
        (((1,), (1,)), ((), ())),
        precision=lax.Precision.HIGHEST,
        preferred_element_type=F32,
    )[:1]
    live = (lax.broadcasted_iota(jnp.int32, (1, rows), 1) < count_ref[0]).astype(F32)
    mism = live * weight_ref[...] * (model - obs_ref[...])
    mism_ref[...] = mism
    weighted = jnp.broadcast_to(mism, (8, rows)).astype(BF16)
    wide = jnp.dot(weighted, belongs.astype(BF16), preferred_element_type=F32)[:1]
    spread_ref[...] = (select_ref[...].astype(F32) * wide).astype(BF16)
    for k in range(1, devices, 2):
        part = jnp.dot(spread_ref[...], masked_ref[k], preferred_element_type=F32)
        other_ref[k // 2] = part.astype(BF16)
    for k in range(0, devices, 2):
        own_ref[k // 2] = jnp.dot(spread_ref[...], masked_ref[k], preferred_element_type=F32)


def adjoint(chunks, masked, select, obs, weight, count, lags):
    devices, depth, own = masked.shape
    width = select.shape[0]
    vmem = pl.BlockSpec(memory_space=pltpu.VMEM)
    half = devices // 2
    return pl.pallas_call(
        functools.partial(adjoint_kernel, devices, lags),
        in_specs=[vmem] * (devices + 4) + [pl.BlockSpec(memory_space=pltpu.SMEM)],
        out_specs=[vmem] * 3,
        out_shape=[
            jax.ShapeDtypeStruct(obs.shape, F32),
            jax.ShapeDtypeStruct((half, width, own), F32),
            jax.ShapeDtypeStruct((half, width, own), BF16),
        ],
        scratch_shapes=[pltpu.VMEM((width, depth), F32), pltpu.VMEM((width, depth), BF16)],
        compiler_params=pltpu.CompilerParams(vmem_limit_bytes=VMEM_LIMIT),
        name="adjoint",
    )(*chunks, masked, select, obs, weight, count)


def join_kernel(own_ref, came_ref, *outs):
    for k, out in enumerate(outs):
        total = own_ref[k] + came_ref[k].astype(F32)
        out[...] = total.astype(out.dtype)


def join(own, came, kept):
    half, width, columns = own.shape
    vmem = pl.BlockSpec(memory_space=pltpu.VMEM)
    return pl.pallas_call(
        join_kernel,
        in_specs=[vmem] * 2,
        out_specs=[vmem] * half,
        out_shape=[
            jax.ShapeDtypeStruct((width, columns), F32 if k in kept else BF16) for k in range(half)
        ],
        name="join",
    )(own, came)


def per_device(flux, footprint, tile_mask, rec_hour, observed, obs_weight, site_count):
    hours, own = flux.shape
    rows, lags, cells = footprint.shape
    devices = cells // own
    far = devices // 2
    near = range(2, far, 2)
    width = hours + RIM
    here = lax.axis_index("hour")
    last = lax.axis_size("hour") - 1
    me = lax.axis_index("rcpt").astype(jnp.int32).reshape(1)

    low = flux.astype(BF16)
    rim = turn(low[hours - RIM :], 1)
    rim = jnp.where(here > 0, rim, jnp.zeros_like(rim))
    window = jnp.concatenate([rim, low], axis=0)

    masked, select = prepare(
        me, footprint.reshape(rows * lags, cells), tile_mask, rec_hour.reshape(1, rows), devices, width
    )

    got = {0: window, far: swap(window, far)}
    for k in near:
        got[k] = swap(window, k)
    for k in near:
        got[far ^ k] = swap(got[far], k)
    for k in range(0, devices, 2):
        got[k ^ 1] = swap(got[k], 1)

    mism, mine, other = adjoint(
        [got[k] for k in range(devices)],
        masked,
        select,
        observed.reshape(1, rows),
        obs_weight.reshape(1, rows),
        site_count,
        lags,
    )
    sums = join(mine, swap(other, 1), (0, far // 2))
    sums = {2 * i: s for i, s in enumerate(sums)}
    across = [swap(sums[far ^ k], k) for k in near]
    close = [swap(sums[k], k) for k in near]
    relay = sums[far]
    for piece in across:
        relay = relay + piece.astype(F32)
    total = sums[0]
    for piece in close + [swap(relay.astype(BF16), far)]:
        total = total + piece.astype(F32)
    back = turn(total[:RIM], -1)
    back = jnp.where(here < last, back, jnp.zeros_like(back))
    gradient = total[RIM:] + jnp.pad(back, ((hours - RIM, 0), (0, 0)))
    return (gradient, mism.reshape(rows))


def solution(mesh):
    placed = (
        P("hour", "rcpt"),
        P(("hour", "rcpt"), None, None),
        P(("hour", "rcpt"), None, None),
        P(("hour", "rcpt")),
        P(("hour", "rcpt")),
        P(("hour", "rcpt")),
        P(("hour", "rcpt")),
    )
    return jax.shard_map(
        per_device,
        mesh=mesh,
        in_specs=placed,
        out_specs=(P("hour", "rcpt"), P(("hour", "rcpt"))),
        check_vma=False,
    )
```

time: 136 us -> 69.4 us (0.51)
  waiting for transfers between devices: 60.4 us -> 10.6 us
  blocking collectives: 25.4 us -> 0 us
  starting transfers between devices: 4.72 us -> 26.8 us
  Pallas kernels: 0 us -> 20.5 us
  matrix products: 17.1 us -> 0 us
  between operations: 14.9 us -> 1.41 us
  other arithmetic: 9.5 us -> 3.45 us
  local copies, waits for them, and re-layouts: 3.69 us -> 6 us
    reduce_scatter x1 -> x0, waiting for transfers between devices: 56.1 us -> none  [per_device(): owned = lax.psum_scatter(part, 'rcpt', scatter_dimension=1, tiled=True)]
    all_gather x1 -> x0, blocking collectives: 25.4 us -> none  [per_device(): full = lax.all_gather(low, 'rcpt', axis=1, tiled=True)]
    ppermute x2 -> x25, starting transfers between devices: 4.68 us -> 26.8 us  [the longest x23 22.2 us: swap(): return lax.ppermute(block, 'rcpt', [(i, i ^ bit) for i in devices])]
    pallas_call x0 -> x3, Pallas kernels: none -> 20.5 us  [the longest x1 13.2 us: prepare(): pl.pallas_call(prepare_kernel, grid_spec=grid_spec, out_shape=[jax.ShapeD...]
    dot_general x2 -> x0, matrix products: 17.1 us -> none  [the longest x1 10.6 us: per_device(): jnp.einsum('rlw,rlc->wc', spread, masked, preferred_element_type=jnp.floa...]
    ppermute x2 -> x25, waiting for transfers between devices: 4.25 us -> 10.6 us  [the longest x23 6.91 us: swap(): return lax.ppermute(block, 'rcpt', [(i, i ^ bit) for i in devices])]
    unnamed x8 -> x12, local copies, waits for them, and re-layouts: 0.45 us -> 6 us
    mul x1 -> x0, other arithmetic: 5.04 us -> none  [per_device(): shaped = shaped * tile_mask.astype(jnp.bfloat16)[:, None, :, :, None]]
  transfers between devices with their start and end apart: 3 -> 25, of which waited for: 2 -> 8; matrix products, arithmetic and copies ran while one was open for 7% -> 1% of each run, Pallas kernels for 0% -> 19%
where the time goes in v1:
time: 69.4 us; the launch traced here: 68.8 us
  starting transfers between devices  26.8 us (39%)
  Pallas kernels  20.5 us (30%)
  waiting for transfers between devices  10.6 us (15%)
  local copies, waits for them, and re-layouts  6 us (9%)
  other arithmetic  3.45 us (5%)
  between operations  1.41 us (2%)
    ppermute x23, starting transfers between devices, swap(): return lax.ppermute(block, 'rcpt', [(i, i ^ bit) for i in devices])  22.2 us
    pallas_call x1, Pallas kernels, prepare(): pl.pallas_call(prepare_kernel, grid_spec=grid_spec, out_shape=[jax.ShapeD...  13.2 us
    ppermute x23, waiting for transfers between devices, swap(): return lax.ppermute(block, 'rcpt', [(i, i ^ bit) for i in devices])  6.91 us
    unnamed x12, local copies, waits for them, and re-layouts  6 us
    pallas_call x1, Pallas kernels, adjoint(): pl.pallas_call(functools.partial(adjoint_kernel, devices, lags), in_specs...  5.24 us
    ppermute x2, starting transfers between devices, turn(): lax.ppermute(block, 'hour', [(i, (i + distance) % size) for i in range(si...  4.58 us
    ppermute x2, waiting for transfers between devices, turn(): lax.ppermute(block, 'hour', [(i, (i + distance) % size) for i in range(si...  3.73 us
    pallas_call x1, Pallas kernels, join(): pl.pallas_call(join_kernel, in_specs=[vmem] * 2, out_specs=[vmem] * half,...  2.05 us
  transfers between devices with their start and end apart: 25, of which 8 were waited for; matrix products, arithmetic and copies ran while one was open for 1% of the time, Pallas kernels for 19%

profile of v1, /device:TPU:0, one launch (start us, length us, event | category | flops | bytes accessed | tf_op | source)
XLA Modules:
  0.0 68.8 jit_solution(5689097742190196547)
XLA Ops:
  0.6 0.9 %convert_element_type.29 = bf16[96,256]{1,0:T(8,128)(2,1)S(1)} convert(f32[96,256]{1,0:T(8,128)} %param.7) | non-fusion elementwise | flops 24576 | bytes 147456 | tf_op jit(solution)/shard_map/convert_element_type | solution.py:186
  1.6 3.0 %collective-permute-start = (bf16[8,256]{1,0:T(8,128)(2,1)S(1)}, bf16[8,256]{1,0:T(8,128)(2,1)S(1)}, u32[]{:S(2)}, u32[]{:S(2)}) collective-permute-start(bf16[8,256]{1,0:T(8,128)(2,1)S(1)} %slice.12), channel_id=1, source_target_pairs={{0,16},{16,0},{1,17},{17,1},{2,18},{18,2},{3,19},{19,3},{4,20},{20... | collective-permute-start | bytes 12296 | tf_op jit(solution)/shard_map/ppermute | solution.py:23
  4.6 1.6 %collective-permute-done = bf16[8,256]{1,0:T(8,128)(2,1)S(1)} collective-permute-done((bf16[8,256]{1,0:T(8,128)(2,1)S(1)}, bf16[8,256]{1,0:T(8,128)(2,1)S(1)}, u32[]{:S(2)}, u32[]{:S(2)}) %collective-permute-start) | collective-permute-done | bytes 4128 | tf_op jit(solution)/shard_map/ppermute | solution.py:23
  6.2 3.2 %collective-permute-start.8 = (bf16[104,256]{1,0:T(8,128)(2,1)S(1)}, bf16[104,256]{1,0:T(8,128)(2,1)S(1)}, u32[]{:S(2)}, u32[]{:S(2)}) collective-permute-start(bf16[104,256]{1,0:T(8,128)(2,1)S(1)} %pad_maximum_fusion.refs_0_), channel_id=1, source_target_pairs={{0,8},{1,9},{2,10},{3,11},{4,12},{5,13},{6,14},{7,15},{8,0},{9,1},... | collective-permute-start | bytes 159752 | tf_op jit(solution)/shard_map/ppermute | solution.py:18
  9.4 2.5 %collective-permute-start.6 = (bf16[104,256]{1,0:T(8,128)(2,1)S(1)}, bf16[104,256]{1,0:T(8,128)(2,1)S(1)}, u32[]{:S(2)}, u32[]{:S(2)}) collective-permute-start(bf16[104,256]{1,0:T(8,128)(2,1)S(1)} %pad_maximum_fusion.refs_0_), channel_id=1, source_target_pairs={{0,6},{1,7},{2,4},{3,5},{4,2},{5,3},{6,0},{7,1},{8,14},{9,15},{10,... | collective-permute-start | bytes 159752 | tf_op jit(solution)/shard_map/ppermute | solution.py:18
  12.9 2.5 %collective-permute-start.14 = (bf16[104,256]{1,0:T(8,128)(2,1)S(1)}, bf16[104,256]{1,0:T(8,128)(2,1)S(1)}, u32[]{:S(2)}, u32[]{:S(2)}) collective-permute-start(bf16[104,256]{1,0:T(8,128)(2,1)S(1)} %collective-permute-done.8.refs_8_), channel_id=1, source_target_pairs={{0,6},{1,7},{2,4},{3,5},{4,2},{5,3},{6,0},{7,1},{8,14},{9,15},{10,... | collective-permute-start | bytes 159752 | tf_op jit(solution)/shard_map/ppermute | solution.py:18
  15.4 0.6 collective-permute-start.12
  16.0 1.5 %collective-permute-start.10 = (bf16[104,256]{1,0:T(8,128)(2,1)S(1)}, bf16[104,256]{1,0:T(8,128)(2,1)S(1)}, u32[]{:S(2)}, u32[]{:S(2)}) collective-permute-start(bf16[104,256]{1,0:T(8,128)(2,1)S(1)} %collective-permute-done.8.refs_8_), channel_id=1, source_target_pairs={{0,2},{1,3},{2,0},{3,1},{4,6},{5,7},{6,4},{7,5},{8,10},{9,11},{10,... | collective-permute-start | bytes 159752 | tf_op jit(solution)/shard_map/ppermute | solution.py:18
  18.1 1.4 %collective-permute-done.12.refs_12_ = bf16[104,256]{1,0:T(8,128)(2,1)S(1)} collective-permute-done((bf16[104,256]{1,0:T(8,128)(2,1)S(1)}, bf16[104,256]{1,0:T(8,128)(2,1)S(1)}, u32[]{:S(2)}, u32[]{:S(2)}) %collective-permute-start.12) | collective-permute-done | bytes 53280 | tf_op jit(solution)/shard_map/ppermute | solution.py:18
  19.5 0.6 collective-permute-done.10.refs_10_
  21.4 13.2 %prepare.1 = (bf16[16,1024,256]{2,1,0:T(8,128)(2,1)}, bf16[104,1024]{1,0:T(8,128)(2,1)}) custom-call(s32[1]{0:T(128)} %bitcast.me_ref, bf16[1024,4096]{1,0:T(8,128)(2,1)} %bitcast.8, s32[8,8,32]{2,1,0:T(8,128)} %mask_ref.1, s32[1,128]{1,0:T(1,128)} %bitcast.9), custom_call_target="tpu_custom_call" | custom-call | flops 4194304 | bytes 16777216 | tf_op jit(solution)/shard_map/prepare/pallas_call | solution.py:84
  34.7 3.4 %copy-done = bf16[16,1024,256]{2,1,0:T(8,128)(2,1)S(1)} copy-done((bf16[16,1024,256]{2,1,0:T(8,128)(2,1)S(1)}, bf16[16,1024,256]{2,1,0:T(8,128)(2,1)}, u32[]{:S(2)}) %copy-start) | copy-done | bytes 8388632
  38.0 0.9 %copy-done.2 = bf16[104,1024]{1,0:T(8,128)(2,1)S(1)} copy-done((bf16[104,1024]{1,0:T(8,128)(2,1)S(1)}, bf16[104,1024]{1,0:T(8,128)(2,1)}, u32[]{:S(2)}) %copy-start.2) | copy-done | bytes 213016
  39.0 5.2 %adjoint.1 = (f32[1,128]{1,0:T(1,128)}, f32[8,104,256]{2,1,0:T(8,128)S(1)}, bf16[8,104,256]{2,1,0:T(8,128)(2,1)S(1)}) custom-call(bf16[104,256]{1,0:T(8,128)(2,1)S(1)} %pad_maximum_fusion.refs_0_, bf16[104,256]{1,0:T(8,128)(2,1)S(1)} %collective-permute-done.1.refs_1_, bf16[104,256]{1,0:T(8,128)(2,1)S(1)} %collective-permute-done.2.refs_2_, ...), custom_call_target="tpu_custom_call" | custom-call | tf_op jit(solution)/shard_map/adjoint/pallas_call | solution.py:140
  44.2 0.9 %copy-done.1 = f32[8,104,256]{2,1,0:T(8,128)} copy-done((f32[8,104,256]{2,1,0:T(8,128)}, f32[8,104,256]{2,1,0:T(8,128)S(1)}, u32[]{:S(2)}) %copy-start.1) | copy-done | bytes 851992
  45.6 1.4 %collective-permute-done.16.came_ref = bf16[8,104,256]{2,1,0:T(8,128)(2,1)S(1)} collective-permute-done((bf16[8,104,256]{2,1,0:T(8,128)(2,1)S(1)}, bf16[8,104,256]{2,1,0:T(8,128)(2,1)S(1)}, u32[]{:S(2)}, u32[]{:S(2)}) %collective-permute-start.16) | collective-permute-done | bytes 426016 | tf_op jit(solution)/shard_map/ppermute | solution.py:18
  47.0 0.8 %copy-done.5 = bf16[8,104,256]{2,1,0:T(8,128)(2,1)} copy-done((bf16[8,104,256]{2,1,0:T(8,128)(2,1)}, bf16[8,104,256]{2,1,0:T(8,128)(2,1)S(1)}, u32[]{:S(2)}) %copy-start.5) | copy-done | bytes 426008
  47.8 2.1 %join.1 = (f32[104,256]{1,0:T(8,128)}, bf16[104,256]{1,0:T(8,128)(2,1)}, bf16[104,256]{1,0:T(8,128)(2,1)}, bf16[104,256]{1,0:T(8,128)(2,1)}, f32[104,256]{1,0:T(...) custom-call(f32[8,104,256]{2,1,0:T(8,128)} %copy-done.1, ...), custom_call_target="tpu_custom_call" | custom-call | tf_op jit(solution)/shard_map/join/pallas_call | solution.py:164
  49.8 1.5 %collective-permute-start.20 = (bf16[104,256]{1,0:T(8,128)(2,1)}, bf16[104,256]{1,0:T(8,128)(2,1)S(1)}, u32[]{:S(2)}, u32[]{:S(2)}) collective-permute-start(bf16[104,256]{1,0:T(8,128)(2,1)} %get-tuple-element.24), channel_id=1, source_target_pairs={{0,2},{1,3},{2,0},{3,1},{4,6},{5,7},{6,4},{7,5},{8,10},{9,11},{10,... | collective-permute-start | bytes 159752 | tf_op jit(solution)/shard_map/ppermute | solution.py:18
  51.3 0.6 collective-permute-start.21
  51.9 1.4 %collective-permute-start.22 = (bf16[104,256]{1,0:T(8,128)(2,1)}, bf16[104,256]{1,0:T(8,128)(2,1)S(1)}, u32[]{:S(2)}, u32[]{:S(2)}) collective-permute-start(bf16[104,256]{1,0:T(8,128)(2,1)} %get-tuple-element.26), channel_id=1, source_target_pairs={{0,6},{1,7},{2,4},{3,5},{4,2},{5,3},{6,0},{7,1},{8,14},{9,15},{10,... | collective-permute-start | bytes 159752 | tf_op jit(solution)/shard_map/ppermute | solution.py:18
  53.3 1.5 %collective-permute-start.17 = (bf16[104,256]{1,0:T(8,128)(2,1)}, bf16[104,256]{1,0:T(8,128)(2,1)S(1)}, u32[]{:S(2)}, u32[]{:S(2)}) collective-permute-start(bf16[104,256]{1,0:T(8,128)(2,1)} %get-tuple-element.20), channel_id=1, source_target_pairs={{0,2},{1,3},{2,0},{3,1},{4,6},{5,7},{6,4},{7,5},{8,10},{9,11},{10,... | collective-permute-start | bytes 159752 | tf_op jit(solution)/shard_map/ppermute | solution.py:18
  54.8 0.6 collective-permute-start.18
  55.4 1.4 %collective-permute-start.19 = (bf16[104,256]{1,0:T(8,128)(2,1)}, bf16[104,256]{1,0:T(8,128)(2,1)S(1)}, u32[]{:S(2)}, u32[]{:S(2)}) collective-permute-start(bf16[104,256]{1,0:T(8,128)(2,1)} %get-tuple-element.22), channel_id=1, source_target_pairs={{0,6},{1,7},{2,4},{3,5},{4,2},{5,3},{6,0},{7,1},{8,14},{9,15},{10,... | collective-permute-start | bytes 159752 | tf_op jit(solution)/shard_map/ppermute | solution.py:18
  56.8 0.6 collective-permute-done.22
  57.5 0.9 %add_convert_fusion = bf16[104,256]{1,0:T(8,128)(2,1)S(1)} fusion(bf16[104,256]{1,0:T(8,128)(2,1)S(1)} %collective-permute-done.22, bf16[104,256]{1,0:T(8,128)(2,1)S(1)} %collective-permute-done.21, f32[104,256]{1,0:T(8,128)} %get-tuple-element.23, bf16[104,256]{1,0:T(8,128)(2,1)S(1)} %collective-permute-done.20), kind=kLoop, calls=%fused_computation.1 | loop fusion | flops 186368 | bytes 319488 | tf_op jit(solution)/shard_map/convert_element_type | solution.py:220
  58.4 2.4 %collective-permute-start.23 = (bf16[104,256]{1,0:T(8,128)(2,1)S(1)}, bf16[104,256]{1,0:T(8,128)(2,1)S(1)}, u32[]{:S(2)}, u32[]{:S(2)}) collective-permute-start(bf16[104,256]{1,0:T(8,128)(2,1)S(1)} %add_convert_fusion), channel_id=1, source_target_pairs={{0,8},{1,9},{2,10},{3,11},{4,12},{5,13},{6,14},{7,15},{8,0},{9,1},... | collective-permute-start | bytes 159752 | tf_op jit(solution)/shard_map/ppermute | solution.py:18
  60.8 2.7 %collective-permute-done.23 = bf16[104,256]{1,0:T(8,128)(2,1)S(1)} collective-permute-done((bf16[104,256]{1,0:T(8,128)(2,1)S(1)}, bf16[104,256]{1,0:T(8,128)(2,1)S(1)}, u32[]{:S(2)}, u32[]{:S(2)}) %collective-permute-start.23) | collective-permute-done | bytes 53280 | tf_op jit(solution)/shard_map/ppermute | solution.py:18
  63.5 0.9 %convert_add_fusion = f32[104,256]{1,0:T(8,128)S(1)} fusion(bf16[104,256]{1,0:T(8,128)(2,1)S(1)} %collective-permute-done.23, bf16[104,256]{1,0:T(8,128)(2,1)S(1)} %collective-permute-done.19, bf16[104,256]{1,0:T(8,128)(2,1)S(1)} %collective-permute-done.18, f32[104,256]{1,0:T(8,128)} %get-tuple-element.19, bf16[104,256]{1,0:T(8,128)(2,1)S(1)} %collective-permute-done.17), kind=kLoop, calls=%fused_computation | loop fusion | flops 212992 | bytes 425984 | tf_op jit(solution)/shard_map/add | solution.py:221
  64.4 1.6 %collective-permute-start.24 = (f32[8,256]{1,0:T(8,128)S(1)}, f32[8,256]{1,0:T(8,128)S(1)}, u32[]{:S(2)}, u32[]{:S(2)}) collective-permute-start(f32[8,256]{1,0:T(8,128)S(1)} %slice.14), channel_id=1, source_target_pairs={{0,16},{16,0},{1,17},{17,1},{2,18},{18,2},{3,19},{19,3},{4,20},{20... | collective-permute-start | bytes 24584 | tf_op jit(solution)/shard_map/ppermute | solution.py:23
  66.0 2.1 %collective-permute-done.24 = f32[8,256]{1,0:T(8,128)S(1)} collective-permute-done((f32[8,256]{1,0:T(8,128)S(1)}, f32[8,256]{1,0:T(8,128)S(1)}, u32[]{:S(2)}, u32[]{:S(2)}) %collective-permute-start.24) | collective-permute-done | bytes 8224 | tf_op jit(solution)/shard_map/ppermute | solution.py:23
  68.2 0.7 slice_add_fusion
  (42 shorter events, 2.7 us)
Async XLA Ops:
  0.6 34.0 %copy-start.4 = (f32[128]{0:T(128)S(1)}, f32[128]{0:T(128)}, u32[]{:S(2)}) copy-start(f32[128]{0:T(128)} %param.12) | copy-start | bytes 1540
  0.6 34.0 %copy-start.3 = (f32[128]{0:T(128)S(1)}, f32[128]{0:T(128)}, u32[]{:S(2)}) copy-start(f32[128]{0:T(128)} %param.11) | copy-start | bytes 1540
  1.6 4.6 %collective-permute-start = (bf16[8,256]{1,0:T(8,128)(2,1)S(1)}, bf16[8,256]{1,0:T(8,128)(2,1)S(1)}, u32[]{:S(2)}, u32[]{:S(2)}) collective-permute-start(bf16[8,256]{1,0:T(8,128)(2,1)S(1)} %slice.12), channel_id=1, source_target_pairs={{0,16},{16,0},{1,17},{17,1},{2,18},{18,2},{3,19},{19,3},{4,20},{20... | collective-permute-start | bytes 12296 | tf_op jit(solution)/shard_map/ppermute | solution.py:23
  6.2 6.7 %collective-permute-start.8 = (bf16[104,256]{1,0:T(8,128)(2,1)S(1)}, bf16[104,256]{1,0:T(8,128)(2,1)S(1)}, u32[]{:S(2)}, u32[]{:S(2)}) collective-permute-start(bf16[104,256]{1,0:T(8,128)(2,1)S(1)} %pad_maximum_fusion.refs_0_), channel_id=1, source_target_pairs={{0,8},{1,9},{2,10},{3,11},{4,12},{5,13},{6,14},{7,15},{8,0},{9,1},... | collective-permute-start | bytes 159752 | tf_op jit(solution)/shard_map/ppermute | solution.py:18
  9.4 6.0 %collective-permute-start.6 = (bf16[104,256]{1,0:T(8,128)(2,1)S(1)}, bf16[104,256]{1,0:T(8,128)(2,1)S(1)}, u32[]{:S(2)}, u32[]{:S(2)}) collective-permute-start(bf16[104,256]{1,0:T(8,128)(2,1)S(1)} %pad_maximum_fusion.refs_0_), channel_id=1, source_target_pairs={{0,6},{1,7},{2,4},{3,5},{4,2},{5,3},{6,0},{7,1},{8,14},{9,15},{10,... | collective-permute-start | bytes 159752 | tf_op jit(solution)/shard_map/ppermute | solution.py:18
  11.9 4.1 %collective-permute-start.4 = (bf16[104,256]{1,0:T(8,128)(2,1)S(1)}, bf16[104,256]{1,0:T(8,128)(2,1)S(1)}, u32[]{:S(2)}, u32[]{:S(2)}) collective-permute-start(bf16[104,256]{1,0:T(8,128)(2,1)S(1)} %pad_maximum_fusion.refs_0_), channel_id=1, source_target_pairs={{0,4},{1,5},{2,6},{3,7},{4,0},{5,1},{6,2},{7,3},{8,12},{9,13},{10,... | collective-permute-start | bytes 159752 | tf_op jit(solution)/shard_map/ppermute | solution.py:18
  12.3 5.2 %collective-permute-start.2 = (bf16[104,256]{1,0:T(8,128)(2,1)S(1)}, bf16[104,256]{1,0:T(8,128)(2,1)S(1)}, u32[]{:S(2)}, u32[]{:S(2)}) collective-permute-start(bf16[104,256]{1,0:T(8,128)(2,1)S(1)} %pad_maximum_fusion.refs_0_), channel_id=1, source_target_pairs={{0,2},{1,3},{2,0},{3,1},{4,6},{5,7},{6,4},{7,5},{8,10},{9,11},{10,... | collective-permute-start | bytes 159752 | tf_op jit(solution)/shard_map/ppermute | solution.py:18
  12.8 4.7 %collective-permute-start.1 = (bf16[104,256]{1,0:T(8,128)(2,1)S(1)}, bf16[104,256]{1,0:T(8,128)(2,1)S(1)}, u32[]{:S(2)}, u32[]{:S(2)}) collective-permute-start(bf16[104,256]{1,0:T(8,128)(2,1)S(1)} %pad_maximum_fusion.refs_0_), channel_id=1, source_target_pairs={{0,1},{1,0},{2,3},{3,2},{4,5},{5,4},{6,7},{7,6},{8,9},{9,8},{10,11... | collective-permute-start | bytes 159752 | tf_op jit(solution)/shard_map/ppermute | solution.py:18
  12.9 5.2 %collective-permute-start.14 = (bf16[104,256]{1,0:T(8,128)(2,1)S(1)}, bf16[104,256]{1,0:T(8,128)(2,1)S(1)}, u32[]{:S(2)}, u32[]{:S(2)}) collective-permute-start(bf16[104,256]{1,0:T(8,128)(2,1)S(1)} %collective-permute-done.8.refs_8_), channel_id=1, source_target_pairs={{0,6},{1,7},{2,4},{3,5},{4,2},{5,3},{6,0},{7,1},{8,14},{9,15},{10,... | collective-permute-start | bytes 159752 | tf_op jit(solution)/shard_map/ppermute | solution.py:18
  15.4 4.1 %collective-permute-start.12 = (bf16[104,256]{1,0:T(8,128)(2,1)S(1)}, bf16[104,256]{1,0:T(8,128)(2,1)S(1)}, u32[]{:S(2)}, u32[]{:S(2)}) collective-permute-start(bf16[104,256]{1,0:T(8,128)(2,1)S(1)} %collective-permute-done.8.refs_8_), channel_id=1, source_target_pairs={{0,4},{1,5},{2,6},{3,7},{4,0},{5,1},{6,2},{7,3},{8,12},{9,13},{10,... | collective-permute-start | bytes 159752 | tf_op jit(solution)/shard_map/ppermute | solution.py:18
  16.0 4.1 %collective-permute-start.10 = (bf16[104,256]{1,0:T(8,128)(2,1)S(1)}, bf16[104,256]{1,0:T(8,128)(2,1)S(1)}, u32[]{:S(2)}, u32[]{:S(2)}) collective-permute-start(bf16[104,256]{1,0:T(8,128)(2,1)S(1)} %collective-permute-done.8.refs_8_), channel_id=1, source_target_pairs={{0,2},{1,3},{2,0},{3,1},{4,6},{5,7},{6,4},{7,5},{8,10},{9,11},{10,... | collective-permute-start | bytes 159752 | tf_op jit(solution)/shard_map/ppermute | solution.py:18
  17.5 2.7 %collective-permute-start.9 = (bf16[104,256]{1,0:T(8,128)(2,1)S(1)}, bf16[104,256]{1,0:T(8,128)(2,1)S(1)}, u32[]{:S(2)}, u32[]{:S(2)}) collective-permute-start(bf16[104,256]{1,0:T(8,128)(2,1)S(1)} %collective-permute-done.8.refs_8_), channel_id=1, source_target_pairs={{0,1},{1,0},{2,3},{3,2},{4,5},{5,4},{6,7},{7,6},{8,9},{9,8},{10,11... | collective-permute-start | bytes 159752 | tf_op jit(solution)/shard_map/ppermute | solution.py:18
  17.5 3.2 %collective-permute-start.7 = (bf16[104,256]{1,0:T(8,128)(2,1)S(1)}, bf16[104,256]{1,0:T(8,128)(2,1)S(1)}, u32[]{:S(2)}, u32[]{:S(2)}) collective-permute-start(bf16[104,256]{1,0:T(8,128)(2,1)S(1)} %collective-permute-done.6.refs_6_), channel_id=1, source_target_pairs={{0,1},{1,0},{2,3},{3,2},{4,5},{5,4},{6,7},{7,6},{8,9},{9,8},{10,11... | collective-permute-start | bytes 159752 | tf_op jit(solution)/shard_map/ppermute | solution.py:18
  18.0 16.6 %collective-permute-start.5 = (bf16[104,256]{1,0:T(8,128)(2,1)S(1)}, bf16[104,256]{1,0:T(8,128)(2,1)S(1)}, u32[]{:S(2)}, u32[]{:S(2)}) collective-permute-start(bf16[104,256]{1,0:T(8,128)(2,1)S(1)} %collective-permute-done.4.refs_4_), channel_id=1, source_target_pairs={{0,1},{1,0},{2,3},{3,2},{4,5},{5,4},{6,7},{7,6},{8,9},{9,8},{10,11... | collective-permute-start | bytes 159752 | tf_op jit(solution)/shard_map/ppermute | solution.py:18
  19.5 15.1 %collective-permute-start.3 = (bf16[104,256]{1,0:T(8,128)(2,1)S(1)}, bf16[104,256]{1,0:T(8,128)(2,1)S(1)}, u32[]{:S(2)}, u32[]{:S(2)}) collective-permute-start(bf16[104,256]{1,0:T(8,128)(2,1)S(1)} %collective-permute-done.2.refs_2_), channel_id=1, source_target_pairs={{0,1},{1,0},{2,3},{3,2},{4,5},{5,4},{6,7},{7,6},{8,9},{9,8},{10,11... | collective-permute-start | bytes 159752 | tf_op jit(solution)/shard_map/ppermute | solution.py:18
  20.2 14.5 %collective-permute-start.15 = (bf16[104,256]{1,0:T(8,128)(2,1)S(1)}, bf16[104,256]{1,0:T(8,128)(2,1)S(1)}, u32[]{:S(2)}, u32[]{:S(2)}) collective-permute-start(bf16[104,256]{1,0:T(8,128)(2,1)S(1)} %collective-permute-done.14.refs_14_), channel_id=1, source_target_pairs={{0,1},{1,0},{2,3},{3,2},{4,5},{5,4},{6,7},{7,6},{8,9},{9,8},{10,11... | collective-permute-start | bytes 159752 | tf_op jit(solution)/shard_map/ppermute | solution.py:18
  20.2 14.5 %collective-permute-start.13 = (bf16[104,256]{1,0:T(8,128)(2,1)S(1)}, bf16[104,256]{1,0:T(8,128)(2,1)S(1)}, u32[]{:S(2)}, u32[]{:S(2)}) collective-permute-start(bf16[104,256]{1,0:T(8,128)(2,1)S(1)} %collective-permute-done.12.refs_12_), channel_id=1, source_target_pairs={{0,1},{1,0},{2,3},{3,2},{4,5},{5,4},{6,7},{7,6},{8,9},{9,8},{10,11... | collective-permute-start | bytes 159752 | tf_op jit(solution)/shard_map/ppermute | solution.py:18
  20.7 14.0 %collective-permute-start.11 = (bf16[104,256]{1,0:T(8,128)(2,1)S(1)}, bf16[104,256]{1,0:T(8,128)(2,1)S(1)}, u32[]{:S(2)}, u32[]{:S(2)}) collective-permute-start(bf16[104,256]{1,0:T(8,128)(2,1)S(1)} %collective-permute-done.10.refs_10_), channel_id=1, source_target_pairs={{0,1},{1,0},{2,3},{3,2},{4,5},{5,4},{6,7},{7,6},{8,9},{9,8},{10,11... | collective-permute-start | bytes 159752 | tf_op jit(solution)/shard_map/ppermute | solution.py:18
  34.7 3.4 %copy-start = (bf16[16,1024,256]{2,1,0:T(8,128)(2,1)S(1)}, bf16[16,1024,256]{2,1,0:T(8,128)(2,1)}, u32[]{:S(2)}) copy-start(bf16[16,1024,256]{2,1,0:T(8,128)(2,1)} %get-tuple-element.15.refs_16_) | copy-start | bytes 25165828
  38.0 0.9 %copy-start.2 = (bf16[104,1024]{1,0:T(8,128)(2,1)S(1)}, bf16[104,1024]{1,0:T(8,128)(2,1)}, u32[]{:S(2)}) copy-start(bf16[104,1024]{1,0:T(8,128)(2,1)} %get-tuple-element.16.refs_17_) | copy-start | bytes 638980
  44.2 0.9 %copy-start.1 = (f32[8,104,256]{2,1,0:T(8,128)}, f32[8,104,256]{2,1,0:T(8,128)S(1)}, u32[]{:S(2)}) copy-start(f32[8,104,256]{2,1,0:T(8,128)S(1)} %get-tuple-element.17.own_ref) | copy-start | bytes 2555908
  45.1 1.8 %collective-permute-start.16 = (bf16[8,104,256]{2,1,0:T(8,128)(2,1)S(1)}, bf16[8,104,256]{2,1,0:T(8,128)(2,1)S(1)}, u32[]{:S(2)}, u32[]{:S(2)}) collective-permute-start(bf16[8,104,256]{2,1,0:T(8,128)(2,1)S(1)} %get-tuple-element.18), channel_id=1, source_target_pairs={{0,1},{1,0},{2,3},{3,2},{4,5},{5,4},{6,7},{7,6},{8,9},{9,8},{10,11... | collective-permute-start | bytes 1277960 | tf_op jit(solution)/shard_map/ppermute | solution.py:18
  47.0 0.8 %copy-start.5 = (bf16[8,104,256]{2,1,0:T(8,128)(2,1)}, bf16[8,104,256]{2,1,0:T(8,128)(2,1)S(1)}, u32[]{:S(2)}) copy-start(bf16[8,104,256]{2,1,0:T(8,128)(2,1)S(1)} %collective-permute-done.16.came_ref) | copy-start | bytes 1277956
  49.8 5.6 %collective-permute-start.20 = (bf16[104,256]{1,0:T(8,128)(2,1)}, bf16[104,256]{1,0:T(8,128)(2,1)S(1)}, u32[]{:S(2)}, u32[]{:S(2)}) collective-permute-start(bf16[104,256]{1,0:T(8,128)(2,1)} %get-tuple-element.24), channel_id=1, source_target_pairs={{0,2},{1,3},{2,0},{3,1},{4,6},{5,7},{6,4},{7,5},{8,10},{9,11},{10,... | collective-permute-start | bytes 159752 | tf_op jit(solution)/shard_map/ppermute | solution.py:18
  51.3 5.5 %collective-permute-start.21 = (bf16[104,256]{1,0:T(8,128)(2,1)}, bf16[104,256]{1,0:T(8,128)(2,1)S(1)}, u32[]{:S(2)}, u32[]{:S(2)}) collective-permute-start(bf16[104,256]{1,0:T(8,128)(2,1)} %get-tuple-element.25), channel_id=1, source_target_pairs={{0,4},{1,5},{2,6},{3,7},{4,0},{5,1},{6,2},{7,3},{8,12},{9,13},{10,... | collective-permute-start | bytes 159752 | tf_op jit(solution)/shard_map/ppermute | solution.py:18
  51.9 5.6 %collective-permute-start.22 = (bf16[104,256]{1,0:T(8,128)(2,1)}, bf16[104,256]{1,0:T(8,128)(2,1)S(1)}, u32[]{:S(2)}, u32[]{:S(2)}) collective-permute-start(bf16[104,256]{1,0:T(8,128)(2,1)} %get-tuple-element.26), channel_id=1, source_target_pairs={{0,6},{1,7},{2,4},{3,5},{4,2},{5,3},{6,0},{7,1},{8,14},{9,15},{10,... | collective-permute-start | bytes 159752 | tf_op jit(solution)/shard_map/ppermute | solution.py:18
  53.3 7.5 %collective-permute-start.17 = (bf16[104,256]{1,0:T(8,128)(2,1)}, bf16[104,256]{1,0:T(8,128)(2,1)S(1)}, u32[]{:S(2)}, u32[]{:S(2)}) collective-permute-start(bf16[104,256]{1,0:T(8,128)(2,1)} %get-tuple-element.20), channel_id=1, source_target_pairs={{0,2},{1,3},{2,0},{3,1},{4,6},{5,7},{6,4},{7,5},{8,10},{9,11},{10,... | collective-permute-start | bytes 159752 | tf_op jit(solution)/shard_map/ppermute | solution.py:18
  54.8 6.0 %collective-permute-start.18 = (bf16[104,256]{1,0:T(8,128)(2,1)}, bf16[104,256]{1,0:T(8,128)(2,1)S(1)}, u32[]{:S(2)}, u32[]{:S(2)}) collective-permute-start(bf16[104,256]{1,0:T(8,128)(2,1)} %get-tuple-element.21), channel_id=1, source_target_pairs={{0,4},{1,5},{2,6},{3,7},{4,0},{5,1},{6,2},{7,3},{8,12},{9,13},{10,... | collective-permute-start | bytes 159752 | tf_op jit(solution)/shard_map/ppermute | solution.py:18
  55.4 5.4 %collective-permute-start.19 = (bf16[104,256]{1,0:T(8,128)(2,1)}, bf16[104,256]{1,0:T(8,128)(2,1)S(1)}, u32[]{:S(2)}, u32[]{:S(2)}) collective-permute-start(bf16[104,256]{1,0:T(8,128)(2,1)} %get-tuple-element.22), channel_id=1, source_target_pairs={{0,6},{1,7},{2,4},{3,5},{4,2},{5,3},{6,0},{7,1},{8,14},{9,15},{10,... | collective-permute-start | bytes 159752 | tf_op jit(solution)/shard_map/ppermute | solution.py:18
  58.4 5.1 %collective-permute-start.23 = (bf16[104,256]{1,0:T(8,128)(2,1)S(1)}, bf16[104,256]{1,0:T(8,128)(2,1)S(1)}, u32[]{:S(2)}, u32[]{:S(2)}) collective-permute-start(bf16[104,256]{1,0:T(8,128)(2,1)S(1)} %add_convert_fusion), channel_id=1, source_target_pairs={{0,8},{1,9},{2,10},{3,11},{4,12},{5,13},{6,14},{7,15},{8,0},{9,1},... | collective-permute-start | bytes 159752 | tf_op jit(solution)/shard_map/ppermute | solution.py:18
  64.4 3.7 %collective-permute-start.24 = (f32[8,256]{1,0:T(8,128)S(1)}, f32[8,256]{1,0:T(8,128)S(1)}, u32[]{:S(2)}, u32[]{:S(2)}) collective-permute-start(f32[8,256]{1,0:T(8,128)S(1)} %slice.14), channel_id=1, source_target_pairs={{0,16},{16,0},{1,17},{17,1},{2,18},{18,2},{3,19},{19,3},{4,20},{20... | collective-permute-start | bytes 24584 | tf_op jit(solution)/shard_map/ppermute | solution.py:23

commit v2 on v0

v2 whole, which is shorter than its diff:
```python
import functools

import jax
import jax.numpy as jnp
from jax import lax
from jax.experimental import pallas as pl
from jax.experimental.pallas import tpu as pltpu
from jax.sharding import PartitionSpec as P

RIM = 8
PAIR = 2 * RIM
F32 = jnp.float32
BF16 = jnp.bfloat16
VMEM_LIMIT = 44 * 1024 * 1024
SMALL_LIMIT = 8 * 1024 * 1024
BUSY = 10**10


def swap(block, bit):
    devices = range(lax.axis_size("rcpt"))
    return lax.ppermute(block, "rcpt", [(i, i ^ bit) for i in devices])


def turn(block, distance):
    size = lax.axis_size("hour")
    return lax.ppermute(block, "hour", [(i, (i + distance) % size) for i in range(size)])


def expander(rows, lags, dtype):
    shape = (rows, rows * lags)
    row = lax.broadcasted_iota(jnp.int32, shape, 0)
    column = lax.broadcasted_iota(jnp.int32, shape, 1)
    first = row * lags
    return ((column >= first) & (column < first + lags)).astype(dtype)


def call(kernel, outs, operands, spaces, scratch=(), limit=SMALL_LIMIT, flops=0, moved=0, name=None):
    where = {"v": pltpu.VMEM, "s": pltpu.SMEM, "a": pl.ANY}
    vmem = pl.BlockSpec(memory_space=pltpu.VMEM)
    return pl.pallas_call(
        kernel,
        in_specs=[pl.BlockSpec(memory_space=where[c]) for c in spaces],
        out_specs=[vmem] * len(outs),
        out_shape=[jax.ShapeDtypeStruct(shape, dtype) for shape, dtype in outs],
        scratch_shapes=scratch,
        compiler_params=pltpu.CompilerParams(vmem_limit_bytes=limit),
        cost_estimate=pl.CostEstimate(flops=flops, bytes_accessed=moved, transcendentals=0),
        name=name,
    )(*operands)


def prepare_kernel(devices, start, foot_hbm, mask_ref, after_ref, masked_ref, foot_ref, sems):
    del after_ref
    me = lax.axis_index("rcpt")
    blocks, lags, tiles = mask_ref.shape
    depth, cells = foot_ref.shape
    own = cells // devices
    tile = cells // tiles
    group = 2 * lags
    part = foot_hbm.shape[0] // blocks
    used = depth // part
    first = start * used
    copies = []
    for b in range(used):
        source = foot_hbm.at[pl.ds((first + b) * part, part)]
        copies.append(pltpu.make_async_copy(source, foot_ref.at[pl.ds(b * part, part)], sems.at[b]))
    for copy in copies:
        copy.start()
    mask = mask_ref[first : first + used].astype(F32)
    twice = jnp.broadcast_to(mask[:, None], (used, 2, lags, tiles)).reshape(used * group, tiles)
    wide = jnp.dot(twice.astype(BF16), expander(tiles, tile, BF16), preferred_element_type=F32)
    wide = wide.astype(BF16)
    for b in range(used):
        copies[b].wait()
        for d in range(devices):
            cut = slice(d * own, (d + 1) * own)
            keep = wide[b * group : (b + 1) * group, cut]
            for j in range(part // group):
                at = pl.ds(b * part + j * group, group)
                masked_ref[me ^ d, at, :] = foot_ref[at, cut] * keep


def prepare(foot, mask, after, devices, start):
    depth, cells = foot.shape
    depth //= 2
    blocks = mask.shape[0] // 2
    return call(
        functools.partial(prepare_kernel, devices, start),
        [((devices, depth, cells // devices), BF16)],
        [foot, mask, after],
        "ava",
        [pltpu.VMEM((depth, cells), BF16), pltpu.SemaphoreType.DMA((blocks,))],
        limit=VMEM_LIMIT,
        flops=BUSY,
        moved=4 * depth * cells,
        name="prepare",
    )[0]


def choose_kernel(lags, hours, hour_ref, obs_ref, weight_ref, count_ref, after_ref, select_ref, line_ref):
    del after_ref
    rows = hour_ref.shape[1]
    times = jnp.broadcast_to(hour_ref[...].astype(F32), (8, rows)).astype(BF16)
    spread = jnp.dot(times, expander(rows, lags, BF16), preferred_element_type=F32)
    column = lax.broadcasted_iota(jnp.int32, (1, rows * lags), 1)
    hour = spread[:1].astype(jnp.int32) - lax.rem(column, lags)
    slot = jnp.where(hour >= 0, hour, hour + (hours + RIM))
    wanted = lax.broadcasted_iota(jnp.int32, select_ref.shape, 0)
    select_ref[...] = (wanted == slot).astype(F32)
    live = (lax.broadcasted_iota(jnp.int32, (1, rows), 1) < count_ref[0]).astype(F32)
    line_ref[0:1] = live * weight_ref[...]
    line_ref[1:2] = obs_ref[...]


def choose(hour, obs, weight, count, after, lags, hours):
    rows = hour.shape[1]
    return call(
        functools.partial(choose_kernel, lags, hours),
        [((hours + PAIR, rows * lags), F32), ((8, rows), F32)],
        [hour, obs, weight, count, after],
        "vvvsa",
        flops=BUSY,
        name="choose",
    )


def tails_kernel(low_ref, far_ref, after_ref, out_ref):
    del after_ref
    hours = low_ref.shape[0]
    ends = [ref[hours - PAIR :].astype(F32)[RIM:] for ref in (low_ref, far_ref)]
    out_ref[...] = jnp.concatenate(ends, axis=0).astype(BF16)


def tails(low, far_low, after):
    outs = [((PAIR, low.shape[1]), BF16)]
    return call(tails_kernel, outs, [low, far_low, after], "vva", name="tails")[0]


def window_kernel(low_ref, far_ref, rims_ref, after_ref, out_ref):
    del after_ref
    hours = low_ref.shape[0]
    inside = (lax.axis_index("hour") > 0).astype(F32)
    out_ref[:hours] = low_ref[...]
    out_ref[hours : 2 * hours] = far_ref[...]
    out_ref[2 * hours :] = (rims_ref[...].astype(F32) * inside).astype(BF16)


def window(low, far_low, rims, after):
    hours, columns = low.shape
    outs = [((2 * hours + PAIR, columns), BF16)]
    return call(window_kernel, outs, [low, far_low, rims, after], "vvva", name="window")[0]


def pack_kernel(*refs):
    *parts, _, out_ref = refs
    height = parts[0].shape[0]
    for i, part in enumerate(parts):
        out_ref[i * height : (i + 1) * height] = part[...]


def pack(parts, after):
    height, columns = parts[0].shape
    outs = [((len(parts) * height, columns), BF16)]
    operands = [*parts, after]
    return call(pack_kernel, outs, operands, "v" * len(operands), name="pack")[0]


def add_scores(windows, masked_refs, start, score_ref, window_ref):
    hours = window_ref.shape[0] - PAIR
    half = masked_refs[0].shape[0] // 2
    depth = masked_refs[0].shape[1]
    for i, read in enumerate(windows):
        rims = read(slice(2 * hours, 2 * hours + PAIR)).astype(F32)
        gap = jnp.zeros_like(rims[:RIM])
        for j in range(2):
            window_ref[:hours] = read(slice(j * hours, (j + 1) * hours))
            rim = rims[j * RIM : (j + 1) * RIM]
            window_ref[hours:] = jnp.concatenate([rim, gap], axis=0).astype(BF16)
            k = (j * half + 2 * i) ^ start
            dims = (((1,), (1,)), ((), ()))
            for n, masked_ref in enumerate(masked_refs):
                at = slice(n * depth, (n + 1) * depth)
                term = lax.dot_general(
                    window_ref[...], masked_ref[k], dims, preferred_element_type=F32
                )
                if start == 0 and i == 0 and j == 0:
                    score_ref[:, at] = term
                else:
                    score_ref[:, at] += term


def readers(first_ref, rest_ref):
    height = first_ref.shape[0]

    def read(i, rows):
        if i == 0:
            return first_ref[rows]
        return rest_ref[(i - 1) * height + rows.start : (i - 1) * height + rows.stop]

    count = 1 + rest_ref.shape[0] // height
    return [functools.partial(read, i) for i in range(count)]


def score_kernel(first_ref, rest_ref, top_ref, low_ref, score_ref, window_ref):
    add_scores(readers(first_ref, rest_ref), (top_ref, low_ref), 0, score_ref, window_ref)


def score(first, rest, masked):
    devices, depth, own = masked[0].shape
    depth *= 2
    width = first.shape[0] // 2 - RIM + PAIR
    return call(
        score_kernel,
        [((width, depth), F32)],
        [first, rest, *masked],
        "vvvv",
        [pltpu.VMEM((width, own), BF16)],
        flops=width * depth * own * devices,
        moved=depth * own * devices,
        name="score",
    )[0]


def terms(spread_ref, masked_refs, k):
    depth = masked_refs[0].shape[1]
    total = None
    for n, masked_ref in enumerate(masked_refs):
        at = slice(n * depth, (n + 1) * depth)
        term = jnp.dot(spread_ref[:, at], masked_ref[k], preferred_element_type=F32)
        total = term if total is None else total + term
    return total


def adjoint_kernel(
    first_ref, rest_ref, top_ref, low_ref, begun_ref, select_ref, line_ref,
    mism_ref, spread_ref, other_ref, score_ref, window_ref,
):
    depth = score_ref.shape[1]
    rows = mism_ref.shape[1]
    lags = depth // rows
    score_ref[...] = begun_ref[...]
    add_scores(readers(first_ref, rest_ref), (top_ref, low_ref), 1, score_ref, window_ref)
    line = jnp.sum(score_ref[...] * select_ref[...], axis=0, keepdims=True)
    belongs = expander(rows, lags, F32)
    model = lax.dot_general(
        jnp.broadcast_to(line, (8, depth)),
        belongs,
        (((1,), (1,)), ((), ())),
        precision=lax.Precision.HIGHEST,
        preferred_element_type=F32,
    )[:1]
    mism = line_ref[0:1] * (model - line_ref[1:2])
    mism_ref[...] = mism
    weighted = jnp.broadcast_to(mism, (8, rows)).astype(BF16)
    wide = jnp.dot(weighted, belongs.astype(BF16), preferred_element_type=F32)[:1]
    spread_ref[...] = (select_ref[...] * wide).astype(BF16)
    for k in range(top_ref.shape[0] // 2):
        other_ref[k] = terms(spread_ref, (top_ref, low_ref), 2 * k + 1).astype(BF16)


def adjoint(first, rest, masked, begun, select, lines):
    devices, depth, own = masked[0].shape
    depth *= 2
    width = begun.shape[0]
    return call(
        adjoint_kernel,
        [
            ((1, lines.shape[1]), F32),
            ((width, depth), BF16),
            ((devices // 2, width, own), BF16),
        ],
        [first, rest, *masked, begun, select, lines],
        "v" * 7,
        [pltpu.VMEM((width, depth), F32), pltpu.VMEM((width, own), BF16)],
        flops=2 * width * depth * own * devices,
        moved=depth * own * devices,
        name="adjoint",
    )


def mine_kernel(spread_ref, top_ref, low_ref, own_ref):
    for k in range(top_ref.shape[0] // 2):
        own_ref[k] = terms(spread_ref, (top_ref, low_ref), 2 * k)


def mine_part(spread, masked):
    devices, depth, own = masked[0].shape
    depth *= 2
    width = spread.shape[0]
    return call(
        mine_kernel,
        [((devices // 2, width, own), F32)],
        [spread, *masked],
        "vvv",
        flops=width * depth * own * devices,
        moved=depth * own * devices,
        name="mine",
    )[0]


def join_kernel(own_ref, came_ref, main_ref, rims_ref):
    half, width, _ = own_ref.shape
    hours = width - PAIR
    for i in range(half // 2):
        edges = []
        for j in range(2):
            k = i + j * (half // 2)
            total = own_ref[k] + came_ref[k].astype(F32)
            main_ref[i, j * hours : (j + 1) * hours] = total[:hours]
            edges.append(total[hours : hours + RIM])
        rims_ref[i * PAIR : (i + 1) * PAIR] = jnp.concatenate(edges, axis=0).astype(BF16)


def join(own, came):
    half, width, columns = own.shape
    outs = [
        ((half // 2, 2 * (width - PAIR), columns), F32),
        ((half // 2 * PAIR, columns), BF16),
    ]
    return call(join_kernel, outs, [own, came], "vv", name="join")


def diagonal_kernel(main_ref, after_ref, out_ref):
    del after_ref
    out_ref[...] = main_ref[main_ref.shape[0] - 1].astype(BF16)


def diagonal(main, after):
    outs = [(main.shape[1:], BF16)]
    return call(diagonal_kernel, outs, [main, after], "vv", flops=BUSY, name="diagonal")[0]


def with_rims(both, rims):
    hours = both.shape[0] // 2
    pieces = []
    for j in range(2):
        at = (j + 1) * hours - RIM
        pieces.append(both[j * hours : at])
        pieces.append(both[at : at + RIM] + rims[j * RIM : (j + 1) * RIM])
    return jnp.concatenate(pieces, axis=0)


def shares_kernel(main_ref, rims_ref, first_ref, edge_ref, *outs):
    inside = (lax.axis_index("hour") < lax.axis_size("hour") - 1).astype(F32)
    for i in range(main_ref.shape[0]):
        rims = rims_ref[i * PAIR : (i + 1) * PAIR].astype(F32) * inside
        if i == 0:
            first_ref[...] = with_rims(main_ref[i], rims)
        elif i == main_ref.shape[0] - 1:
            edge_ref[...] = rims.astype(BF16)
        else:
            outs[i - 1][...] = with_rims(main_ref[i], rims).astype(BF16)


def shares(main, rims):
    count, both, columns = main.shape
    outs = [((both, columns), F32), ((PAIR, columns), BF16)]
    outs += [((both, columns), BF16)] * (count - 2)
    return call(shares_kernel, outs, [main, rims], "vv", name="shares")


def sums_kernel(first_ref, edge_ref, *refs):
    *arrived, total_ref, relay_ref = refs
    hours = total_ref.shape[0]
    total = first_ref[...]
    for piece in arrived:
        total += piece[...].astype(F32)
    total = with_rims(total, edge_ref[...].astype(F32))
    total_ref[...] = total[:hours]
    relay_ref[...] = total[hours:].astype(BF16)


def sums(first, edge, arrived):
    both, columns = first.shape
    main = (both // 2, columns)
    operands = [first, edge, *arrived]
    return call(sums_kernel, [(main, F32), (main, BF16)], operands, "v" * len(operands), name="sums")


def per_device(flux, footprint, tile_mask, rec_hour, observed, obs_weight, site_count):
    hours, own = flux.shape
    rows, lags, cells = footprint.shape
    devices = cells // own
    far = devices // 2
    near = range(2, far - 2, 2)
    diag = far - 2

    low = flux.astype(BF16)
    far_low = swap(low, far)
    foot = footprint.reshape(rows * lags, cells)
    top = prepare(foot, tile_mask, low, devices, 0)
    ends = tails(low, far_low, top)
    bottom = prepare(foot, tile_mask, ends, devices, 1)
    first = window(low, far_low, turn(ends, 1), bottom)
    parts = [swap(first, k) for k in range(2, far, 2)]
    other_first = swap(first, 1)
    select, lines = choose(
        rec_hour.reshape(1, rows),
        observed.reshape(1, rows),
        obs_weight.reshape(1, rows),
        site_count,
        first,
        lags,
        hours,
    )
    rest = pack(parts, lines)
    masked = (top, bottom)
    begun = score(first, rest, masked)
    mism, spread, other = adjoint(other_first, swap(rest, 1), masked, begun, select, lines)

    main, rims = join(mine_part(spread, masked), swap(other, 1))
    back = turn(rims, -1)
    diag_main = swap(diagonal(main, rims), diag)
    first, edge, *outward = shares(main, back)
    arrived = [swap(part, k) for part, k in zip(outward, near)]
    edge = swap(edge, diag)
    total, relay = sums(first, edge, [diag_main, *arrived])
    gradient = total + swap(relay, far).astype(F32)
    return (gradient, mism.reshape(rows))


def solution(mesh):
    placed = (
        P("hour", "rcpt"),
        P(("hour", "rcpt"), None, None),
        P(("hour", "rcpt"), None, None),
        P(("hour", "rcpt")),
        P(("hour", "rcpt")),
        P(("hour", "rcpt")),
        P(("hour", "rcpt")),
    )
    return jax.shard_map(
        per_device,
        mesh=mesh,
        in_specs=placed,
        out_specs=(P("hour", "rcpt"), P(("hour", "rcpt"))),
        check_vma=False,
    )
```

time: 136 us -> 46.3 us (0.34)
  waiting for transfers between devices: 60.4 us -> 14.1 us
  blocking collectives: 25.4 us -> 0 us
  matrix products: 17.1 us -> 0 us
  between operations: 14.9 us -> 1.42 us
  starting transfers between devices: 4.72 us -> 17.5 us
  Pallas kernels: 0 us -> 10.7 us
  other arithmetic: 9.5 us -> 1.55 us
  local copies, waits for them, and re-layouts: 3.69 us -> 0.78 us
    reduce_scatter x1 -> x0, waiting for transfers between devices: 56.1 us -> none  [per_device(): owned = lax.psum_scatter(part, 'rcpt', scatter_dimension=1, tiled=True)]
    all_gather x1 -> x0, blocking collectives: 25.4 us -> none  [per_device(): full = lax.all_gather(low, 'rcpt', axis=1, tiled=True)]
    dot_general x2 -> x0, matrix products: 17.1 us -> none  [the longest x1 10.6 us: per_device(): jnp.einsum('rlw,rlc->wc', spread, masked, preferred_element_type=jnp.floa...]
    ppermute x2 -> x14, starting transfers between devices: 4.68 us -> 17.5 us  [the longest x12 14.6 us: swap(): return lax.ppermute(block, 'rcpt', [(i, i ^ bit) for i in devices])]
    pallas_call x0 -> x13, Pallas kernels: none -> 10.7 us  [call(): pl.pallas_call(kernel, in_specs=[pl.BlockSpec(memory_space=where[c]) for...]
    ppermute x2 -> x14, waiting for transfers between devices: 4.25 us -> 14.1 us  [the longest x12 13.1 us: swap(): return lax.ppermute(block, 'rcpt', [(i, i ^ bit) for i in devices])]
    mul x1 -> x0, other arithmetic: 5.04 us -> none  [per_device(): shaped = shaped * tile_mask.astype(jnp.bfloat16)[:, None, :, :, None]]
    mul x1 -> x0, local copies, waits for them, and re-layouts: 2.15 us -> none  [per_device(): shaped = shaped * tile_mask.astype(jnp.bfloat16)[:, None, :, :, None]]
  transfers between devices with their start and end apart: 3 -> 14, of which waited for: 2 -> 7; matrix products, arithmetic and copies ran while one was open for 7% -> 0% of each run, Pallas kernels for 0% -> 15%
where the time goes in v2:
time: 46.3 us; the launch traced here: 46 us
  starting transfers between devices  17.5 us (38%)
  waiting for transfers between devices  14.1 us (30%)
  Pallas kernels  10.7 us (23%)
  other arithmetic  1.55 us (3%)
  between operations  1.42 us (3%)
  local copies, waits for them, and re-layouts  0.78 us (2%)
    ppermute x12, starting transfers between devices, swap(): return lax.ppermute(block, 'rcpt', [(i, i ^ bit) for i in devices])  14.6 us
    ppermute x12, waiting for transfers between devices, swap(): return lax.ppermute(block, 'rcpt', [(i, i ^ bit) for i in devices])  13.1 us
    pallas_call x13, Pallas kernels, call(): pl.pallas_call(kernel, in_specs=[pl.BlockSpec(memory_space=where[c]) for...  10.7 us
    ppermute x2, starting transfers between devices, turn(): lax.ppermute(block, 'hour', [(i, (i + distance) % size) for i in range(si...  2.9 us
    ppermute x2, waiting for transfers between devices, turn(): lax.ppermute(block, 'hour', [(i, (i + distance) % size) for i in range(si...  0.97 us
  transfers between devices with their start and end apart: 14, of which 7 were waited for; matrix products, arithmetic and copies ran while one was open for 0% of the time, Pallas kernels for 15%

profile of v2, /device:TPU:0, one launch (start us, length us, event | category | flops | bytes accessed | tf_op | source)
XLA Modules:
  0.0 46.0 jit_solution(14901419913214399702)
XLA Ops:
  0.6 0.9 %convert_element_type.6.after_ref.low_ref = bf16[96,256]{1,0:T(8,128)(2,1)S(1)} convert(f32[96,256]{1,0:T(8,128)} %param.7) | non-fusion elementwise | flops 24576 | bytes 147456 | tf_op jit(solution)/shard_map/convert_element_type | solution.py:388
  1.5 4.0 %collective-permute-start = (bf16[96,256]{1,0:T(8,128)(2,1)S(1)}, bf16[96,256]{1,0:T(8,128)(2,1)S(1)}, u32[]{:S(2)}, u32[]{:S(2)}) collective-permute-start(bf16[96,256]{1,0:T(8,128)(2,1)S(1)} %convert_element_type.6.after_ref.low_ref), channel_id=1, source_target_pairs={{0,8},{1,9},{2,10},{3,11},{4,12},{5,13},{6,14},{7,15},{8,0},{9,1},... | collective-permute-start | bytes 147464 | tf_op jit(solution)/shard_map/ppermute | solution.py:21
  5.6 0.8 %copy-done = s32[8,8,32]{2,1,0:T(8,128)S(1)} copy-done((s32[8,8,32]{2,1,0:T(8,128)S(1)}, s32[8,8,32]{2,1,0:T(8,128)}, u32[]{:S(2)}) %copy-start) | copy-done | bytes 8216
  6.3 2.3 %prepare.2.after_ref.top_ref = bf16[16,512,256]{2,1,0:T(8,128)(2,1)S(1)} custom-call(bf16[1024,4096]{1,0:T(8,128)(2,1)} %bitcast.8, s32[8,8,32]{2,1,0:T(8,128)S(1)} %copy-done, bf16[96,256]{1,0:T(8,128)(2,1)S(1)} %convert_element_type.6.after_ref.low_ref), custom_call_target="tpu_custom_call" | custom-call | flops 10000000000 | bytes 8388608 | tf_op jit(solution)/shard_map/prepare/pallas_call | solution.py:40
  9.3 1.6 %collective-permute-start.1 = (bf16[16,256]{1,0:T(8,128)(2,1)S(1)}, bf16[16,256]{1,0:T(8,128)(2,1)S(1)}, u32[]{:S(2)}, u32[]{:S(2)}) collective-permute-start(bf16[16,256]{1,0:T(8,128)(2,1)S(1)} %tails.1.after_ref), channel_id=1, source_target_pairs={{0,16},{16,0},{1,17},{17,1},{2,18},{18,2},{3,19},{19,3},{4,20},{20... | collective-permute-start | bytes 24584 | tf_op jit(solution)/shard_map/ppermute | solution.py:26
  10.8 2.3 %prepare.3.after_ref.low_ref = bf16[16,512,256]{2,1,0:T(8,128)(2,1)S(1)} custom-call(bf16[1024,4096]{1,0:T(8,128)(2,1)} %bitcast.9, s32[8,8,32]{2,1,0:T(8,128)S(1)} %copy-done, bf16[16,256]{1,0:T(8,128)(2,1)S(1)} %tails.1.after_ref), custom_call_target="tpu_custom_call" | custom-call | flops 10000000000 | bytes 8388608 | tf_op jit(solution)/shard_map/prepare/pallas_call | solution.py:40
  13.2 2.6 %collective-permute-start.5 = (bf16[208,256]{1,0:T(8,128)(2,1)S(1)}, bf16[208,256]{1,0:T(8,128)(2,1)S(1)}, u32[]{:S(2)}, u32[]{:S(2)}) collective-permute-start(bf16[208,256]{1,0:T(8,128)(2,1)S(1)} %window.1.after_ref.first_ref), channel_id=1, source_target_pairs={{0,6},{1,7},{2,4},{3,5},{4,2},{5,3},{6,0},{7,1},{8,14},{9,15},{10,... | collective-permute-start | bytes 319496 | tf_op jit(solution)/shard_map/ppermute | solution.py:21
  15.8 0.4 collective-permute-start.4
  16.3 0.5 %collective-permute-start.3 = (bf16[208,256]{1,0:T(8,128)(2,1)S(1)}, bf16[208,256]{1,0:T(8,128)(2,1)S(1)}, u32[]{:S(2)}, u32[]{:S(2)}) collective-permute-start(bf16[208,256]{1,0:T(8,128)(2,1)S(1)} %window.1.after_ref.first_ref), channel_id=1, source_target_pairs={{0,2},{1,3},{2,0},{3,1},{4,6},{5,7},{6,4},{7,5},{8,10},{9,11},{10,... | collective-permute-start | bytes 319496 | tf_op jit(solution)/shard_map/ppermute | solution.py:21
  16.8 0.2 choose.1
  17.0 2.7 %collective-permute-done.5.refs_2_ = bf16[208,256]{1,0:T(8,128)(2,1)S(1)} collective-permute-done((bf16[208,256]{1,0:T(8,128)(2,1)S(1)}, bf16[208,256]{1,0:T(8,128)(2,1)S(1)}, u32[]{:S(2)}, u32[]{:S(2)}) %collective-permute-start.5) | collective-permute-done | bytes 106528 | tf_op jit(solution)/shard_map/ppermute | solution.py:21
  19.7 1.2 %collective-permute-done.4.refs_1_ = bf16[208,256]{1,0:T(8,128)(2,1)S(1)} collective-permute-done((bf16[208,256]{1,0:T(8,128)(2,1)S(1)}, bf16[208,256]{1,0:T(8,128)(2,1)S(1)}, u32[]{:S(2)}, u32[]{:S(2)}) %collective-permute-start.4) | collective-permute-done | bytes 106528 | tf_op jit(solution)/shard_map/ppermute | solution.py:21
  20.8 0.2 collective-permute-done.3.refs_0_
  21.0 0.1 collective-permute-start.6
  21.1 0.5 %collective-permute-start.2 = (bf16[208,256]{1,0:T(8,128)(2,1)S(1)}, bf16[208,256]{1,0:T(8,128)(2,1)S(1)}, u32[]{:S(2)}, u32[]{:S(2)}) collective-permute-start(bf16[208,256]{1,0:T(8,128)(2,1)S(1)} %window.1.after_ref.first_ref), channel_id=1, source_target_pairs={{0,1},{1,0},{2,3},{3,2},{4,5},{5,4},{6,7},{7,6},{8,9},{9,8},{10,11... | collective-permute-start | bytes 319496 | tf_op jit(solution)/shard_map/ppermute | solution.py:21
  21.6 1.4 %score.1.begun_ref = f32[112,1024]{1,0:T(8,128)S(1)} custom-call(bf16[208,256]{1,0:T(8,128)(2,1)S(1)} %window.1.after_ref.first_ref, bf16[624,256]{1,0:T(8,128)(2,1)S(1)} %pack.1.rest_ref, bf16[16,512,256]{2,1,0:T(8,128)(2,1)S(1)} %prepare.2.after_ref.top_ref, bf16[16,512,256]{2,1,0:T(8,128)(2,1)S(1)} %prepare.3.after_ref.low_ref), custom_call_target="tpu_custom_call" | custom-call | flops 469762048 | bytes 4194304 | tf_op jit(solution)/shard_map/score/pallas_call | solution.py:40
  23.0 3.5 %adjoint.1 = (f32[1,128]{1,0:T(1,128)}, bf16[112,1024]{1,0:T(8,128)(2,1)S(1)}, bf16[8,112,256]{2,1,0:T(8,128)(2,1)S(1)}) custom-call(bf16[208,256]{1,0:T(8,128)(2,1)S(1)} %collective-permute-done.2.first_ref, bf16[624,256]{1,0:T(8,128)(2,1)S(1)} %collective-permute-done.6.rest_ref, bf16[16,512,256]{2,1,0:T(8,128)(2,1)S(1)} %prepare.2.after_ref.top_ref, ...), custom_call_target="tpu_custom_call" | custom-call | flops 939524096 | bytes 4194304 | tf_op jit(solution)/shard_map/adjoint/pallas_call | solution.py:40
  26.5 0.1 collective-permute-start.7
  26.6 0.8 %mine.1.own_ref = f32[8,112,256]{2,1,0:T(8,128)S(1)} custom-call(bf16[112,1024]{1,0:T(8,128)(2,1)S(1)} %get-tuple-element.17.spread_ref, bf16[16,512,256]{2,1,0:T(8,128)(2,1)S(1)} %prepare.2.after_ref.top_ref, bf16[16,512,256]{2,1,0:T(8,128)(2,1)S(1)} %prepare.3.after_ref.low_ref), custom_call_target="tpu_custom_call" | custom-call | flops 469762048 | bytes 4194304 | tf_op jit(solution)/shard_map/mine/pallas_call | solution.py:40
  27.4 0.9 %collective-permute-done.7.came_ref = bf16[8,112,256]{2,1,0:T(8,128)(2,1)S(1)} collective-permute-done((bf16[8,112,256]{2,1,0:T(8,128)(2,1)S(1)}, bf16[8,112,256]{2,1,0:T(8,128)(2,1)S(1)}, u32[]{:S(2)}, u32[]{:S(2)}) %collective-permute-start.7) | collective-permute-done | bytes 458784 | tf_op jit(solution)/shard_map/ppermute | solution.py:21
  28.4 0.1 join.1
  28.5 1.3 %collective-permute-start.8 = (bf16[64,256]{1,0:T(8,128)(2,1)S(1)}, bf16[64,256]{1,0:T(8,128)(2,1)S(1)}, u32[]{:S(2)}, u32[]{:S(2)}) collective-permute-start(bf16[64,256]{1,0:T(8,128)(2,1)S(1)} %get-tuple-element.20.after_ref), channel_id=1, source_target_pairs={{0,16},{16,0},{1,17},{17,1},{2,18},{18,2},{3,19},{19,3},{4,20},{20... | collective-permute-start | bytes 98312 | tf_op jit(solution)/shard_map/ppermute | solution.py:26
  29.8 1.7 %collective-permute-start.10 = (bf16[192,256]{1,0:T(8,128)(2,1)S(1)}, bf16[192,256]{1,0:T(8,128)(2,1)S(1)}, u32[]{:S(2)}, u32[]{:S(2)}) collective-permute-start(bf16[192,256]{1,0:T(8,128)(2,1)S(1)} %diagonal.1), channel_id=1, source_target_pairs={{0,6},{1,7},{2,4},{3,5},{4,2},{5,3},{6,0},{7,1},{8,14},{9,15},{10,... | collective-permute-start | bytes 294920 | tf_op jit(solution)/shard_map/ppermute | solution.py:21
  31.5 1.0 %collective-permute-done.8.rims_ref = bf16[64,256]{1,0:T(8,128)(2,1)S(1)} collective-permute-done((bf16[64,256]{1,0:T(8,128)(2,1)S(1)}, bf16[64,256]{1,0:T(8,128)(2,1)S(1)}, u32[]{:S(2)}, u32[]{:S(2)}) %collective-permute-start.8) | collective-permute-done | bytes 32800 | tf_op jit(solution)/shard_map/ppermute | solution.py:26
  32.5 1.2 %collective-permute-start.11 = (bf16[192,256]{1,0:T(8,128)(2,1)S(1)}, bf16[192,256]{1,0:T(8,128)(2,1)S(1)}, u32[]{:S(2)}, u32[]{:S(2)}) collective-permute-start(bf16[192,256]{1,0:T(8,128)(2,1)S(1)} %get-tuple-element.23), channel_id=1, source_target_pairs={{0,2},{1,3},{2,0},{3,1},{4,6},{5,7},{6,4},{7,5},{8,10},{9,11},{10,... | collective-permute-start | bytes 294920 | tf_op jit(solution)/shard_map/ppermute | solution.py:21
  33.7 1.6 %collective-permute-start.12 = (bf16[192,256]{1,0:T(8,128)(2,1)S(1)}, bf16[192,256]{1,0:T(8,128)(2,1)S(1)}, u32[]{:S(2)}, u32[]{:S(2)}) collective-permute-start(bf16[192,256]{1,0:T(8,128)(2,1)S(1)} %get-tuple-element.24), channel_id=1, source_target_pairs={{0,4},{1,5},{2,6},{3,7},{4,0},{5,1},{6,2},{7,3},{8,12},{9,13},{10,... | collective-permute-start | bytes 294920 | tf_op jit(solution)/shard_map/ppermute | solution.py:21
  35.2 0.8 %collective-permute-start.9 = (bf16[16,256]{1,0:T(8,128)(2,1)S(1)}, bf16[16,256]{1,0:T(8,128)(2,1)S(1)}, u32[]{:S(2)}, u32[]{:S(2)}) collective-permute-start(bf16[16,256]{1,0:T(8,128)(2,1)S(1)} %get-tuple-element.22), channel_id=1, source_target_pairs={{0,6},{1,7},{2,4},{3,5},{4,2},{5,3},{6,0},{7,1},{8,14},{9,15},{10,... | collective-permute-start | bytes 24584 | tf_op jit(solution)/shard_map/ppermute | solution.py:21
  36.0 3.8 %collective-permute-done.9.edge_ref = bf16[16,256]{1,0:T(8,128)(2,1)S(1)} collective-permute-done((bf16[16,256]{1,0:T(8,128)(2,1)S(1)}, bf16[16,256]{1,0:T(8,128)(2,1)S(1)}, u32[]{:S(2)}, u32[]{:S(2)}) %collective-permute-start.9) | collective-permute-done | bytes 8224 | tf_op jit(solution)/shard_map/ppermute | solution.py:21
  39.8 0.1 sums.1
  39.9 1.1 %collective-permute-start.13 = (bf16[96,256]{1,0:T(8,128)(2,1)S(1)}, bf16[96,256]{1,0:T(8,128)(2,1)S(1)}, u32[]{:S(2)}, u32[]{:S(2)}) collective-permute-start(bf16[96,256]{1,0:T(8,128)(2,1)S(1)} %get-tuple-element.26), channel_id=1, source_target_pairs={{0,8},{1,9},{2,10},{3,11},{4,12},{5,13},{6,14},{7,15},{8,0},{9,1},... | collective-permute-start | bytes 147464 | tf_op jit(solution)/shard_map/ppermute | solution.py:21
  41.0 4.4 %collective-permute-done.13 = bf16[96,256]{1,0:T(8,128)(2,1)S(1)} collective-permute-done((bf16[96,256]{1,0:T(8,128)(2,1)S(1)}, bf16[96,256]{1,0:T(8,128)(2,1)S(1)}, u32[]{:S(2)}, u32[]{:S(2)}) %collective-permute-start.13) | collective-permute-done | bytes 49184 | tf_op jit(solution)/shard_map/ppermute | solution.py:21
  45.4 0.7 %convert_add_fusion = f32[96,256]{1,0:T(8,128)} fusion(f32[96,256]{1,0:T(8,128)S(1)} %get-tuple-element.25, bf16[96,256]{1,0:T(8,128)(2,1)S(1)} %collective-permute-done.13), kind=kLoop, calls=%fused_computation | loop fusion | flops 49152 | bytes 245760 | tf_op jit(solution)/shard_map/add | solution.py:418
  (19 shorter events, 0.1 us)
Async XLA Ops:
  1.5 7.7 %collective-permute-start = (bf16[96,256]{1,0:T(8,128)(2,1)S(1)}, bf16[96,256]{1,0:T(8,128)(2,1)S(1)}, u32[]{:S(2)}, u32[]{:S(2)}) collective-permute-start(bf16[96,256]{1,0:T(8,128)(2,1)S(1)} %convert_element_type.6.after_ref.low_ref), channel_id=1, source_target_pairs={{0,8},{1,9},{2,10},{3,11},{4,12},{5,13},{6,14},{7,15},{8,0},{9,1},... | collective-permute-start | bytes 147464 | tf_op jit(solution)/shard_map/ppermute | solution.py:21
  5.6 0.8 %copy-start = (s32[8,8,32]{2,1,0:T(8,128)S(1)}, s32[8,8,32]{2,1,0:T(8,128)}, u32[]{:S(2)}) copy-start(s32[8,8,32]{2,1,0:T(8,128)} %mask_ref.3) | copy-start | bytes 24580
  9.3 3.9 %collective-permute-start.1 = (bf16[16,256]{1,0:T(8,128)(2,1)S(1)}, bf16[16,256]{1,0:T(8,128)(2,1)S(1)}, u32[]{:S(2)}, u32[]{:S(2)}) collective-permute-start(bf16[16,256]{1,0:T(8,128)(2,1)S(1)} %tails.1.after_ref), channel_id=1, source_target_pairs={{0,16},{16,0},{1,17},{17,1},{2,18},{18,2},{3,19},{19,3},{4,20},{20... | collective-permute-start | bytes 24584 | tf_op jit(solution)/shard_map/ppermute | solution.py:26
  13.1 3.6 %copy-start.1 = (s32[128]{0:T(128)S(1)}, s32[128]{0:T(128)}, u32[]{:S(2)}) copy-start(s32[128]{0:T(128)} %param.10) | copy-start | bytes 1540
  13.2 3.6 %copy-start.2 = (f32[128]{0:T(128)S(1)}, f32[128]{0:T(128)}, u32[]{:S(2)}) copy-start(f32[128]{0:T(128)} %param.11) | copy-start | bytes 1540
  13.2 3.6 %copy-start.3 = (f32[128]{0:T(128)S(1)}, f32[128]{0:T(128)}, u32[]{:S(2)}) copy-start(f32[128]{0:T(128)} %param.12) | copy-start | bytes 1540
  13.2 6.4 %collective-permute-start.5 = (bf16[208,256]{1,0:T(8,128)(2,1)S(1)}, bf16[208,256]{1,0:T(8,128)(2,1)S(1)}, u32[]{:S(2)}, u32[]{:S(2)}) collective-permute-start(bf16[208,256]{1,0:T(8,128)(2,1)S(1)} %window.1.after_ref.first_ref), channel_id=1, source_target_pairs={{0,6},{1,7},{2,4},{3,5},{4,2},{5,3},{6,0},{7,1},{8,14},{9,15},{10,... | collective-permute-start | bytes 319496 | tf_op jit(solution)/shard_map/ppermute | solution.py:21
  15.8 5.0 %collective-permute-start.4 = (bf16[208,256]{1,0:T(8,128)(2,1)S(1)}, bf16[208,256]{1,0:T(8,128)(2,1)S(1)}, u32[]{:S(2)}, u32[]{:S(2)}) collective-permute-start(bf16[208,256]{1,0:T(8,128)(2,1)S(1)} %window.1.after_ref.first_ref), channel_id=1, source_target_pairs={{0,4},{1,5},{2,6},{3,7},{4,0},{5,1},{6,2},{7,3},{8,12},{9,13},{10,... | collective-permute-start | bytes 319496 | tf_op jit(solution)/shard_map/ppermute | solution.py:21
  16.3 4.7 %collective-permute-start.3 = (bf16[208,256]{1,0:T(8,128)(2,1)S(1)}, bf16[208,256]{1,0:T(8,128)(2,1)S(1)}, u32[]{:S(2)}, u32[]{:S(2)}) collective-permute-start(bf16[208,256]{1,0:T(8,128)(2,1)S(1)} %window.1.after_ref.first_ref), channel_id=1, source_target_pairs={{0,2},{1,3},{2,0},{3,1},{4,6},{5,7},{6,4},{7,5},{8,10},{9,11},{10,... | collective-permute-start | bytes 319496 | tf_op jit(solution)/shard_map/ppermute | solution.py:21
  21.0 2.0 %collective-permute-start.6 = (bf16[624,256]{1,0:T(8,128)(2,1)S(1)}, bf16[624,256]{1,0:T(8,128)(2,1)S(1)}, u32[]{:S(2)}, u32[]{:S(2)}) collective-permute-start(bf16[624,256]{1,0:T(8,128)(2,1)S(1)} %pack.1.rest_ref), channel_id=1, source_target_pairs={{0,1},{1,0},{2,3},{3,2},{4,5},{5,4},{6,7},{7,6},{8,9},{9,8},{10,11... | collective-permute-start | bytes 958472 | tf_op jit(solution)/shard_map/ppermute | solution.py:21
  21.1 1.9 %collective-permute-start.2 = (bf16[208,256]{1,0:T(8,128)(2,1)S(1)}, bf16[208,256]{1,0:T(8,128)(2,1)S(1)}, u32[]{:S(2)}, u32[]{:S(2)}) collective-permute-start(bf16[208,256]{1,0:T(8,128)(2,1)S(1)} %window.1.after_ref.first_ref), channel_id=1, source_target_pairs={{0,1},{1,0},{2,3},{3,2},{4,5},{5,4},{6,7},{7,6},{8,9},{9,8},{10,11... | collective-permute-start | bytes 319496 | tf_op jit(solution)/shard_map/ppermute | solution.py:21
  26.5 1.9 %collective-permute-start.7 = (bf16[8,112,256]{2,1,0:T(8,128)(2,1)S(1)}, bf16[8,112,256]{2,1,0:T(8,128)(2,1)S(1)}, u32[]{:S(2)}, u32[]{:S(2)}) collective-permute-start(bf16[8,112,256]{2,1,0:T(8,128)(2,1)S(1)} %get-tuple-element.18), channel_id=1, source_target_pairs={{0,1},{1,0},{2,3},{3,2},{4,5},{5,4},{6,7},{7,6},{8,9},{9,8},{10,11... | collective-permute-start | bytes 1376264 | tf_op jit(solution)/shard_map/ppermute | solution.py:21
  28.5 4.0 %collective-permute-start.8 = (bf16[64,256]{1,0:T(8,128)(2,1)S(1)}, bf16[64,256]{1,0:T(8,128)(2,1)S(1)}, u32[]{:S(2)}, u32[]{:S(2)}) collective-permute-start(bf16[64,256]{1,0:T(8,128)(2,1)S(1)} %get-tuple-element.20.after_ref), channel_id=1, source_target_pairs={{0,16},{16,0},{1,17},{17,1},{2,18},{18,2},{3,19},{19,3},{4,20},{20... | collective-permute-start | bytes 98312 | tf_op jit(solution)/shard_map/ppermute | solution.py:26
  29.8 10.0 %collective-permute-start.10 = (bf16[192,256]{1,0:T(8,128)(2,1)S(1)}, bf16[192,256]{1,0:T(8,128)(2,1)S(1)}, u32[]{:S(2)}, u32[]{:S(2)}) collective-permute-start(bf16[192,256]{1,0:T(8,128)(2,1)S(1)} %diagonal.1), channel_id=1, source_target_pairs={{0,6},{1,7},{2,4},{3,5},{4,2},{5,3},{6,0},{7,1},{8,14},{9,15},{10,... | collective-permute-start | bytes 294920 | tf_op jit(solution)/shard_map/ppermute | solution.py:21
  32.5 7.3 %collective-permute-start.11 = (bf16[192,256]{1,0:T(8,128)(2,1)S(1)}, bf16[192,256]{1,0:T(8,128)(2,1)S(1)}, u32[]{:S(2)}, u32[]{:S(2)}) collective-permute-start(bf16[192,256]{1,0:T(8,128)(2,1)S(1)} %get-tuple-element.23), channel_id=1, source_target_pairs={{0,2},{1,3},{2,0},{3,1},{4,6},{5,7},{6,4},{7,5},{8,10},{9,11},{10,... | collective-permute-start | bytes 294920 | tf_op jit(solution)/shard_map/ppermute | solution.py:21
  33.7 6.1 %collective-permute-start.12 = (bf16[192,256]{1,0:T(8,128)(2,1)S(1)}, bf16[192,256]{1,0:T(8,128)(2,1)S(1)}, u32[]{:S(2)}, u32[]{:S(2)}) collective-permute-start(bf16[192,256]{1,0:T(8,128)(2,1)S(1)} %get-tuple-element.24), channel_id=1, source_target_pairs={{0,4},{1,5},{2,6},{3,7},{4,0},{5,1},{6,2},{7,3},{8,12},{9,13},{10,... | collective-permute-start | bytes 294920 | tf_op jit(solution)/shard_map/ppermute | solution.py:21
  35.2 4.5 %collective-permute-start.9 = (bf16[16,256]{1,0:T(8,128)(2,1)S(1)}, bf16[16,256]{1,0:T(8,128)(2,1)S(1)}, u32[]{:S(2)}, u32[]{:S(2)}) collective-permute-start(bf16[16,256]{1,0:T(8,128)(2,1)S(1)} %get-tuple-element.22), channel_id=1, source_target_pairs={{0,6},{1,7},{2,4},{3,5},{4,2},{5,3},{6,0},{7,1},{8,14},{9,15},{10,... | collective-permute-start | bytes 24584 | tf_op jit(solution)/shard_map/ppermute | solution.py:21
  39.9 5.5 %collective-permute-start.13 = (bf16[96,256]{1,0:T(8,128)(2,1)S(1)}, bf16[96,256]{1,0:T(8,128)(2,1)S(1)}, u32[]{:S(2)}, u32[]{:S(2)}) collective-permute-start(bf16[96,256]{1,0:T(8,128)(2,1)S(1)} %get-tuple-element.26), channel_id=1, source_target_pairs={{0,8},{1,9},{2,10},{3,11},{4,12},{5,13},{6,14},{7,15},{8,0},{9,1},... | collective-permute-start | bytes 147464 | tf_op jit(solution)/shard_map/ppermute | solution.py:21

commit v3 on v2

--- a/solution.py
+++ b/solution.py
@@ -49,7 +49,7 @@
     )(*operands)
 
 
-def prepare_kernel(devices, start, foot_hbm, mask_ref, after_ref, masked_ref, foot_ref, sems):
+def prepare_kernel(devices, first, foot_hbm, mask_ref, after_ref, masked_ref, foot_ref, sems):
     del after_ref
     me = lax.axis_index("rcpt")
     blocks, lags, tiles = mask_ref.shape
@@ -59,7 +59,6 @@
     group = 2 * lags
     part = foot_hbm.shape[0] // blocks
     used = depth // part
-    first = start * used
     copies = []
     for b in range(used):
         source = foot_hbm.at[pl.ds((first + b) * part, part)]
@@ -80,12 +79,11 @@
                 masked_ref[me ^ d, at, :] = foot_ref[at, cut] * keep
 
 
-def prepare(foot, mask, after, devices, start):
+def prepare(foot, mask, after, devices, first, blocks):
     depth, cells = foot.shape
-    depth //= 2
-    blocks = mask.shape[0] // 2
+    depth = depth // mask.shape[0] * blocks
     return call(
-        functools.partial(prepare_kernel, devices, start),
+        functools.partial(prepare_kernel, devices, first),
         [((devices, depth, cells // devices), BF16)],
         [foot, mask, after],
         "ava",
@@ -100,23 +98,28 @@
 def choose_kernel(lags, hours, hour_ref, obs_ref, weight_ref, count_ref, after_ref, select_ref, line_ref):
     del after_ref
     rows = hour_ref.shape[1]
-    times = jnp.broadcast_to(hour_ref[...].astype(F32), (8, rows)).astype(BF16)
-    spread = jnp.dot(times, expander(rows, lags, BF16), preferred_element_type=F32)
+    live = (lax.broadcasted_iota(jnp.int32, (1, rows), 1) < count_ref[0]).astype(F32)
+    sides = [live * weight_ref[...], obs_ref[...], hour_ref[...].astype(F32)]
+    sides = jnp.concatenate([jnp.broadcast_to(side, (8, rows)) for side in sides], axis=0)
+    wide = jnp.dot(
+        sides,
+        expander(rows, lags, F32),
+        precision=lax.Precision.HIGHEST,
+        preferred_element_type=F32,
+    )
+    line_ref[...] = wide[: 2 * 8]
     column = lax.broadcasted_iota(jnp.int32, (1, rows * lags), 1)
-    hour = spread[:1].astype(jnp.int32) - lax.rem(column, lags)
+    hour = wide[2 * 8 : 2 * 8 + 1].astype(jnp.int32) - lax.rem(column, lags)
     slot = jnp.where(hour >= 0, hour, hour + (hours + RIM))
     wanted = lax.broadcasted_iota(jnp.int32, select_ref.shape, 0)
     select_ref[...] = (wanted == slot).astype(F32)
-    live = (lax.broadcasted_iota(jnp.int32, (1, rows), 1) < count_ref[0]).astype(F32)
-    line_ref[0:1] = live * weight_ref[...]
-    line_ref[1:2] = obs_ref[...]
 
 
 def choose(hour, obs, weight, count, after, lags, hours):
     rows = hour.shape[1]
     return call(
         functools.partial(choose_kernel, lags, hours),
-        [((hours + PAIR, rows * lags), F32), ((8, rows), F32)],
+        [((hours + PAIR, rows * lags), F32), ((2 * 8, rows * lags), F32)],
         [hour, obs, weight, count, after],
         "vvvsa",
         flops=BUSY,
@@ -165,10 +168,18 @@
     return call(pack_kernel, outs, operands, "v" * len(operands), name="pack")[0]
 
 
+def row_spans(masked_refs):
+    spans, at = [], 0
+    for masked_ref in masked_refs:
+        spans.append(slice(at, at + masked_ref.shape[1]))
+        at += masked_ref.shape[1]
+    return spans
+
+
 def add_scores(windows, masked_refs, start, score_ref, window_ref):
     hours = window_ref.shape[0] - PAIR
     half = masked_refs[0].shape[0] // 2
-    depth = masked_refs[0].shape[1]
+    spans = row_spans(masked_refs)
     for i, read in enumerate(windows):
         rims = read(slice(2 * hours, 2 * hours + PAIR)).astype(F32)
         gap = jnp.zeros_like(rims[:RIM])
@@ -178,8 +189,7 @@
             window_ref[hours:] = jnp.concatenate([rim, gap], axis=0).astype(BF16)
             k = (j * half + 2 * i) ^ start
             dims = (((1,), (1,)), ((), ()))
-            for n, masked_ref in enumerate(masked_refs):
-                at = slice(n * depth, (n + 1) * depth)
+            for at, masked_ref in zip(spans, masked_refs):
                 term = lax.dot_general(
                     window_ref[...], masked_ref[k], dims, preferred_element_type=F32
                 )
@@ -206,8 +216,8 @@
 
 
 def score(first, rest, masked):
-    devices, depth, own = masked[0].shape
-    depth *= 2
+    devices, _, own = masked[0].shape
+    depth = sum(part.shape[1] for part in masked)
     width = first.shape[0] // 2 - RIM + PAIR
     return call(
         score_kernel,
@@ -222,50 +232,51 @@
 
 
 def terms(spread_ref, masked_refs, k):
-    depth = masked_refs[0].shape[1]
     total = None
-    for n, masked_ref in enumerate(masked_refs):
-        at = slice(n * depth, (n + 1) * depth)
+    for at, masked_ref in zip(row_spans(masked_refs), masked_refs):
         term = jnp.dot(spread_ref[:, at], masked_ref[k], preferred_element_type=F32)
         total = term if total is None else total + term
     return total
 
 
+def group_sums(values, lags):
+    lane = lax.broadcasted_iota(jnp.int32, values.shape, 1)
+    size = values.shape[1]
+    step = 1
+    while step < lags:
+        up, down = pltpu.roll(values, step, 1), pltpu.roll(values, size - step, 1)
+        values = values + jnp.where((lane & step) != 0, up, down)
+        step *= 2
+    return values
+
+
 def adjoint_kernel(
-    first_ref, rest_ref, top_ref, low_ref, begun_ref, select_ref, line_ref,
+    lags, first_ref, rest_ref, top_ref, low_ref, begun_ref, select_ref, line_ref,
     mism_ref, spread_ref, other_ref, score_ref, window_ref,
 ):
-    depth = score_ref.shape[1]
-    rows = mism_ref.shape[1]
-    lags = depth // rows
+    width, depth = score_ref.shape
     score_ref[...] = begun_ref[...]
     add_scores(readers(first_ref, rest_ref), (top_ref, low_ref), 1, score_ref, window_ref)
     line = jnp.sum(score_ref[...] * select_ref[...], axis=0, keepdims=True)
-    belongs = expander(rows, lags, F32)
-    model = lax.dot_general(
-        jnp.broadcast_to(line, (8, depth)),
-        belongs,
-        (((1,), (1,)), ((), ())),
-        precision=lax.Precision.HIGHEST,
-        preferred_element_type=F32,
-    )[:1]
-    mism = line_ref[0:1] * (model - line_ref[1:2])
+    model = group_sums(jnp.broadcast_to(line, (8, depth)), lags)
+    mism = line_ref[:8] * (model - line_ref[8:])
     mism_ref[...] = mism
-    weighted = jnp.broadcast_to(mism, (8, rows)).astype(BF16)
-    wide = jnp.dot(weighted, belongs.astype(BF16), preferred_element_type=F32)[:1]
-    spread_ref[...] = (select_ref[...] * wide).astype(BF16)
+    weighted = mism.astype(BF16).astype(F32)
+    for i in range(0, width, PAIR):
+        rows = [select_ref[i + j : i + j + 8] * weighted for j in (0, 8)]
+        spread_ref[i : i + PAIR] = jnp.concatenate(rows, axis=0).astype(BF16)
     for k in range(top_ref.shape[0] // 2):
         other_ref[k] = terms(spread_ref, (top_ref, low_ref), 2 * k + 1).astype(BF16)
 
 
-def adjoint(first, rest, masked, begun, select, lines):
-    devices, depth, own = masked[0].shape
-    depth *= 2
+def adjoint(first, rest, masked, begun, select, lines, lags):
+    devices, _, own = masked[0].shape
+    depth = sum(part.shape[1] for part in masked)
     width = begun.shape[0]
     return call(
-        adjoint_kernel,
+        functools.partial(adjoint_kernel, lags),
         [
-            ((1, lines.shape[1]), F32),
+            ((8, depth), F32),
             ((width, depth), BF16),
             ((devices // 2, width, own), BF16),
         ],
@@ -284,8 +295,8 @@
 
 
 def mine_part(spread, masked):
-    devices, depth, own = masked[0].shape
-    depth *= 2
+    devices, _, own = masked[0].shape
+    depth = sum(part.shape[1] for part in masked)
     width = spread.shape[0]
     return call(
         mine_kernel,
@@ -296,6 +307,26 @@
         moved=depth * own * devices,
         name="mine",
     )[0]
+
+
+def narrow_kernel(mism_ref, after_ref, out_ref):
+    del after_ref
+    rows, depth = out_ref.shape[1], mism_ref.shape[1]
+    row, column = (lax.broadcasted_iota(jnp.int32, (rows, depth), i) for i in range(2))
+    first = (column == row * (depth // rows)).astype(F32)
+    narrow = lax.dot_general(
+        mism_ref[...],
+        first,
+        (((1,), (1,)), ((), ())),
+        precision=lax.Precision.HIGHEST,
+        preferred_element_type=F32,
+    )
+    out_ref[...] = narrow[:1]
+
+
+def narrow(mism, after, rows):
+    outs = [((1, rows), F32)]
+    return call(narrow_kernel, outs, [mism, after], "va", flops=BUSY, name="narrow")[0]
 
 
 def join_kernel(own_ref, came_ref, main_ref, rims_ref):
@@ -320,61 +351,44 @@
     return call(join_kernel, outs, [own, came], "vv", name="join")
 
 
-def diagonal_kernel(main_ref, after_ref, out_ref):
-    del after_ref
-    out_ref[...] = main_ref[main_ref.shape[0] - 1].astype(BF16)
-
-
-def diagonal(main, after):
-    outs = [(main.shape[1:], BF16)]
-    return call(diagonal_kernel, outs, [main, after], "vv", flops=BUSY, name="diagonal")[0]
-
-
-def with_rims(both, rims):
-    hours = both.shape[0] // 2
-    pieces = []
-    for j in range(2):
-        at = (j + 1) * hours - RIM
-        pieces.append(both[j * hours : at])
-        pieces.append(both[at : at + RIM] + rims[j * RIM : (j + 1) * RIM])
-    return jnp.concatenate(pieces, axis=0)
-
-
-def shares_kernel(main_ref, rims_ref, first_ref, edge_ref, *outs):
+def with_rims(main_ref, rims_ref, i, j):
+    hours = main_ref.shape[1] // 2
     inside = (lax.axis_index("hour") < lax.axis_size("hour") - 1).astype(F32)
-    for i in range(main_ref.shape[0]):
-        rims = rims_ref[i * PAIR : (i + 1) * PAIR].astype(F32) * inside
-        if i == 0:
-            first_ref[...] = with_rims(main_ref[i], rims)
-        elif i == main_ref.shape[0] - 1:
-            edge_ref[...] = rims.astype(BF16)
-        else:
-            outs[i - 1][...] = with_rims(main_ref[i], rims).astype(BF16)
-
-
-def shares(main, rims):
+    rims = rims_ref[i * PAIR : (i + 1) * PAIR].astype(F32) * inside
+    at = (j + 1) * hours - RIM
+    last = main_ref[i, at : at + RIM] + rims[j * RIM : (j + 1) * RIM]
+    return jnp.concatenate([main_ref[i, j * hours : at], last], axis=0)
+
+
+def shares_kernel(j, main_ref, rims_ref, after_ref, first_ref, *outs):
+    del after_ref
+    first_ref[...] = with_rims(main_ref, rims_ref, 0, j)
+    for i, out in enumerate(outs):
+        out[...] = with_rims(main_ref, rims_ref, i + 1, j).astype(BF16)
+
+
+def shares(main, rims, j, after):
     count, both, columns = main.shape
-    outs = [((both, columns), F32), ((PAIR, columns), BF16)]
-    outs += [((both, columns), BF16)] * (count - 2)
-    return call(shares_kernel, outs, [main, rims], "vv", name="shares")
-
-
-def sums_kernel(first_ref, edge_ref, *refs):
-    *arrived, total_ref, relay_ref = refs
-    hours = total_ref.shape[0]
+    shape = (both // 2, columns)
+    outs = [(shape, F32)] + [(shape, BF16)] * (count - 1)
+    first, *parts = call(
+        functools.partial(shares_kernel, j), outs, [main, rims, after], "vva", flops=BUSY, name="shares"
+    )
+    return first, parts
+
+
+def outward_kernel(first_ref, *refs):
+    *arrived, out_ref = refs
     total = first_ref[...]
     for piece in arrived:
         total += piece[...].astype(F32)
-    total = with_rims(total, edge_ref[...].astype(F32))
-    total_ref[...] = total[:hours]
-    relay_ref[...] = total[hours:].astype(BF16)
-
-
-def sums(first, edge, arrived):
-    both, columns = first.shape
-    main = (both // 2, columns)
-    operands = [first, edge, *arrived]
-    return call(sums_kernel, [(main, F32), (main, BF16)], operands, "v" * len(operands), name="sums")
+    out_ref[...] = total.astype(out_ref.dtype)
+
+
+def outward(first, arrived, dtype):
+    operands = [first, *arrived]
+    outs = [(first.shape, dtype)]
+    return call(outward_kernel, outs, operands, "v" * len(operands), name="outward")[0]
 
 
 def per_device(flux, footprint, tile_mask, rec_hour, observed, obs_weight, site_count):
@@ -382,15 +396,16 @@
     rows, lags, cells = footprint.shape
     devices = cells // own
     far = devices // 2
-    near = range(2, far - 2, 2)
-    diag = far - 2
+    near = range(2, far, 2)
 
     low = flux.astype(BF16)
     far_low = swap(low, far)
     foot = footprint.reshape(rows * lags, cells)
-    top = prepare(foot, tile_mask, low, devices, 0)
+    blocks = tile_mask.shape[0]
+    head = blocks * 5 // 8
+    top = prepare(foot, tile_mask, low, devices, 0, head)
     ends = tails(low, far_low, top)
-    bottom = prepare(foot, tile_mask, ends, devices, 1)
+    bottom = prepare(foot, tile_mask, ends, devices, head, blocks - head)
     first = window(low, far_low, turn(ends, 1), bottom)
     parts = [swap(first, k) for k in range(2, far, 2)]
     other_first = swap(first, 1)
@@ -406,15 +421,19 @@
     rest = pack(parts, lines)
     masked = (top, bottom)
     begun = score(first, rest, masked)
-    mism, spread, other = adjoint(other_first, swap(rest, 1), masked, begun, select, lines)
+    mism, spread, other = adjoint(
+        other_first, swap(rest, 1), masked, begun, select, lines, lags
+    )
 
     main, rims = join(mine_part(spread, masked), swap(other, 1))
     back = turn(rims, -1)
-    diag_main = swap(diagonal(main, rims), diag)
-    first, edge, *outward = shares(main, back)
-    arrived = [swap(part, k) for part, k in zip(outward, near)]
-    edge = swap(edge, diag)
-    total, relay = sums(first, edge, [diag_main, *arrived])
+    far_sum, parts = shares(main, back, 1, rims)
+    passed = [swap(part, k) for part, k in zip(parts, near)]
+    near_sum, others = shares(main, back, 0, parts[0])
+    arrived = [swap(part, k) for part, k in zip(others, near)]
+    mism = narrow(mism, far_sum, rows)
+    relay = outward(far_sum, passed, BF16)
+    total = outward(near_sum, arrived, F32)
     gradient = total + swap(relay, far).astype(F32)
     return (gradient, mism.reshape(rows))
 

time: 46.3 us -> 44.7 us (0.965)
  waiting for transfers between devices: 14.1 us -> 10.2 us
  starting transfers between devices: 17.5 us -> 19.5 us
    ppermute x12 -> x14, waiting for transfers between devices: 13.1 us -> 7.56 us  [swap(): return lax.ppermute(block, 'rcpt', [(i, i ^ bit) for i in devices])]
    ppermute x12 -> x14, starting transfers between devices: 14.6 us -> 16.4 us  [swap(): return lax.ppermute(block, 'rcpt', [(i, i ^ bit) for i in devices])]
    ppermute x2, waiting for transfers between devices: 0.97 us -> 2.6 us  [turn(): lax.ppermute(block, 'hour', [(i, (i + distance) % size) for i in range(si...]
    pallas_call x13 -> x15, Pallas kernels: 10.7 us -> 11 us  [call(): pl.pallas_call(kernel, in_specs=[pl.BlockSpec(memory_space=where[c]) for...]
  transfers between devices with their start and end apart: 14 -> 16, of which waited for: 7 -> 8; matrix products, arithmetic and copies ran while one was open for 0% -> 0% of each run, Pallas kernels for 15% -> 19%
where the time goes in v3:
time: 44.7 us; the launch traced here: 44.4 us
  starting transfers between devices  19.5 us (44%)
  Pallas kernels  11 us (25%)
  waiting for transfers between devices  10.2 us (23%)
  other arithmetic  1.55 us (3%)
  between operations  1.43 us (3%)
  local copies, waits for them, and re-layouts  0.78 us (2%)
    ppermute x14, starting transfers between devices, swap(): return lax.ppermute(block, 'rcpt', [(i, i ^ bit) for i in devices])  16.4 us
    pallas_call x15, Pallas kernels, call(): pl.pallas_call(kernel, in_specs=[pl.BlockSpec(memory_space=where[c]) for...  11 us
    ppermute x14, waiting for transfers between devices, swap(): return lax.ppermute(block, 'rcpt', [(i, i ^ bit) for i in devices])  7.56 us
    ppermute x2, starting transfers between devices, turn(): lax.ppermute(block, 'hour', [(i, (i + distance) % size) for i in range(si...  3.12 us
    ppermute x2, waiting for transfers between devices, turn(): lax.ppermute(block, 'hour', [(i, (i + distance) % size) for i in range(si...  2.6 us
    convert_element_type x1, other arithmetic, per_device(): low = flux.astype(BF16)  0.9 us
  transfers between devices with their start and end apart: 16, of which 8 were waited for; matrix products, arithmetic and copies ran while one was open for 0% of the time, Pallas kernels for 19%

profile of v3, /device:TPU:0, one launch (start us, length us, event | category | flops | bytes accessed | tf_op | source)
XLA Modules:
  0.0 44.4 jit_solution(4745132648147171478)
XLA Ops:
  0.6 0.9 %convert_element_type.6.after_ref.low_ref = bf16[96,256]{1,0:T(8,128)(2,1)S(1)} convert(f32[96,256]{1,0:T(8,128)} %param.7) | non-fusion elementwise | flops 24576 | bytes 147456 | tf_op jit(solution)/shard_map/convert_element_type | solution.py:401
  1.5 4.0 %collective-permute-start = (bf16[96,256]{1,0:T(8,128)(2,1)S(1)}, bf16[96,256]{1,0:T(8,128)(2,1)S(1)}, u32[]{:S(2)}, u32[]{:S(2)}) collective-permute-start(bf16[96,256]{1,0:T(8,128)(2,1)S(1)} %convert_element_type.6.after_ref.low_ref), channel_id=1, source_target_pairs={{0,8},{1,9},{2,10},{3,11},{4,12},{5,13},{6,14},{7,15},{8,0},{9,1},... | collective-permute-start | bytes 147464 | tf_op jit(solution)/shard_map/ppermute | solution.py:21
  5.6 0.8 %copy-done = s32[8,8,32]{2,1,0:T(8,128)S(1)} copy-done((s32[8,8,32]{2,1,0:T(8,128)S(1)}, s32[8,8,32]{2,1,0:T(8,128)}, u32[]{:S(2)}) %copy-start) | copy-done | bytes 8216
  6.3 2.6 %prepare.2.after_ref.top_ref = bf16[16,640,256]{2,1,0:T(8,128)(2,1)S(1)} custom-call(bf16[1024,4096]{1,0:T(8,128)(2,1)} %bitcast.8, s32[8,8,32]{2,1,0:T(8,128)S(1)} %copy-done, bf16[96,256]{1,0:T(8,128)(2,1)S(1)} %convert_element_type.6.after_ref.low_ref), custom_call_target="tpu_custom_call" | custom-call | flops 10000000000 | bytes 10485760 | tf_op jit(solution)/shard_map/prepare/pallas_call | solution.py:40
  9.7 1.6 %collective-permute-start.1 = (bf16[16,256]{1,0:T(8,128)(2,1)S(1)}, bf16[16,256]{1,0:T(8,128)(2,1)S(1)}, u32[]{:S(2)}, u32[]{:S(2)}) collective-permute-start(bf16[16,256]{1,0:T(8,128)(2,1)S(1)} %tails.1.after_ref), channel_id=1, source_target_pairs={{0,16},{16,0},{1,17},{17,1},{2,18},{18,2},{3,19},{19,3},{4,20},{20... | collective-permute-start | bytes 24584 | tf_op jit(solution)/shard_map/ppermute | solution.py:26
  11.2 2.0 %prepare.3.after_ref.low_ref = bf16[16,384,256]{2,1,0:T(8,128)(2,1)S(1)} custom-call(bf16[1024,4096]{1,0:T(8,128)(2,1)} %bitcast.9, s32[8,8,32]{2,1,0:T(8,128)S(1)} %copy-done, bf16[16,256]{1,0:T(8,128)(2,1)S(1)} %tails.1.after_ref), custom_call_target="tpu_custom_call" | custom-call | flops 10000000000 | bytes 6291456 | tf_op jit(solution)/shard_map/prepare/pallas_call | solution.py:40
  13.2 0.2 collective-permute-done.1.rims_ref
  13.4 2.6 %collective-permute-start.5 = (bf16[208,256]{1,0:T(8,128)(2,1)S(1)}, bf16[208,256]{1,0:T(8,128)(2,1)S(1)}, u32[]{:S(2)}, u32[]{:S(2)}) collective-permute-start(bf16[208,256]{1,0:T(8,128)(2,1)S(1)} %window.1.after_ref.first_ref), channel_id=1, source_target_pairs={{0,6},{1,7},{2,4},{3,5},{4,2},{5,3},{6,0},{7,1},{8,14},{9,15},{10,... | collective-permute-start | bytes 319496 | tf_op jit(solution)/shard_map/ppermute | solution.py:21
  16.0 0.4 %collective-permute-start.4 = (bf16[208,256]{1,0:T(8,128)(2,1)S(1)}, bf16[208,256]{1,0:T(8,128)(2,1)S(1)}, u32[]{:S(2)}, u32[]{:S(2)}) collective-permute-start(bf16[208,256]{1,0:T(8,128)(2,1)S(1)} %window.1.after_ref.first_ref), channel_id=1, source_target_pairs={{0,4},{1,5},{2,6},{3,7},{4,0},{5,1},{6,2},{7,3},{8,12},{9,13},{10,... | collective-permute-start | bytes 319496 | tf_op jit(solution)/shard_map/ppermute | solution.py:21
  16.4 0.5 %collective-permute-start.3 = (bf16[208,256]{1,0:T(8,128)(2,1)S(1)}, bf16[208,256]{1,0:T(8,128)(2,1)S(1)}, u32[]{:S(2)}, u32[]{:S(2)}) collective-permute-start(bf16[208,256]{1,0:T(8,128)(2,1)S(1)} %window.1.after_ref.first_ref), channel_id=1, source_target_pairs={{0,2},{1,3},{2,0},{3,1},{4,6},{5,7},{6,4},{7,5},{8,10},{9,11},{10,... | collective-permute-start | bytes 319496 | tf_op jit(solution)/shard_map/ppermute | solution.py:21
  17.0 0.5 %choose.1 = (f32[112,1024]{1,0:T(8,128)S(1)}, f32[16,1024]{1,0:T(8,128)S(1)}) custom-call(s32[1,128]{1,0:T(1,128)S(1)} %bitcast.5, f32[1,128]{1,0:T(1,128)S(1)} %bitcast.6, f32[1,128]{1,0:T(1,128)S(1)} %bitcast.7, s32[1]{0:T(128)S(6)} %copy.9.count_ref, bf16[208,256]{1,0:T(8,128)(2,1)S(1)} %window.1.after_ref.first_ref), custom_call_target="tpu_custom_call" | custom-call | flops 10000000000 | tf_op jit(solution)/shard_map/choose/pallas_call | solution.py:40
  17.5 2.2 %collective-permute-done.5.refs_2_ = bf16[208,256]{1,0:T(8,128)(2,1)S(1)} collective-permute-done((bf16[208,256]{1,0:T(8,128)(2,1)S(1)}, bf16[208,256]{1,0:T(8,128)(2,1)S(1)}, u32[]{:S(2)}, u32[]{:S(2)}) %collective-permute-start.5) | collective-permute-done | bytes 106528 | tf_op jit(solution)/shard_map/ppermute | solution.py:21
  19.7 1.1 %collective-permute-done.4.refs_1_ = bf16[208,256]{1,0:T(8,128)(2,1)S(1)} collective-permute-done((bf16[208,256]{1,0:T(8,128)(2,1)S(1)}, bf16[208,256]{1,0:T(8,128)(2,1)S(1)}, u32[]{:S(2)}, u32[]{:S(2)}) %collective-permute-start.4) | collective-permute-done | bytes 106528 | tf_op jit(solution)/shard_map/ppermute | solution.py:21
  20.8 0.3 collective-permute-done.3.refs_0_
  21.2 0.5 %collective-permute-start.2 = (bf16[208,256]{1,0:T(8,128)(2,1)S(1)}, bf16[208,256]{1,0:T(8,128)(2,1)S(1)}, u32[]{:S(2)}, u32[]{:S(2)}) collective-permute-start(bf16[208,256]{1,0:T(8,128)(2,1)S(1)} %window.1.after_ref.first_ref), channel_id=1, source_target_pairs={{0,1},{1,0},{2,3},{3,2},{4,5},{5,4},{6,7},{7,6},{8,9},{9,8},{10,11... | collective-permute-start | bytes 319496 | tf_op jit(solution)/shard_map/ppermute | solution.py:21
  21.7 1.3 %score.1.begun_ref = f32[112,1024]{1,0:T(8,128)S(1)} custom-call(bf16[208,256]{1,0:T(8,128)(2,1)S(1)} %window.1.after_ref.first_ref, bf16[624,256]{1,0:T(8,128)(2,1)S(1)} %pack.1.rest_ref, bf16[16,640,256]{2,1,0:T(8,128)(2,1)S(1)} %prepare.2.after_ref.top_ref, bf16[16,384,256]{2,1,0:T(8,128)(2,1)S(1)} %prepare.3.after_ref.low_ref), custom_call_target="tpu_custom_call" | custom-call | flops 469762048 | bytes 4194304 | tf_op jit(solution)/shard_map/score/pallas_call | solution.py:40
  23.1 2.5 %adjoint.1 = (f32[8,1024]{1,0:T(8,128)S(1)}, bf16[112,1024]{1,0:T(8,128)(2,1)S(1)}, bf16[8,112,256]{2,1,0:T(8,128)(2,1)S(1)}) custom-call(bf16[208,256]{1,0:T(8,128)(2,1)S(1)} %collective-permute-done.2.first_ref, bf16[624,256]{1,0:T(8,128)(2,1)S(1)} %collective-permute-done.6.rest_ref, bf16[16,640,256]{2,1,0:T(8,128)(2,1)S(1)} %prepare.2.after_ref.top_ref, ...), custom_call_target="tpu_custom_call" | custom-call | flops 939524096 | bytes 4194304 | tf_op jit(solution)/shard_map/adjoint/pallas_call | solution.py:40
  25.7 0.8 %mine.1.own_ref = f32[8,112,256]{2,1,0:T(8,128)S(1)} custom-call(bf16[112,1024]{1,0:T(8,128)(2,1)S(1)} %get-tuple-element.19.spread_ref, bf16[16,640,256]{2,1,0:T(8,128)(2,1)S(1)} %prepare.2.after_ref.top_ref, bf16[16,384,256]{2,1,0:T(8,128)(2,1)S(1)} %prepare.3.after_ref.low_ref), custom_call_target="tpu_custom_call" | custom-call | flops 469762048 | bytes 4194304 | tf_op jit(solution)/shard_map/mine/pallas_call | solution.py:40
  26.6 0.9 %collective-permute-done.7.came_ref = bf16[8,112,256]{2,1,0:T(8,128)(2,1)S(1)} collective-permute-done((bf16[8,112,256]{2,1,0:T(8,128)(2,1)S(1)}, bf16[8,112,256]{2,1,0:T(8,128)(2,1)S(1)}, u32[]{:S(2)}, u32[]{:S(2)}) %collective-permute-start.7) | collective-permute-done | bytes 458784 | tf_op jit(solution)/shard_map/ppermute | solution.py:21
  27.5 1.6 %collective-permute-start.8 = (bf16[64,256]{1,0:T(8,128)(2,1)S(1)}, bf16[64,256]{1,0:T(8,128)(2,1)S(1)}, u32[]{:S(2)}, u32[]{:S(2)}) collective-permute-start(bf16[64,256]{1,0:T(8,128)(2,1)S(1)} %get-tuple-element.22.after_ref), channel_id=1, source_target_pairs={{0,16},{16,0},{1,17},{17,1},{2,18},{18,2},{3,19},{19,3},{4,20},{20... | collective-permute-start | bytes 98312 | tf_op jit(solution)/shard_map/ppermute | solution.py:26
  29.1 2.4 %collective-permute-done.8.rims_ref = bf16[64,256]{1,0:T(8,128)(2,1)S(1)} collective-permute-done((bf16[64,256]{1,0:T(8,128)(2,1)S(1)}, bf16[64,256]{1,0:T(8,128)(2,1)S(1)}, u32[]{:S(2)}, u32[]{:S(2)}) %collective-permute-start.8) | collective-permute-done | bytes 32800 | tf_op jit(solution)/shard_map/ppermute | solution.py:26
  31.5 1.6 %collective-permute-start.13 = (bf16[96,256]{1,0:T(8,128)(2,1)S(1)}, bf16[96,256]{1,0:T(8,128)(2,1)S(1)}, u32[]{:S(2)}, u32[]{:S(2)}) collective-permute-start(bf16[96,256]{1,0:T(8,128)(2,1)S(1)} %get-tuple-element.29), channel_id=1, source_target_pairs={{0,4},{1,5},{2,6},{3,7},{4,0},{5,1},{6,2},{7,3},{8,12},{9,13},{10,... | collective-permute-start | bytes 147464 | tf_op jit(solution)/shard_map/ppermute | solution.py:21
  33.2 1.0 %collective-permute-start.14 = (bf16[96,256]{1,0:T(8,128)(2,1)S(1)}, bf16[96,256]{1,0:T(8,128)(2,1)S(1)}, u32[]{:S(2)}, u32[]{:S(2)}) collective-permute-start(bf16[96,256]{1,0:T(8,128)(2,1)S(1)} %get-tuple-element.30), channel_id=1, source_target_pairs={{0,6},{1,7},{2,4},{3,5},{4,2},{5,3},{6,0},{7,1},{8,14},{9,15},{10,... | collective-permute-start | bytes 147464 | tf_op jit(solution)/shard_map/ppermute | solution.py:21
  34.2 0.9 %collective-permute-start.12 = (bf16[96,256]{1,0:T(8,128)(2,1)S(1)}, bf16[96,256]{1,0:T(8,128)(2,1)S(1)}, u32[]{:S(2)}, u32[]{:S(2)}) collective-permute-start(bf16[96,256]{1,0:T(8,128)(2,1)S(1)} %get-tuple-element.23.after_ref), channel_id=1, source_target_pairs={{0,2},{1,3},{2,0},{3,1},{4,6},{5,7},{6,4},{7,5},{8,10},{9,11},{10,... | collective-permute-start | bytes 147464 | tf_op jit(solution)/shard_map/ppermute | solution.py:21
  35.1 1.1 %collective-permute-start.9 = (bf16[96,256]{1,0:T(8,128)(2,1)S(1)}, bf16[96,256]{1,0:T(8,128)(2,1)S(1)}, u32[]{:S(2)}, u32[]{:S(2)}) collective-permute-start(bf16[96,256]{1,0:T(8,128)(2,1)S(1)} %get-tuple-element.25), channel_id=1, source_target_pairs={{0,2},{1,3},{2,0},{3,1},{4,6},{5,7},{6,4},{7,5},{8,10},{9,11},{10,... | collective-permute-start | bytes 147464 | tf_op jit(solution)/shard_map/ppermute | solution.py:21
  36.3 1.5 %collective-permute-start.10 = (bf16[96,256]{1,0:T(8,128)(2,1)S(1)}, bf16[96,256]{1,0:T(8,128)(2,1)S(1)}, u32[]{:S(2)}, u32[]{:S(2)}) collective-permute-start(bf16[96,256]{1,0:T(8,128)(2,1)S(1)} %get-tuple-element.26), channel_id=1, source_target_pairs={{0,4},{1,5},{2,6},{3,7},{4,0},{5,1},{6,2},{7,3},{8,12},{9,13},{10,... | collective-permute-start | bytes 147464 | tf_op jit(solution)/shard_map/ppermute | solution.py:21
  37.8 0.9 %collective-permute-start.11 = (bf16[96,256]{1,0:T(8,128)(2,1)S(1)}, bf16[96,256]{1,0:T(8,128)(2,1)S(1)}, u32[]{:S(2)}, u32[]{:S(2)}) collective-permute-start(bf16[96,256]{1,0:T(8,128)(2,1)S(1)} %get-tuple-element.27), channel_id=1, source_target_pairs={{0,6},{1,7},{2,4},{3,5},{4,2},{5,3},{6,0},{7,1},{8,14},{9,15},{10,... | collective-permute-start | bytes 147464 | tf_op jit(solution)/shard_map/ppermute | solution.py:21
  38.7 1.0 %collective-permute-start.15 = (bf16[96,256]{1,0:T(8,128)(2,1)S(1)}, bf16[96,256]{1,0:T(8,128)(2,1)S(1)}, u32[]{:S(2)}, u32[]{:S(2)}) collective-permute-start(bf16[96,256]{1,0:T(8,128)(2,1)S(1)} %outward.3), channel_id=1, source_target_pairs={{0,8},{1,9},{2,10},{3,11},{4,12},{5,13},{6,14},{7,15},{8,0},{9,1},... | collective-permute-start | bytes 147464 | tf_op jit(solution)/shard_map/ppermute | solution.py:21
  39.8 1.0 %narrow.1 = f32[1,128]{1,0:T(1,128)} custom-call(f32[8,1024]{1,0:T(8,128)S(1)} %get-tuple-element.31.mism_ref, f32[96,256]{1,0:T(8,128)S(1)} %get-tuple-element.28.first_ref.after_ref), custom_call_target="tpu_custom_call" | custom-call | flops 10000000000 | tf_op jit(solution)/shard_map/narrow/pallas_call | solution.py:40
  40.8 2.0 %collective-permute-done.11.refs_2_ = bf16[96,256]{1,0:T(8,128)(2,1)S(1)} collective-permute-done((bf16[96,256]{1,0:T(8,128)(2,1)S(1)}, bf16[96,256]{1,0:T(8,128)(2,1)S(1)}, u32[]{:S(2)}, u32[]{:S(2)}) %collective-permute-start.11) | collective-permute-done | bytes 49184 | tf_op jit(solution)/shard_map/ppermute | solution.py:21
  42.8 1.0 %collective-permute-done.15 = bf16[96,256]{1,0:T(8,128)(2,1)S(1)} collective-permute-done((bf16[96,256]{1,0:T(8,128)(2,1)S(1)}, bf16[96,256]{1,0:T(8,128)(2,1)S(1)}, u32[]{:S(2)}, u32[]{:S(2)}) %collective-permute-start.15) | collective-permute-done | bytes 49184 | tf_op jit(solution)/shard_map/ppermute | solution.py:21
  43.8 0.7 %convert_add_fusion = f32[96,256]{1,0:T(8,128)} fusion(f32[96,256]{1,0:T(8,128)S(1)} %outward.2, bf16[96,256]{1,0:T(8,128)(2,1)S(1)} %collective-permute-done.15), kind=kLoop, calls=%fused_computation | loop fusion | flops 49152 | bytes 245760 | tf_op jit(solution)/shard_map/add | solution.py:437
  (25 shorter events, 0.5 us)
Async XLA Ops:
  1.5 8.1 %collective-permute-start = (bf16[96,256]{1,0:T(8,128)(2,1)S(1)}, bf16[96,256]{1,0:T(8,128)(2,1)S(1)}, u32[]{:S(2)}, u32[]{:S(2)}) collective-permute-start(bf16[96,256]{1,0:T(8,128)(2,1)S(1)} %convert_element_type.6.after_ref.low_ref), channel_id=1, source_target_pairs={{0,8},{1,9},{2,10},{3,11},{4,12},{5,13},{6,14},{7,15},{8,0},{9,1},... | collective-permute-start | bytes 147464 | tf_op jit(solution)/shard_map/ppermute | solution.py:21
  5.6 0.8 %copy-start = (s32[8,8,32]{2,1,0:T(8,128)S(1)}, s32[8,8,32]{2,1,0:T(8,128)}, u32[]{:S(2)}) copy-start(s32[8,8,32]{2,1,0:T(8,128)} %mask_ref.3) | copy-start | bytes 24580
  9.6 7.3 %copy-start.1 = (s32[128]{0:T(128)S(1)}, s32[128]{0:T(128)}, u32[]{:S(2)}) copy-start(s32[128]{0:T(128)} %param.10) | copy-start | bytes 1540
  9.6 7.3 %copy-start.2 = (f32[128]{0:T(128)S(1)}, f32[128]{0:T(128)}, u32[]{:S(2)}) copy-start(f32[128]{0:T(128)} %param.11) | copy-start | bytes 1540
  9.6 7.3 %copy-start.3 = (f32[128]{0:T(128)S(1)}, f32[128]{0:T(128)}, u32[]{:S(2)}) copy-start(f32[128]{0:T(128)} %param.12) | copy-start | bytes 1540
  9.7 3.7 %collective-permute-start.1 = (bf16[16,256]{1,0:T(8,128)(2,1)S(1)}, bf16[16,256]{1,0:T(8,128)(2,1)S(1)}, u32[]{:S(2)}, u32[]{:S(2)}) collective-permute-start(bf16[16,256]{1,0:T(8,128)(2,1)S(1)} %tails.1.after_ref), channel_id=1, source_target_pairs={{0,16},{16,0},{1,17},{17,1},{2,18},{18,2},{3,19},{19,3},{4,20},{20... | collective-permute-start | bytes 24584 | tf_op jit(solution)/shard_map/ppermute | solution.py:26
  13.4 6.3 %collective-permute-start.5 = (bf16[208,256]{1,0:T(8,128)(2,1)S(1)}, bf16[208,256]{1,0:T(8,128)(2,1)S(1)}, u32[]{:S(2)}, u32[]{:S(2)}) collective-permute-start(bf16[208,256]{1,0:T(8,128)(2,1)S(1)} %window.1.after_ref.first_ref), channel_id=1, source_target_pairs={{0,6},{1,7},{2,4},{3,5},{4,2},{5,3},{6,0},{7,1},{8,14},{9,15},{10,... | collective-permute-start | bytes 319496 | tf_op jit(solution)/shard_map/ppermute | solution.py:21
  16.0 4.8 %collective-permute-start.4 = (bf16[208,256]{1,0:T(8,128)(2,1)S(1)}, bf16[208,256]{1,0:T(8,128)(2,1)S(1)}, u32[]{:S(2)}, u32[]{:S(2)}) collective-permute-start(bf16[208,256]{1,0:T(8,128)(2,1)S(1)} %window.1.after_ref.first_ref), channel_id=1, source_target_pairs={{0,4},{1,5},{2,6},{3,7},{4,0},{5,1},{6,2},{7,3},{8,12},{9,13},{10,... | collective-permute-start | bytes 319496 | tf_op jit(solution)/shard_map/ppermute | solution.py:21
  16.4 4.7 %collective-permute-start.3 = (bf16[208,256]{1,0:T(8,128)(2,1)S(1)}, bf16[208,256]{1,0:T(8,128)(2,1)S(1)}, u32[]{:S(2)}, u32[]{:S(2)}) collective-permute-start(bf16[208,256]{1,0:T(8,128)(2,1)S(1)} %window.1.after_ref.first_ref), channel_id=1, source_target_pairs={{0,2},{1,3},{2,0},{3,1},{4,6},{5,7},{6,4},{7,5},{8,10},{9,11},{10,... | collective-permute-start | bytes 319496 | tf_op jit(solution)/shard_map/ppermute | solution.py:21
  21.2 1.9 %collective-permute-start.6 = (bf16[624,256]{1,0:T(8,128)(2,1)S(1)}, bf16[624,256]{1,0:T(8,128)(2,1)S(1)}, u32[]{:S(2)}, u32[]{:S(2)}) collective-permute-start(bf16[624,256]{1,0:T(8,128)(2,1)S(1)} %pack.1.rest_ref), channel_id=1, source_target_pairs={{0,1},{1,0},{2,3},{3,2},{4,5},{5,4},{6,7},{7,6},{8,9},{9,8},{10,11... | collective-permute-start | bytes 958472 | tf_op jit(solution)/shard_map/ppermute | solution.py:21
  21.2 1.8 %collective-permute-start.2 = (bf16[208,256]{1,0:T(8,128)(2,1)S(1)}, bf16[208,256]{1,0:T(8,128)(2,1)S(1)}, u32[]{:S(2)}, u32[]{:S(2)}) collective-permute-start(bf16[208,256]{1,0:T(8,128)(2,1)S(1)} %window.1.after_ref.first_ref), channel_id=1, source_target_pairs={{0,1},{1,0},{2,3},{3,2},{4,5},{5,4},{6,7},{7,6},{8,9},{9,8},{10,11... | collective-permute-start | bytes 319496 | tf_op jit(solution)/shard_map/ppermute | solution.py:21
  25.6 1.9 %collective-permute-start.7 = (bf16[8,112,256]{2,1,0:T(8,128)(2,1)S(1)}, bf16[8,112,256]{2,1,0:T(8,128)(2,1)S(1)}, u32[]{:S(2)}, u32[]{:S(2)}) collective-permute-start(bf16[8,112,256]{2,1,0:T(8,128)(2,1)S(1)} %get-tuple-element.20), channel_id=1, source_target_pairs={{0,1},{1,0},{2,3},{3,2},{4,5},{5,4},{6,7},{7,6},{8,9},{9,8},{10,11... | collective-permute-start | bytes 1376264 | tf_op jit(solution)/shard_map/ppermute | solution.py:21
  27.5 4.0 %collective-permute-start.8 = (bf16[64,256]{1,0:T(8,128)(2,1)S(1)}, bf16[64,256]{1,0:T(8,128)(2,1)S(1)}, u32[]{:S(2)}, u32[]{:S(2)}) collective-permute-start(bf16[64,256]{1,0:T(8,128)(2,1)S(1)} %get-tuple-element.22.after_ref), channel_id=1, source_target_pairs={{0,16},{16,0},{1,17},{17,1},{2,18},{18,2},{3,19},{19,3},{4,20},{20... | collective-permute-start | bytes 98312 | tf_op jit(solution)/shard_map/ppermute | solution.py:26
  31.5 6.2 %collective-permute-start.13 = (bf16[96,256]{1,0:T(8,128)(2,1)S(1)}, bf16[96,256]{1,0:T(8,128)(2,1)S(1)}, u32[]{:S(2)}, u32[]{:S(2)}) collective-permute-start(bf16[96,256]{1,0:T(8,128)(2,1)S(1)} %get-tuple-element.29), channel_id=1, source_target_pairs={{0,4},{1,5},{2,6},{3,7},{4,0},{5,1},{6,2},{7,3},{8,12},{9,13},{10,... | collective-permute-start | bytes 147464 | tf_op jit(solution)/shard_map/ppermute | solution.py:21
  33.2 5.5 %collective-permute-start.14 = (bf16[96,256]{1,0:T(8,128)(2,1)S(1)}, bf16[96,256]{1,0:T(8,128)(2,1)S(1)}, u32[]{:S(2)}, u32[]{:S(2)}) collective-permute-start(bf16[96,256]{1,0:T(8,128)(2,1)S(1)} %get-tuple-element.30), channel_id=1, source_target_pairs={{0,6},{1,7},{2,4},{3,5},{4,2},{5,3},{6,0},{7,1},{8,14},{9,15},{10,... | collective-permute-start | bytes 147464 | tf_op jit(solution)/shard_map/ppermute | solution.py:21
  34.2 4.5 %collective-permute-start.12 = (bf16[96,256]{1,0:T(8,128)(2,1)S(1)}, bf16[96,256]{1,0:T(8,128)(2,1)S(1)}, u32[]{:S(2)}, u32[]{:S(2)}) collective-permute-start(bf16[96,256]{1,0:T(8,128)(2,1)S(1)} %get-tuple-element.23.after_ref), channel_id=1, source_target_pairs={{0,2},{1,3},{2,0},{3,1},{4,6},{5,7},{6,4},{7,5},{8,10},{9,11},{10,... | collective-permute-start | bytes 147464 | tf_op jit(solution)/shard_map/ppermute | solution.py:21
  35.1 5.7 %collective-permute-start.9 = (bf16[96,256]{1,0:T(8,128)(2,1)S(1)}, bf16[96,256]{1,0:T(8,128)(2,1)S(1)}, u32[]{:S(2)}, u32[]{:S(2)}) collective-permute-start(bf16[96,256]{1,0:T(8,128)(2,1)S(1)} %get-tuple-element.25), channel_id=1, source_target_pairs={{0,2},{1,3},{2,0},{3,1},{4,6},{5,7},{6,4},{7,5},{8,10},{9,11},{10,... | collective-permute-start | bytes 147464 | tf_op jit(solution)/shard_map/ppermute | solution.py:21
  36.3 4.5 %collective-permute-start.10 = (bf16[96,256]{1,0:T(8,128)(2,1)S(1)}, bf16[96,256]{1,0:T(8,128)(2,1)S(1)}, u32[]{:S(2)}, u32[]{:S(2)}) collective-permute-start(bf16[96,256]{1,0:T(8,128)(2,1)S(1)} %get-tuple-element.26), channel_id=1, source_target_pairs={{0,4},{1,5},{2,6},{3,7},{4,0},{5,1},{6,2},{7,3},{8,12},{9,13},{10,... | collective-permute-start | bytes 147464 | tf_op jit(solution)/shard_map/ppermute | solution.py:21
  37.8 5.0 %collective-permute-start.11 = (bf16[96,256]{1,0:T(8,128)(2,1)S(1)}, bf16[96,256]{1,0:T(8,128)(2,1)S(1)}, u32[]{:S(2)}, u32[]{:S(2)}) collective-permute-start(bf16[96,256]{1,0:T(8,128)(2,1)S(1)} %get-tuple-element.27), channel_id=1, source_target_pairs={{0,6},{1,7},{2,4},{3,5},{4,2},{5,3},{6,0},{7,1},{8,14},{9,15},{10,... | collective-permute-start | bytes 147464 | tf_op jit(solution)/shard_map/ppermute | solution.py:21
  38.7 5.1 %collective-permute-start.15 = (bf16[96,256]{1,0:T(8,128)(2,1)S(1)}, bf16[96,256]{1,0:T(8,128)(2,1)S(1)}, u32[]{:S(2)}, u32[]{:S(2)}) collective-permute-start(bf16[96,256]{1,0:T(8,128)(2,1)S(1)} %outward.3), channel_id=1, source_target_pairs={{0,8},{1,9},{2,10},{3,11},{4,12},{5,13},{6,14},{7,15},{8,0},{9,1},... | collective-permute-start | bytes 147464 | tf_op jit(solution)/shard_map/ppermute | solution.py:21

commit v4 on v3

--- a/solution.py
+++ b/solution.py
@@ -252,9 +252,10 @@
 
 def adjoint_kernel(
     lags, first_ref, rest_ref, top_ref, low_ref, begun_ref, select_ref, line_ref,
-    mism_ref, spread_ref, other_ref, score_ref, window_ref,
+    mism_ref, spread_ref, other_ref, rims_ref, score_ref, window_ref,
 ):
     width, depth = score_ref.shape
+    hours = other_ref.shape[1]
     score_ref[...] = begun_ref[...]
     add_scores(readers(first_ref, rest_ref), (top_ref, low_ref), 1, score_ref, window_ref)
     line = jnp.sum(score_ref[...] * select_ref[...], axis=0, keepdims=True)
@@ -265,8 +266,14 @@
     for i in range(0, width, PAIR):
         rows = [select_ref[i + j : i + j + 8] * weighted for j in (0, 8)]
         spread_ref[i : i + PAIR] = jnp.concatenate(rows, axis=0).astype(BF16)
-    for k in range(top_ref.shape[0] // 2):
-        other_ref[k] = terms(spread_ref, (top_ref, low_ref), 2 * k + 1).astype(BF16)
+    count = top_ref.shape[0] // 4
+    for i in range(count):
+        edges = []
+        for k in (i, i + count):
+            term = terms(spread_ref, (top_ref, low_ref), 2 * k + 1)
+            other_ref[k] = term[:hours].astype(BF16)
+            edges.append(term[hours : hours + RIM])
+        rims_ref[i * PAIR : (i + 1) * PAIR] = jnp.concatenate(edges, axis=0).astype(BF16)
 
 
 def adjoint(first, rest, masked, begun, select, lines, lags):
@@ -278,7 +285,8 @@
         [
             ((8, depth), F32),
             ((width, depth), BF16),
-            ((devices // 2, width, own), BF16),
+            ((devices // 2, width - PAIR, own), BF16),
+            ((devices // 4 * PAIR, own), BF16),
         ],
         [first, rest, *masked, begun, select, lines],
         "v" * 7,
@@ -289,9 +297,16 @@
     )
 
 
-def mine_kernel(spread_ref, top_ref, low_ref, own_ref):
-    for k in range(top_ref.shape[0] // 2):
-        own_ref[k] = terms(spread_ref, (top_ref, low_ref), 2 * k)
+def mine_kernel(spread_ref, top_ref, low_ref, own_ref, rims_ref):
+    count = top_ref.shape[0] // 4
+    hours = own_ref.shape[1]
+    for i in range(count):
+        edges = []
+        for k in (i, i + count):
+            term = terms(spread_ref, (top_ref, low_ref), 2 * k)
+            own_ref[k] = term[:hours]
+            edges.append(term[hours : hours + RIM])
+        rims_ref[i * PAIR : (i + 1) * PAIR] = jnp.concatenate(edges, axis=0)
 
 
 def mine_part(spread, masked):
@@ -300,13 +315,13 @@
     width = spread.shape[0]
     return call(
         mine_kernel,
-        [((devices // 2, width, own), F32)],
+        [((devices // 2, width - PAIR, own), F32), ((devices // 4 * PAIR, own), F32)],
         [spread, *masked],
         "vvv",
         flops=width * depth * own * devices,
         moved=depth * own * devices,
         name="mine",
-    )[0]
+    )
 
 
 def narrow_kernel(mism_ref, after_ref, out_ref):
@@ -329,26 +344,37 @@
     return call(narrow_kernel, outs, [mism, after], "va", flops=BUSY, name="narrow")[0]
 
 
-def join_kernel(own_ref, came_ref, main_ref, rims_ref):
-    half, width, _ = own_ref.shape
-    hours = width - PAIR
+def gate_kernel(rows_ref, after_ref, out_ref):
+    del after_ref
+    out_ref[...] = rows_ref[...]
+
+
+def gate(rows, after):
+    outs = [(rows.shape, rows.dtype)]
+    return call(gate_kernel, outs, [rows, after], "va", name="gate")[0]
+
+
+def join_rims_kernel(own_ref, came_ref, out_ref):
+    out_ref[...] = (own_ref[...] + came_ref[...].astype(F32)).astype(BF16)
+
+
+def join_rims(own, came):
+    return call(join_rims_kernel, [(own.shape, BF16)], [own, came], "vv", name="rims")[0]
+
+
+def join_kernel(own_ref, came_ref, after_ref, main_ref):
+    del after_ref
+    half, hours, _ = own_ref.shape
     for i in range(half // 2):
-        edges = []
         for j in range(2):
             k = i + j * (half // 2)
-            total = own_ref[k] + came_ref[k].astype(F32)
-            main_ref[i, j * hours : (j + 1) * hours] = total[:hours]
-            edges.append(total[hours : hours + RIM])
-        rims_ref[i * PAIR : (i + 1) * PAIR] = jnp.concatenate(edges, axis=0).astype(BF16)
-
-
-def join(own, came):
-    half, width, columns = own.shape
-    outs = [
-        ((half // 2, 2 * (width - PAIR), columns), F32),
-        ((half // 2 * PAIR, columns), BF16),
-    ]
-    return call(join_kernel, outs, [own, came], "vv", name="join")
+            main_ref[i, j * hours : (j + 1) * hours] = own_ref[k] + came_ref[k].astype(F32)
+
+
+def join(own, came, after):
+    half, hours, columns = own.shape
+    outs = [((half // 2, 2 * hours, columns), F32)]
+    return call(join_kernel, outs, [own, came, after], "vva", flops=BUSY, name="join")[0]
 
 
 def with_rims(main_ref, rims_ref, i, j):
@@ -421,12 +447,16 @@
     rest = pack(parts, lines)
     masked = (top, bottom)
     begun = score(first, rest, masked)
-    mism, spread, other = adjoint(
+    mism, spread, other, other_rims = adjoint(
         other_first, swap(rest, 1), masked, begun, select, lines, lags
     )
 
-    main, rims = join(mine_part(spread, masked), swap(other, 1))
+    came_rims = swap(other_rims, 1)
+    own_part, own_rims = mine_part(spread, masked)
+    rims = join_rims(own_rims, came_rims)
+    came = swap(gate(other, rims), 1)
     back = turn(rims, -1)
+    main = join(own_part, came, rims)
     far_sum, parts = shares(main, back, 1, rims)
     passed = [swap(part, k) for part, k in zip(parts, near)]
     near_sum, others = shares(main, back, 0, parts[0])

time: 44.7 us -> 44.3 us (level)
  waiting for transfers between devices: 10.2 us -> 9.55 us
    ppermute x14 -> x15, waiting for transfers between devices: 7.56 us -> 7.06 us  [swap(): return lax.ppermute(block, 'rcpt', [(i, i ^ bit) for i in devices])]
    ppermute x14 -> x15, starting transfers between devices: 16.4 us -> 16.6 us  [swap(): return lax.ppermute(block, 'rcpt', [(i, i ^ bit) for i in devices])]
    pallas_call x15 -> x17, Pallas kernels: 11 us -> 11 us  [call(): pl.pallas_call(kernel, in_specs=[pl.BlockSpec(memory_space=where[c]) for...]
  transfers between devices with their start and end apart: 16 -> 17, of which waited for: 8 -> 10; matrix products, arithmetic and copies ran while one was open for 0% -> 0% of each run, Pallas kernels for 19% -> 19%
where the time goes in v4:
time: 44.3 us; the launch traced here: 44 us
  starting transfers between devices  19.7 us (44%)
  Pallas kernels  11 us (25%)
  waiting for transfers between devices  9.55 us (22%)
  other arithmetic  1.55 us (3%)
  between operations  1.44 us (3%)
  local copies, waits for them, and re-layouts  0.78 us (2%)
    ppermute x15, starting transfers between devices, swap(): return lax.ppermute(block, 'rcpt', [(i, i ^ bit) for i in devices])  16.6 us
    pallas_call x17, Pallas kernels, call(): pl.pallas_call(kernel, in_specs=[pl.BlockSpec(memory_space=where[c]) for...  11 us
    ppermute x15, waiting for transfers between devices, swap(): return lax.ppermute(block, 'rcpt', [(i, i ^ bit) for i in devices])  7.06 us
    ppermute x2, starting transfers between devices, turn(): lax.ppermute(block, 'hour', [(i, (i + distance) % size) for i in range(si...  3.05 us
    ppermute x2, waiting for transfers between devices, turn(): lax.ppermute(block, 'hour', [(i, (i + distance) % size) for i in range(si...  2.48 us
    convert_element_type x1, other arithmetic, per_device(): low = flux.astype(BF16)  0.9 us
  transfers between devices with their start and end apart: 17, of which 10 were waited for; matrix products, arithmetic and copies ran while one was open for 0% of the time, Pallas kernels for 19%

profile of v4, /device:TPU:0, one launch (start us, length us, event | category | flops | bytes accessed | tf_op | source)
XLA Modules:
  0.0 44.0 jit_solution(13487580339175100947)
XLA Ops:
  0.6 0.9 %convert_element_type.6.after_ref.low_ref = bf16[96,256]{1,0:T(8,128)(2,1)S(1)} convert(f32[96,256]{1,0:T(8,128)} %param.7) | non-fusion elementwise | flops 24576 | bytes 147456 | tf_op jit(solution)/shard_map/convert_element_type | solution.py:427
  1.5 4.0 %collective-permute-start = (bf16[96,256]{1,0:T(8,128)(2,1)S(1)}, bf16[96,256]{1,0:T(8,128)(2,1)S(1)}, u32[]{:S(2)}, u32[]{:S(2)}) collective-permute-start(bf16[96,256]{1,0:T(8,128)(2,1)S(1)} %convert_element_type.6.after_ref.low_ref), channel_id=1, source_target_pairs={{0,8},{1,9},{2,10},{3,11},{4,12},{5,13},{6,14},{7,15},{8,0},{9,1},... | collective-permute-start | bytes 147464 | tf_op jit(solution)/shard_map/ppermute | solution.py:21
  5.6 0.8 %copy-done = s32[8,8,32]{2,1,0:T(8,128)S(1)} copy-done((s32[8,8,32]{2,1,0:T(8,128)S(1)}, s32[8,8,32]{2,1,0:T(8,128)}, u32[]{:S(2)}) %copy-start) | copy-done | bytes 8216
  6.3 2.6 %prepare.2.after_ref.top_ref = bf16[16,640,256]{2,1,0:T(8,128)(2,1)S(1)} custom-call(bf16[1024,4096]{1,0:T(8,128)(2,1)} %bitcast.8, s32[8,8,32]{2,1,0:T(8,128)S(1)} %copy-done, bf16[96,256]{1,0:T(8,128)(2,1)S(1)} %convert_element_type.6.after_ref.low_ref), custom_call_target="tpu_custom_call" | custom-call | flops 10000000000 | bytes 10485760 | tf_op jit(solution)/shard_map/prepare/pallas_call | solution.py:40
  9.7 1.6 %collective-permute-start.1 = (bf16[16,256]{1,0:T(8,128)(2,1)S(1)}, bf16[16,256]{1,0:T(8,128)(2,1)S(1)}, u32[]{:S(2)}, u32[]{:S(2)}) collective-permute-start(bf16[16,256]{1,0:T(8,128)(2,1)S(1)} %tails.1.after_ref), channel_id=1, source_target_pairs={{0,16},{16,0},{1,17},{17,1},{2,18},{18,2},{3,19},{19,3},{4,20},{20... | collective-permute-start | bytes 24584 | tf_op jit(solution)/shard_map/ppermute | solution.py:26
  11.2 2.0 %prepare.3.after_ref.low_ref = bf16[16,384,256]{2,1,0:T(8,128)(2,1)S(1)} custom-call(bf16[1024,4096]{1,0:T(8,128)(2,1)} %bitcast.9, s32[8,8,32]{2,1,0:T(8,128)S(1)} %copy-done, bf16[16,256]{1,0:T(8,128)(2,1)S(1)} %tails.1.after_ref), custom_call_target="tpu_custom_call" | custom-call | flops 10000000000 | bytes 6291456 | tf_op jit(solution)/shard_map/prepare/pallas_call | solution.py:40
  13.4 2.6 %collective-permute-start.5 = (bf16[208,256]{1,0:T(8,128)(2,1)S(1)}, bf16[208,256]{1,0:T(8,128)(2,1)S(1)}, u32[]{:S(2)}, u32[]{:S(2)}) collective-permute-start(bf16[208,256]{1,0:T(8,128)(2,1)S(1)} %window.1.after_ref.first_ref), channel_id=1, source_target_pairs={{0,6},{1,7},{2,4},{3,5},{4,2},{5,3},{6,0},{7,1},{8,14},{9,15},{10,... | collective-permute-start | bytes 319496 | tf_op jit(solution)/shard_map/ppermute | solution.py:21
  16.0 0.4 %collective-permute-start.4 = (bf16[208,256]{1,0:T(8,128)(2,1)S(1)}, bf16[208,256]{1,0:T(8,128)(2,1)S(1)}, u32[]{:S(2)}, u32[]{:S(2)}) collective-permute-start(bf16[208,256]{1,0:T(8,128)(2,1)S(1)} %window.1.after_ref.first_ref), channel_id=1, source_target_pairs={{0,4},{1,5},{2,6},{3,7},{4,0},{5,1},{6,2},{7,3},{8,12},{9,13},{10,... | collective-permute-start | bytes 319496 | tf_op jit(solution)/shard_map/ppermute | solution.py:21
  16.4 0.5 %collective-permute-start.3 = (bf16[208,256]{1,0:T(8,128)(2,1)S(1)}, bf16[208,256]{1,0:T(8,128)(2,1)S(1)}, u32[]{:S(2)}, u32[]{:S(2)}) collective-permute-start(bf16[208,256]{1,0:T(8,128)(2,1)S(1)} %window.1.after_ref.first_ref), channel_id=1, source_target_pairs={{0,2},{1,3},{2,0},{3,1},{4,6},{5,7},{6,4},{7,5},{8,10},{9,11},{10,... | collective-permute-start | bytes 319496 | tf_op jit(solution)/shard_map/ppermute | solution.py:21
  17.0 0.5 %choose.1 = (f32[112,1024]{1,0:T(8,128)S(1)}, f32[16,1024]{1,0:T(8,128)S(1)}) custom-call(s32[1,128]{1,0:T(1,128)S(1)} %bitcast.5, f32[1,128]{1,0:T(1,128)S(1)} %bitcast.6, f32[1,128]{1,0:T(1,128)S(1)} %bitcast.7, s32[1]{0:T(128)S(6)} %copy.9.count_ref, bf16[208,256]{1,0:T(8,128)(2,1)S(1)} %window.1.after_ref.first_ref), custom_call_target="tpu_custom_call" | custom-call | flops 10000000000 | tf_op jit(solution)/shard_map/choose/pallas_call | solution.py:40
  17.5 2.2 %collective-permute-done.5.refs_2_ = bf16[208,256]{1,0:T(8,128)(2,1)S(1)} collective-permute-done((bf16[208,256]{1,0:T(8,128)(2,1)S(1)}, bf16[208,256]{1,0:T(8,128)(2,1)S(1)}, u32[]{:S(2)}, u32[]{:S(2)}) %collective-permute-start.5) | collective-permute-done | bytes 106528 | tf_op jit(solution)/shard_map/ppermute | solution.py:21
  19.7 1.1 %collective-permute-done.4.refs_1_ = bf16[208,256]{1,0:T(8,128)(2,1)S(1)} collective-permute-done((bf16[208,256]{1,0:T(8,128)(2,1)S(1)}, bf16[208,256]{1,0:T(8,128)(2,1)S(1)}, u32[]{:S(2)}, u32[]{:S(2)}) %collective-permute-start.4) | collective-permute-done | bytes 106528 | tf_op jit(solution)/shard_map/ppermute | solution.py:21
  20.8 0.3 collective-permute-done.3.refs_0_
  21.2 0.5 %collective-permute-start.2 = (bf16[208,256]{1,0:T(8,128)(2,1)S(1)}, bf16[208,256]{1,0:T(8,128)(2,1)S(1)}, u32[]{:S(2)}, u32[]{:S(2)}) collective-permute-start(bf16[208,256]{1,0:T(8,128)(2,1)S(1)} %window.1.after_ref.first_ref), channel_id=1, source_target_pairs={{0,1},{1,0},{2,3},{3,2},{4,5},{5,4},{6,7},{7,6},{8,9},{9,8},{10,11... | collective-permute-start | bytes 319496 | tf_op jit(solution)/shard_map/ppermute | solution.py:21
  21.7 1.3 %score.1.begun_ref = f32[112,1024]{1,0:T(8,128)S(1)} custom-call(bf16[208,256]{1,0:T(8,128)(2,1)S(1)} %window.1.after_ref.first_ref, bf16[624,256]{1,0:T(8,128)(2,1)S(1)} %pack.1.rest_ref, bf16[16,640,256]{2,1,0:T(8,128)(2,1)S(1)} %prepare.2.after_ref.top_ref, bf16[16,384,256]{2,1,0:T(8,128)(2,1)S(1)} %prepare.3.after_ref.low_ref), custom_call_target="tpu_custom_call" | custom-call | flops 469762048 | bytes 4194304 | tf_op jit(solution)/shard_map/score/pallas_call | solution.py:40
  23.1 2.5 %adjoint.1 = (f32[8,1024]{1,0:T(8,128)S(1)}, bf16[112,1024]{1,0:T(8,128)(2,1)S(1)}, bf16[8,96,256]{2,1,0:T(8,128)(2,1)S(1)}, bf16[64,256]{1,0:T(8,128)(2,1)S(1)}) custom-call(bf16[208,256]{1,0:T(8,128)(2,1)S(1)} %collective-permute-done.2.first_ref, bf16[624,256]{1,0:T(8,128)(2,1)S(1)} %collective-permute-done.6.rest_ref, ...), custom_call_target="tpu_custom_call" | custom-call | flops 939524096 | bytes 4194304 | tf_op jit(solution)/shard_map/adjoint/pallas_call | solution.py:40
  25.7 0.8 %mine.1 = (f32[8,96,256]{2,1,0:T(8,128)S(1)}, f32[64,256]{1,0:T(8,128)S(1)}) custom-call(bf16[112,1024]{1,0:T(8,128)(2,1)S(1)} %get-tuple-element.20.spread_ref, bf16[16,640,256]{2,1,0:T(8,128)(2,1)S(1)} %prepare.2.after_ref.top_ref, bf16[16,384,256]{2,1,0:T(8,128)(2,1)S(1)} %prepare.3.after_ref.low_ref), custom_call_target="tpu_custom_call" | custom-call | flops 469762048 | bytes 4194304 | tf_op jit(solution)/shard_map/mine/pallas_call | solution.py:40
  26.6 0.3 collective-permute-done.7.came_ref
  26.9 0.2 collective-permute-start.8
  27.1 1.5 %collective-permute-start.9 = (bf16[64,256]{1,0:T(8,128)(2,1)S(1)}, bf16[64,256]{1,0:T(8,128)(2,1)S(1)}, u32[]{:S(2)}, u32[]{:S(2)}) collective-permute-start(bf16[64,256]{1,0:T(8,128)(2,1)S(1)} %rims.1.after_ref), channel_id=1, source_target_pairs={{0,16},{16,0},{1,17},{17,1},{2,18},{18,2},{3,19},{19,3},{4,20},{20... | collective-permute-start | bytes 98312 | tf_op jit(solution)/shard_map/ppermute | solution.py:26
  28.8 2.3 %collective-permute-done.9.rims_ref = bf16[64,256]{1,0:T(8,128)(2,1)S(1)} collective-permute-done((bf16[64,256]{1,0:T(8,128)(2,1)S(1)}, bf16[64,256]{1,0:T(8,128)(2,1)S(1)}, u32[]{:S(2)}, u32[]{:S(2)}) %collective-permute-start.9) | collective-permute-done | bytes 32800 | tf_op jit(solution)/shard_map/ppermute | solution.py:26
  31.1 1.6 %collective-permute-start.14 = (bf16[96,256]{1,0:T(8,128)(2,1)S(1)}, bf16[96,256]{1,0:T(8,128)(2,1)S(1)}, u32[]{:S(2)}, u32[]{:S(2)}) collective-permute-start(bf16[96,256]{1,0:T(8,128)(2,1)S(1)} %get-tuple-element.31), channel_id=1, source_target_pairs={{0,4},{1,5},{2,6},{3,7},{4,0},{5,1},{6,2},{7,3},{8,12},{9,13},{10,... | collective-permute-start | bytes 147464 | tf_op jit(solution)/shard_map/ppermute | solution.py:21
  32.7 1.0 %collective-permute-start.15 = (bf16[96,256]{1,0:T(8,128)(2,1)S(1)}, bf16[96,256]{1,0:T(8,128)(2,1)S(1)}, u32[]{:S(2)}, u32[]{:S(2)}) collective-permute-start(bf16[96,256]{1,0:T(8,128)(2,1)S(1)} %get-tuple-element.32), channel_id=1, source_target_pairs={{0,6},{1,7},{2,4},{3,5},{4,2},{5,3},{6,0},{7,1},{8,14},{9,15},{10,... | collective-permute-start | bytes 147464 | tf_op jit(solution)/shard_map/ppermute | solution.py:21
  33.7 0.9 %collective-permute-start.13 = (bf16[96,256]{1,0:T(8,128)(2,1)S(1)}, bf16[96,256]{1,0:T(8,128)(2,1)S(1)}, u32[]{:S(2)}, u32[]{:S(2)}) collective-permute-start(bf16[96,256]{1,0:T(8,128)(2,1)S(1)} %get-tuple-element.25.after_ref), channel_id=1, source_target_pairs={{0,2},{1,3},{2,0},{3,1},{4,6},{5,7},{6,4},{7,5},{8,10},{9,11},{10,... | collective-permute-start | bytes 147464 | tf_op jit(solution)/shard_map/ppermute | solution.py:21
  34.7 1.1 %collective-permute-start.10 = (bf16[96,256]{1,0:T(8,128)(2,1)S(1)}, bf16[96,256]{1,0:T(8,128)(2,1)S(1)}, u32[]{:S(2)}, u32[]{:S(2)}) collective-permute-start(bf16[96,256]{1,0:T(8,128)(2,1)S(1)} %get-tuple-element.27), channel_id=1, source_target_pairs={{0,2},{1,3},{2,0},{3,1},{4,6},{5,7},{6,4},{7,5},{8,10},{9,11},{10,... | collective-permute-start | bytes 147464 | tf_op jit(solution)/shard_map/ppermute | solution.py:21
  35.8 1.5 %collective-permute-start.11 = (bf16[96,256]{1,0:T(8,128)(2,1)S(1)}, bf16[96,256]{1,0:T(8,128)(2,1)S(1)}, u32[]{:S(2)}, u32[]{:S(2)}) collective-permute-start(bf16[96,256]{1,0:T(8,128)(2,1)S(1)} %get-tuple-element.28), channel_id=1, source_target_pairs={{0,4},{1,5},{2,6},{3,7},{4,0},{5,1},{6,2},{7,3},{8,12},{9,13},{10,... | collective-permute-start | bytes 147464 | tf_op jit(solution)/shard_map/ppermute | solution.py:21
  37.3 0.9 %collective-permute-start.12 = (bf16[96,256]{1,0:T(8,128)(2,1)S(1)}, bf16[96,256]{1,0:T(8,128)(2,1)S(1)}, u32[]{:S(2)}, u32[]{:S(2)}) collective-permute-start(bf16[96,256]{1,0:T(8,128)(2,1)S(1)} %get-tuple-element.29), channel_id=1, source_target_pairs={{0,6},{1,7},{2,4},{3,5},{4,2},{5,3},{6,0},{7,1},{8,14},{9,15},{10,... | collective-permute-start | bytes 147464 | tf_op jit(solution)/shard_map/ppermute | solution.py:21
  38.3 1.0 %collective-permute-start.16 = (bf16[96,256]{1,0:T(8,128)(2,1)S(1)}, bf16[96,256]{1,0:T(8,128)(2,1)S(1)}, u32[]{:S(2)}, u32[]{:S(2)}) collective-permute-start(bf16[96,256]{1,0:T(8,128)(2,1)S(1)} %outward.3), channel_id=1, source_target_pairs={{0,8},{1,9},{2,10},{3,11},{4,12},{5,13},{6,14},{7,15},{8,0},{9,1},... | collective-permute-start | bytes 147464 | tf_op jit(solution)/shard_map/ppermute | solution.py:21
  39.3 1.0 %narrow.1 = f32[1,128]{1,0:T(1,128)} custom-call(f32[8,1024]{1,0:T(8,128)S(1)} %get-tuple-element.33.mism_ref, f32[96,256]{1,0:T(8,128)S(1)} %get-tuple-element.30.first_ref.after_ref), custom_call_target="tpu_custom_call" | custom-call | flops 10000000000 | tf_op jit(solution)/shard_map/narrow/pallas_call | solution.py:40
  40.4 1.9 %collective-permute-done.12.refs_2_ = bf16[96,256]{1,0:T(8,128)(2,1)S(1)} collective-permute-done((bf16[96,256]{1,0:T(8,128)(2,1)S(1)}, bf16[96,256]{1,0:T(8,128)(2,1)S(1)}, u32[]{:S(2)}, u32[]{:S(2)}) %collective-permute-start.12) | collective-permute-done | bytes 49184 | tf_op jit(solution)/shard_map/ppermute | solution.py:21
  42.3 1.0 %collective-permute-done.16 = bf16[96,256]{1,0:T(8,128)(2,1)S(1)} collective-permute-done((bf16[96,256]{1,0:T(8,128)(2,1)S(1)}, bf16[96,256]{1,0:T(8,128)(2,1)S(1)}, u32[]{:S(2)}, u32[]{:S(2)}) %collective-permute-start.16) | collective-permute-done | bytes 49184 | tf_op jit(solution)/shard_map/ppermute | solution.py:21
  43.4 0.7 %convert_add_fusion = f32[96,256]{1,0:T(8,128)} fusion(f32[96,256]{1,0:T(8,128)S(1)} %outward.2, bf16[96,256]{1,0:T(8,128)(2,1)S(1)} %collective-permute-done.16), kind=kLoop, calls=%fused_computation | loop fusion | flops 49152 | bytes 245760 | tf_op jit(solution)/shard_map/add | solution.py:467
  (29 shorter events, 0.9 us)
Async XLA Ops:
  1.5 8.1 %collective-permute-start = (bf16[96,256]{1,0:T(8,128)(2,1)S(1)}, bf16[96,256]{1,0:T(8,128)(2,1)S(1)}, u32[]{:S(2)}, u32[]{:S(2)}) collective-permute-start(bf16[96,256]{1,0:T(8,128)(2,1)S(1)} %convert_element_type.6.after_ref.low_ref), channel_id=1, source_target_pairs={{0,8},{1,9},{2,10},{3,11},{4,12},{5,13},{6,14},{7,15},{8,0},{9,1},... | collective-permute-start | bytes 147464 | tf_op jit(solution)/shard_map/ppermute | solution.py:21
  5.6 0.8 %copy-start = (s32[8,8,32]{2,1,0:T(8,128)S(1)}, s32[8,8,32]{2,1,0:T(8,128)}, u32[]{:S(2)}) copy-start(s32[8,8,32]{2,1,0:T(8,128)} %mask_ref.3) | copy-start | bytes 24580
  9.6 7.3 %copy-start.1 = (s32[128]{0:T(128)S(1)}, s32[128]{0:T(128)}, u32[]{:S(2)}) copy-start(s32[128]{0:T(128)} %param.10) | copy-start | bytes 1540
  9.6 7.3 %copy-start.2 = (f32[128]{0:T(128)S(1)}, f32[128]{0:T(128)}, u32[]{:S(2)}) copy-start(f32[128]{0:T(128)} %param.11) | copy-start | bytes 1540
  9.6 7.3 %copy-start.3 = (f32[128]{0:T(128)S(1)}, f32[128]{0:T(128)}, u32[]{:S(2)}) copy-start(f32[128]{0:T(128)} %param.12) | copy-start | bytes 1540
  9.7 3.7 %collective-permute-start.1 = (bf16[16,256]{1,0:T(8,128)(2,1)S(1)}, bf16[16,256]{1,0:T(8,128)(2,1)S(1)}, u32[]{:S(2)}, u32[]{:S(2)}) collective-permute-start(bf16[16,256]{1,0:T(8,128)(2,1)S(1)} %tails.1.after_ref), channel_id=1, source_target_pairs={{0,16},{16,0},{1,17},{17,1},{2,18},{18,2},{3,19},{19,3},{4,20},{20... | collective-permute-start | bytes 24584 | tf_op jit(solution)/shard_map/ppermute | solution.py:26
  13.4 6.3 %collective-permute-start.5 = (bf16[208,256]{1,0:T(8,128)(2,1)S(1)}, bf16[208,256]{1,0:T(8,128)(2,1)S(1)}, u32[]{:S(2)}, u32[]{:S(2)}) collective-permute-start(bf16[208,256]{1,0:T(8,128)(2,1)S(1)} %window.1.after_ref.first_ref), channel_id=1, source_target_pairs={{0,6},{1,7},{2,4},{3,5},{4,2},{5,3},{6,0},{7,1},{8,14},{9,15},{10,... | collective-permute-start | bytes 319496 | tf_op jit(solution)/shard_map/ppermute | solution.py:21
  16.0 4.8 %collective-permute-start.4 = (bf16[208,256]{1,0:T(8,128)(2,1)S(1)}, bf16[208,256]{1,0:T(8,128)(2,1)S(1)}, u32[]{:S(2)}, u32[]{:S(2)}) collective-permute-start(bf16[208,256]{1,0:T(8,128)(2,1)S(1)} %window.1.after_ref.first_ref), channel_id=1, source_target_pairs={{0,4},{1,5},{2,6},{3,7},{4,0},{5,1},{6,2},{7,3},{8,12},{9,13},{10,... | collective-permute-start | bytes 319496 | tf_op jit(solution)/shard_map/ppermute | solution.py:21
  16.4 4.7 %collective-permute-start.3 = (bf16[208,256]{1,0:T(8,128)(2,1)S(1)}, bf16[208,256]{1,0:T(8,128)(2,1)S(1)}, u32[]{:S(2)}, u32[]{:S(2)}) collective-permute-start(bf16[208,256]{1,0:T(8,128)(2,1)S(1)} %window.1.after_ref.first_ref), channel_id=1, source_target_pairs={{0,2},{1,3},{2,0},{3,1},{4,6},{5,7},{6,4},{7,5},{8,10},{9,11},{10,... | collective-permute-start | bytes 319496 | tf_op jit(solution)/shard_map/ppermute | solution.py:21
  21.2 1.9 %collective-permute-start.6 = (bf16[624,256]{1,0:T(8,128)(2,1)S(1)}, bf16[624,256]{1,0:T(8,128)(2,1)S(1)}, u32[]{:S(2)}, u32[]{:S(2)}) collective-permute-start(bf16[624,256]{1,0:T(8,128)(2,1)S(1)} %pack.1.rest_ref), channel_id=1, source_target_pairs={{0,1},{1,0},{2,3},{3,2},{4,5},{5,4},{6,7},{7,6},{8,9},{9,8},{10,11... | collective-permute-start | bytes 958472 | tf_op jit(solution)/shard_map/ppermute | solution.py:21
  21.2 1.8 %collective-permute-start.2 = (bf16[208,256]{1,0:T(8,128)(2,1)S(1)}, bf16[208,256]{1,0:T(8,128)(2,1)S(1)}, u32[]{:S(2)}, u32[]{:S(2)}) collective-permute-start(bf16[208,256]{1,0:T(8,128)(2,1)S(1)} %window.1.after_ref.first_ref), channel_id=1, source_target_pairs={{0,1},{1,0},{2,3},{3,2},{4,5},{5,4},{6,7},{7,6},{8,9},{9,8},{10,11... | collective-permute-start | bytes 319496 | tf_op jit(solution)/shard_map/ppermute | solution.py:21
  25.6 1.3 %collective-permute-start.7 = (bf16[64,256]{1,0:T(8,128)(2,1)S(1)}, bf16[64,256]{1,0:T(8,128)(2,1)S(1)}, u32[]{:S(2)}, u32[]{:S(2)}) collective-permute-start(bf16[64,256]{1,0:T(8,128)(2,1)S(1)} %get-tuple-element.24), channel_id=1, source_target_pairs={{0,1},{1,0},{2,3},{3,2},{4,5},{5,4},{6,7},{7,6},{8,9},{9,8},{10,11... | collective-permute-start | bytes 98312 | tf_op jit(solution)/shard_map/ppermute | solution.py:21
  26.9 1.8 %collective-permute-start.8 = (bf16[8,96,256]{2,1,0:T(8,128)(2,1)S(1)}, bf16[8,96,256]{2,1,0:T(8,128)(2,1)S(1)}, u32[]{:S(2)}, u32[]{:S(2)}) collective-permute-start(bf16[8,96,256]{2,1,0:T(8,128)(2,1)S(1)} %gate.1), channel_id=1, source_target_pairs={{0,1},{1,0},{2,3},{3,2},{4,5},{5,4},{6,7},{7,6},{8,9},{9,8},{10,11... | collective-permute-start | bytes 1179656 | tf_op jit(solution)/shard_map/ppermute | solution.py:21
  27.1 3.9 %collective-permute-start.9 = (bf16[64,256]{1,0:T(8,128)(2,1)S(1)}, bf16[64,256]{1,0:T(8,128)(2,1)S(1)}, u32[]{:S(2)}, u32[]{:S(2)}) collective-permute-start(bf16[64,256]{1,0:T(8,128)(2,1)S(1)} %rims.1.after_ref), channel_id=1, source_target_pairs={{0,16},{16,0},{1,17},{17,1},{2,18},{18,2},{3,19},{19,3},{4,20},{20... | collective-permute-start | bytes 98312 | tf_op jit(solution)/shard_map/ppermute | solution.py:26
  31.1 6.2 %collective-permute-start.14 = (bf16[96,256]{1,0:T(8,128)(2,1)S(1)}, bf16[96,256]{1,0:T(8,128)(2,1)S(1)}, u32[]{:S(2)}, u32[]{:S(2)}) collective-permute-start(bf16[96,256]{1,0:T(8,128)(2,1)S(1)} %get-tuple-element.31), channel_id=1, source_target_pairs={{0,4},{1,5},{2,6},{3,7},{4,0},{5,1},{6,2},{7,3},{8,12},{9,13},{10,... | collective-permute-start | bytes 147464 | tf_op jit(solution)/shard_map/ppermute | solution.py:21
  32.7 5.5 %collective-permute-start.15 = (bf16[96,256]{1,0:T(8,128)(2,1)S(1)}, bf16[96,256]{1,0:T(8,128)(2,1)S(1)}, u32[]{:S(2)}, u32[]{:S(2)}) collective-permute-start(bf16[96,256]{1,0:T(8,128)(2,1)S(1)} %get-tuple-element.32), channel_id=1, source_target_pairs={{0,6},{1,7},{2,4},{3,5},{4,2},{5,3},{6,0},{7,1},{8,14},{9,15},{10,... | collective-permute-start | bytes 147464 | tf_op jit(solution)/shard_map/ppermute | solution.py:21
  33.7 4.6 %collective-permute-start.13 = (bf16[96,256]{1,0:T(8,128)(2,1)S(1)}, bf16[96,256]{1,0:T(8,128)(2,1)S(1)}, u32[]{:S(2)}, u32[]{:S(2)}) collective-permute-start(bf16[96,256]{1,0:T(8,128)(2,1)S(1)} %get-tuple-element.25.after_ref), channel_id=1, source_target_pairs={{0,2},{1,3},{2,0},{3,1},{4,6},{5,7},{6,4},{7,5},{8,10},{9,11},{10,... | collective-permute-start | bytes 147464 | tf_op jit(solution)/shard_map/ppermute | solution.py:21
  34.7 5.7 %collective-permute-start.10 = (bf16[96,256]{1,0:T(8,128)(2,1)S(1)}, bf16[96,256]{1,0:T(8,128)(2,1)S(1)}, u32[]{:S(2)}, u32[]{:S(2)}) collective-permute-start(bf16[96,256]{1,0:T(8,128)(2,1)S(1)} %get-tuple-element.27), channel_id=1, source_target_pairs={{0,2},{1,3},{2,0},{3,1},{4,6},{5,7},{6,4},{7,5},{8,10},{9,11},{10,... | collective-permute-start | bytes 147464 | tf_op jit(solution)/shard_map/ppermute | solution.py:21
  35.8 4.6 %collective-permute-start.11 = (bf16[96,256]{1,0:T(8,128)(2,1)S(1)}, bf16[96,256]{1,0:T(8,128)(2,1)S(1)}, u32[]{:S(2)}, u32[]{:S(2)}) collective-permute-start(bf16[96,256]{1,0:T(8,128)(2,1)S(1)} %get-tuple-element.28), channel_id=1, source_target_pairs={{0,4},{1,5},{2,6},{3,7},{4,0},{5,1},{6,2},{7,3},{8,12},{9,13},{10,... | collective-permute-start | bytes 147464 | tf_op jit(solution)/shard_map/ppermute | solution.py:21
  37.3 5.0 %collective-permute-start.12 = (bf16[96,256]{1,0:T(8,128)(2,1)S(1)}, bf16[96,256]{1,0:T(8,128)(2,1)S(1)}, u32[]{:S(2)}, u32[]{:S(2)}) collective-permute-start(bf16[96,256]{1,0:T(8,128)(2,1)S(1)} %get-tuple-element.29), channel_id=1, source_target_pairs={{0,6},{1,7},{2,4},{3,5},{4,2},{5,3},{6,0},{7,1},{8,14},{9,15},{10,... | collective-permute-start | bytes 147464 | tf_op jit(solution)/shard_map/ppermute | solution.py:21
  38.3 5.1 %collective-permute-start.16 = (bf16[96,256]{1,0:T(8,128)(2,1)S(1)}, bf16[96,256]{1,0:T(8,128)(2,1)S(1)}, u32[]{:S(2)}, u32[]{:S(2)}) collective-permute-start(bf16[96,256]{1,0:T(8,128)(2,1)S(1)} %outward.3), channel_id=1, source_target_pairs={{0,8},{1,9},{2,10},{3,11},{4,12},{5,13},{6,14},{7,15},{8,0},{9,1},... | collective-permute-start | bytes 147464 | tf_op jit(solution)/shard_map/ppermute | solution.py:21

commit v5 on v4

--- a/solution.py
+++ b/solution.py
@@ -154,18 +154,19 @@
     return call(window_kernel, outs, [low, far_low, rims, after], "vvva", name="window")[0]
 
 
-def pack_kernel(*refs):
-    *parts, _, out_ref = refs
+def pack_kernel(count, *refs):
+    parts, out_ref = refs[:count], refs[-1]
     height = parts[0].shape[0]
     for i, part in enumerate(parts):
         out_ref[i * height : (i + 1) * height] = part[...]
 
 
-def pack(parts, after):
+def pack(parts, *after):
     height, columns = parts[0].shape
     outs = [((len(parts) * height, columns), BF16)]
-    operands = [*parts, after]
-    return call(pack_kernel, outs, operands, "v" * len(operands), name="pack")[0]
+    spaces = "v" * len(parts) + "a" * len(after)
+    kernel = functools.partial(pack_kernel, len(parts))
+    return call(kernel, outs, [*parts, *after], spaces, name="pack")[0]
 
 
 def row_spans(masked_refs):
@@ -428,13 +429,13 @@
     far_low = swap(low, far)
     foot = footprint.reshape(rows * lags, cells)
     blocks = tile_mask.shape[0]
-    head = blocks * 5 // 8
+    head = blocks * 3 // 8
     top = prepare(foot, tile_mask, low, devices, 0, head)
     ends = tails(low, far_low, top)
-    bottom = prepare(foot, tile_mask, ends, devices, head, blocks - head)
-    first = window(low, far_low, turn(ends, 1), bottom)
-    parts = [swap(first, k) for k in range(2, far, 2)]
+    first = window(low, far_low, turn(ends, 1), ends)
+    parts = [swap(first, k) for k in near]
     other_first = swap(first, 1)
+    bottom = prepare(foot, tile_mask, first, devices, head, blocks - head)
     select, lines = choose(
         rec_hour.reshape(1, rows),
         observed.reshape(1, rows),
@@ -444,7 +445,7 @@
         lags,
         hours,
     )
-    rest = pack(parts, lines)
+    rest = pack(parts, lines, bottom)
     masked = (top, bottom)
     begun = score(first, rest, masked)
     mism, spread, other, other_rims = adjoint(

time: 44.3 us -> 42.7 us (0.964)
  waiting for transfers between devices: 9.55 us -> 6.83 us
  starting transfers between devices: 19.7 us -> 21 us
    ppermute x15, waiting for transfers between devices: 7.06 us -> 3.03 us  [swap(): return lax.ppermute(block, 'rcpt', [(i, i ^ bit) for i in devices])]
    ppermute x15, starting transfers between devices: 16.6 us -> 18 us  [swap(): return lax.ppermute(block, 'rcpt', [(i, i ^ bit) for i in devices])]
    ppermute x2, waiting for transfers between devices: 2.48 us -> 3.8 us  [turn(): lax.ppermute(block, 'hour', [(i, (i + distance) % size) for i in range(si...]
  transfers between devices with their start and end apart: 17 -> 17, of which waited for: 10 -> 8; matrix products, arithmetic and copies ran while one was open for 0% -> 0% of each run, Pallas kernels for 19% -> 20%
where the time goes in v5:
time: 42.7 us; the launch traced here: 42.5 us
  starting transfers between devices  21 us (49%)
  Pallas kernels  10.8 us (25%)
  waiting for transfers between devices  6.83 us (16%)
  other arithmetic  1.55 us (4%)
  between operations  1.47 us (3%)
  local copies, waits for them, and re-layouts  0.78 us (2%)
    ppermute x15, starting transfers between devices, swap(): return lax.ppermute(block, 'rcpt', [(i, i ^ bit) for i in devices])  18 us
    pallas_call x17, Pallas kernels, call(): pl.pallas_call(kernel, in_specs=[pl.BlockSpec(memory_space=where[c]) for...  10.8 us
    ppermute x2, waiting for transfers between devices, turn(): lax.ppermute(block, 'hour', [(i, (i + distance) % size) for i in range(si...  3.8 us
    ppermute x2, starting transfers between devices, turn(): lax.ppermute(block, 'hour', [(i, (i + distance) % size) for i in range(si...  3.05 us
    ppermute x15, waiting for transfers between devices, swap(): return lax.ppermute(block, 'rcpt', [(i, i ^ bit) for i in devices])  3.03 us
    convert_element_type x1, other arithmetic, per_device(): low = flux.astype(BF16)  0.9 us
  transfers between devices with their start and end apart: 17, of which 8 were waited for; matrix products, arithmetic and copies ran while one was open for 0% of the time, Pallas kernels for 20%

profile of v5, /device:TPU:0, one launch (start us, length us, event | category | flops | bytes accessed | tf_op | source)
XLA Modules:
  0.0 42.5 jit_solution(3053754428502413027)
XLA Ops:
  0.6 0.9 %convert_element_type.6.after_ref.low_ref = bf16[96,256]{1,0:T(8,128)(2,1)S(1)} convert(f32[96,256]{1,0:T(8,128)} %param.7) | non-fusion elementwise | flops 24576 | bytes 147456 | tf_op jit(solution)/shard_map/convert_element_type | solution.py:428
  1.5 4.0 %collective-permute-start = (bf16[96,256]{1,0:T(8,128)(2,1)S(1)}, bf16[96,256]{1,0:T(8,128)(2,1)S(1)}, u32[]{:S(2)}, u32[]{:S(2)}) collective-permute-start(bf16[96,256]{1,0:T(8,128)(2,1)S(1)} %convert_element_type.6.after_ref.low_ref), channel_id=1, source_target_pairs={{0,8},{1,9},{2,10},{3,11},{4,12},{5,13},{6,14},{7,15},{8,0},{9,1},... | collective-permute-start | bytes 147464 | tf_op jit(solution)/shard_map/ppermute | solution.py:21
  5.6 0.8 %copy-done = s32[8,8,32]{2,1,0:T(8,128)S(1)} copy-done((s32[8,8,32]{2,1,0:T(8,128)S(1)}, s32[8,8,32]{2,1,0:T(8,128)}, u32[]{:S(2)}) %copy-start) | copy-done | bytes 8216
  6.3 2.0 %prepare.2.after_ref.top_ref = bf16[16,384,256]{2,1,0:T(8,128)(2,1)S(1)} custom-call(bf16[1024,4096]{1,0:T(8,128)(2,1)} %bitcast.8, s32[8,8,32]{2,1,0:T(8,128)S(1)} %copy-done, bf16[96,256]{1,0:T(8,128)(2,1)S(1)} %convert_element_type.6.after_ref.low_ref), custom_call_target="tpu_custom_call" | custom-call | flops 10000000000 | bytes 6291456 | tf_op jit(solution)/shard_map/prepare/pallas_call | solution.py:40
  8.3 1.6 %collective-permute-start.1 = (bf16[16,256]{1,0:T(8,128)(2,1)S(1)}, bf16[16,256]{1,0:T(8,128)(2,1)S(1)}, u32[]{:S(2)}, u32[]{:S(2)}) collective-permute-start(bf16[16,256]{1,0:T(8,128)(2,1)S(1)} %tails.1.after_ref), channel_id=1, source_target_pairs={{0,16},{16,0},{1,17},{17,1},{2,18},{18,2},{3,19},{19,3},{4,20},{20... | collective-permute-start | bytes 24584 | tf_op jit(solution)/shard_map/ppermute | solution.py:26
  10.5 1.5 %collective-permute-done.1.rims_ref = bf16[16,256]{1,0:T(8,128)(2,1)S(1)} collective-permute-done((bf16[16,256]{1,0:T(8,128)(2,1)S(1)}, bf16[16,256]{1,0:T(8,128)(2,1)S(1)}, u32[]{:S(2)}, u32[]{:S(2)}) %collective-permute-start.1) | collective-permute-done | bytes 8224 | tf_op jit(solution)/shard_map/ppermute | solution.py:26
  12.1 2.6 %collective-permute-start.5 = (bf16[208,256]{1,0:T(8,128)(2,1)S(1)}, bf16[208,256]{1,0:T(8,128)(2,1)S(1)}, u32[]{:S(2)}, u32[]{:S(2)}) collective-permute-start(bf16[208,256]{1,0:T(8,128)(2,1)S(1)} %window.1.after_ref.first_ref), channel_id=1, source_target_pairs={{0,6},{1,7},{2,4},{3,5},{4,2},{5,3},{6,0},{7,1},{8,14},{9,15},{10,... | collective-permute-start | bytes 319496 | tf_op jit(solution)/shard_map/ppermute | solution.py:21
  14.7 0.4 %collective-permute-start.4 = (bf16[208,256]{1,0:T(8,128)(2,1)S(1)}, bf16[208,256]{1,0:T(8,128)(2,1)S(1)}, u32[]{:S(2)}, u32[]{:S(2)}) collective-permute-start(bf16[208,256]{1,0:T(8,128)(2,1)S(1)} %window.1.after_ref.first_ref), channel_id=1, source_target_pairs={{0,4},{1,5},{2,6},{3,7},{4,0},{5,1},{6,2},{7,3},{8,12},{9,13},{10,... | collective-permute-start | bytes 319496 | tf_op jit(solution)/shard_map/ppermute | solution.py:21
  15.1 0.5 %collective-permute-start.3 = (bf16[208,256]{1,0:T(8,128)(2,1)S(1)}, bf16[208,256]{1,0:T(8,128)(2,1)S(1)}, u32[]{:S(2)}, u32[]{:S(2)}) collective-permute-start(bf16[208,256]{1,0:T(8,128)(2,1)S(1)} %window.1.after_ref.first_ref), channel_id=1, source_target_pairs={{0,2},{1,3},{2,0},{3,1},{4,6},{5,7},{6,4},{7,5},{8,10},{9,11},{10,... | collective-permute-start | bytes 319496 | tf_op jit(solution)/shard_map/ppermute | solution.py:21
  15.6 2.6 %prepare.3.refs_4_.low_ref = bf16[16,640,256]{2,1,0:T(8,128)(2,1)S(1)} custom-call(bf16[1024,4096]{1,0:T(8,128)(2,1)} %bitcast.9, s32[8,8,32]{2,1,0:T(8,128)S(1)} %copy-done, bf16[208,256]{1,0:T(8,128)(2,1)S(1)} %window.1.after_ref.first_ref), custom_call_target="tpu_custom_call" | custom-call | flops 10000000000 | bytes 10485760 | tf_op jit(solution)/shard_map/prepare/pallas_call | solution.py:40
  18.3 0.5 %choose.1 = (f32[112,1024]{1,0:T(8,128)S(1)}, f32[16,1024]{1,0:T(8,128)S(1)}) custom-call(s32[1,128]{1,0:T(1,128)S(1)} %bitcast.5, f32[1,128]{1,0:T(1,128)S(1)} %bitcast.6, f32[1,128]{1,0:T(1,128)S(1)} %bitcast.7, s32[1]{0:T(128)S(6)} %copy.9.count_ref, bf16[208,256]{1,0:T(8,128)(2,1)S(1)} %window.1.after_ref.first_ref), custom_call_target="tpu_custom_call" | custom-call | flops 10000000000 | tf_op jit(solution)/shard_map/choose/pallas_call | solution.py:40
  18.8 0.6 %collective-permute-done.4.refs_1_ = bf16[208,256]{1,0:T(8,128)(2,1)S(1)} collective-permute-done((bf16[208,256]{1,0:T(8,128)(2,1)S(1)}, bf16[208,256]{1,0:T(8,128)(2,1)S(1)}, u32[]{:S(2)}, u32[]{:S(2)}) %collective-permute-start.4) | collective-permute-done | bytes 106528 | tf_op jit(solution)/shard_map/ppermute | solution.py:21
  19.4 0.4 %collective-permute-done.3.refs_0_ = bf16[208,256]{1,0:T(8,128)(2,1)S(1)} collective-permute-done((bf16[208,256]{1,0:T(8,128)(2,1)S(1)}, bf16[208,256]{1,0:T(8,128)(2,1)S(1)}, u32[]{:S(2)}, u32[]{:S(2)}) %collective-permute-start.3) | collective-permute-done | bytes 106528 | tf_op jit(solution)/shard_map/ppermute | solution.py:21
  19.9 0.5 %collective-permute-start.2 = (bf16[208,256]{1,0:T(8,128)(2,1)S(1)}, bf16[208,256]{1,0:T(8,128)(2,1)S(1)}, u32[]{:S(2)}, u32[]{:S(2)}) collective-permute-start(bf16[208,256]{1,0:T(8,128)(2,1)S(1)} %window.1.after_ref.first_ref), channel_id=1, source_target_pairs={{0,1},{1,0},{2,3},{3,2},{4,5},{5,4},{6,7},{7,6},{8,9},{9,8},{10,11... | collective-permute-start | bytes 319496 | tf_op jit(solution)/shard_map/ppermute | solution.py:21
  20.4 1.3 %score.1.begun_ref = f32[112,1024]{1,0:T(8,128)S(1)} custom-call(bf16[208,256]{1,0:T(8,128)(2,1)S(1)} %window.1.after_ref.first_ref, bf16[624,256]{1,0:T(8,128)(2,1)S(1)} %pack.1.rest_ref, bf16[16,384,256]{2,1,0:T(8,128)(2,1)S(1)} %prepare.2.after_ref.top_ref, bf16[16,640,256]{2,1,0:T(8,128)(2,1)S(1)} %prepare.3.refs_4_.low_ref), custom_call_target="tpu_custom_call" | custom-call | flops 469762048 | bytes 4194304 | tf_op jit(solution)/shard_map/score/pallas_call | solution.py:40
  21.7 2.4 %adjoint.1 = (f32[8,1024]{1,0:T(8,128)S(1)}, bf16[112,1024]{1,0:T(8,128)(2,1)S(1)}, bf16[8,96,256]{2,1,0:T(8,128)(2,1)S(1)}, bf16[64,256]{1,0:T(8,128)(2,1)S(1)}) custom-call(bf16[208,256]{1,0:T(8,128)(2,1)S(1)} %collective-permute-done.2.first_ref, bf16[624,256]{1,0:T(8,128)(2,1)S(1)} %collective-permute-done.6.rest_ref, ...), custom_call_target="tpu_custom_call" | custom-call | flops 939524096 | bytes 4194304 | tf_op jit(solution)/shard_map/adjoint/pallas_call | solution.py:40
  24.3 0.8 %mine.1 = (f32[8,96,256]{2,1,0:T(8,128)S(1)}, f32[64,256]{1,0:T(8,128)S(1)}) custom-call(bf16[112,1024]{1,0:T(8,128)(2,1)S(1)} %get-tuple-element.20.spread_ref, bf16[16,384,256]{2,1,0:T(8,128)(2,1)S(1)} %prepare.2.after_ref.top_ref, bf16[16,640,256]{2,1,0:T(8,128)(2,1)S(1)} %prepare.3.refs_4_.low_ref), custom_call_target="tpu_custom_call" | custom-call | flops 469762048 | bytes 4194304 | tf_op jit(solution)/shard_map/mine/pallas_call | solution.py:40
  25.1 0.2 collective-permute-done.7.came_ref
  25.4 0.2 collective-permute-start.8
  25.7 1.5 %collective-permute-start.9 = (bf16[64,256]{1,0:T(8,128)(2,1)S(1)}, bf16[64,256]{1,0:T(8,128)(2,1)S(1)}, u32[]{:S(2)}, u32[]{:S(2)}) collective-permute-start(bf16[64,256]{1,0:T(8,128)(2,1)S(1)} %rims.1.after_ref), channel_id=1, source_target_pairs={{0,16},{16,0},{1,17},{17,1},{2,18},{18,2},{3,19},{19,3},{4,20},{20... | collective-permute-start | bytes 98312 | tf_op jit(solution)/shard_map/ppermute | solution.py:26
  27.3 2.3 %collective-permute-done.9.rims_ref = bf16[64,256]{1,0:T(8,128)(2,1)S(1)} collective-permute-done((bf16[64,256]{1,0:T(8,128)(2,1)S(1)}, bf16[64,256]{1,0:T(8,128)(2,1)S(1)}, u32[]{:S(2)}, u32[]{:S(2)}) %collective-permute-start.9) | collective-permute-done | bytes 32800 | tf_op jit(solution)/shard_map/ppermute | solution.py:26
  29.6 1.6 %collective-permute-start.14 = (bf16[96,256]{1,0:T(8,128)(2,1)S(1)}, bf16[96,256]{1,0:T(8,128)(2,1)S(1)}, u32[]{:S(2)}, u32[]{:S(2)}) collective-permute-start(bf16[96,256]{1,0:T(8,128)(2,1)S(1)} %get-tuple-element.31), channel_id=1, source_target_pairs={{0,4},{1,5},{2,6},{3,7},{4,0},{5,1},{6,2},{7,3},{8,12},{9,13},{10,... | collective-permute-start | bytes 147464 | tf_op jit(solution)/shard_map/ppermute | solution.py:21
  31.2 0.5 %collective-permute-start.15 = (bf16[96,256]{1,0:T(8,128)(2,1)S(1)}, bf16[96,256]{1,0:T(8,128)(2,1)S(1)}, u32[]{:S(2)}, u32[]{:S(2)}) collective-permute-start(bf16[96,256]{1,0:T(8,128)(2,1)S(1)} %get-tuple-element.32), channel_id=1, source_target_pairs={{0,6},{1,7},{2,4},{3,5},{4,2},{5,3},{6,0},{7,1},{8,14},{9,15},{10,... | collective-permute-start | bytes 147464 | tf_op jit(solution)/shard_map/ppermute | solution.py:21
  31.7 1.4 %collective-permute-start.13 = (bf16[96,256]{1,0:T(8,128)(2,1)S(1)}, bf16[96,256]{1,0:T(8,128)(2,1)S(1)}, u32[]{:S(2)}, u32[]{:S(2)}) collective-permute-start(bf16[96,256]{1,0:T(8,128)(2,1)S(1)} %get-tuple-element.25.after_ref), channel_id=1, source_target_pairs={{0,2},{1,3},{2,0},{3,1},{4,6},{5,7},{6,4},{7,5},{8,10},{9,11},{10,... | collective-permute-start | bytes 147464 | tf_op jit(solution)/shard_map/ppermute | solution.py:21
  33.2 0.6 %collective-permute-start.10 = (bf16[96,256]{1,0:T(8,128)(2,1)S(1)}, bf16[96,256]{1,0:T(8,128)(2,1)S(1)}, u32[]{:S(2)}, u32[]{:S(2)}) collective-permute-start(bf16[96,256]{1,0:T(8,128)(2,1)S(1)} %get-tuple-element.27), channel_id=1, source_target_pairs={{0,2},{1,3},{2,0},{3,1},{4,6},{5,7},{6,4},{7,5},{8,10},{9,11},{10,... | collective-permute-start | bytes 147464 | tf_op jit(solution)/shard_map/ppermute | solution.py:21
  33.8 1.6 %collective-permute-start.11 = (bf16[96,256]{1,0:T(8,128)(2,1)S(1)}, bf16[96,256]{1,0:T(8,128)(2,1)S(1)}, u32[]{:S(2)}, u32[]{:S(2)}) collective-permute-start(bf16[96,256]{1,0:T(8,128)(2,1)S(1)} %get-tuple-element.28), channel_id=1, source_target_pairs={{0,4},{1,5},{2,6},{3,7},{4,0},{5,1},{6,2},{7,3},{8,12},{9,13},{10,... | collective-permute-start | bytes 147464 | tf_op jit(solution)/shard_map/ppermute | solution.py:21
  35.4 1.3 %collective-permute-start.12 = (bf16[96,256]{1,0:T(8,128)(2,1)S(1)}, bf16[96,256]{1,0:T(8,128)(2,1)S(1)}, u32[]{:S(2)}, u32[]{:S(2)}) collective-permute-start(bf16[96,256]{1,0:T(8,128)(2,1)S(1)} %get-tuple-element.29), channel_id=1, source_target_pairs={{0,6},{1,7},{2,4},{3,5},{4,2},{5,3},{6,0},{7,1},{8,14},{9,15},{10,... | collective-permute-start | bytes 147464 | tf_op jit(solution)/shard_map/ppermute | solution.py:21
  36.8 2.3 %collective-permute-start.16 = (bf16[96,256]{1,0:T(8,128)(2,1)S(1)}, bf16[96,256]{1,0:T(8,128)(2,1)S(1)}, u32[]{:S(2)}, u32[]{:S(2)}) collective-permute-start(bf16[96,256]{1,0:T(8,128)(2,1)S(1)} %outward.3), channel_id=1, source_target_pairs={{0,8},{1,9},{2,10},{3,11},{4,12},{5,13},{6,14},{7,15},{8,0},{9,1},... | collective-permute-start | bytes 147464 | tf_op jit(solution)/shard_map/ppermute | solution.py:21
  39.1 1.0 %narrow.1 = f32[1,128]{1,0:T(1,128)} custom-call(f32[8,1024]{1,0:T(8,128)S(1)} %get-tuple-element.33.mism_ref, f32[96,256]{1,0:T(8,128)S(1)} %get-tuple-element.30.first_ref.after_ref), custom_call_target="tpu_custom_call" | custom-call | flops 10000000000 | tf_op jit(solution)/shard_map/narrow/pallas_call | solution.py:40
  40.1 0.3 collective-permute-done.12.refs_2_
  40.4 1.4 %collective-permute-done.16 = bf16[96,256]{1,0:T(8,128)(2,1)S(1)} collective-permute-done((bf16[96,256]{1,0:T(8,128)(2,1)S(1)}, bf16[96,256]{1,0:T(8,128)(2,1)S(1)}, u32[]{:S(2)}, u32[]{:S(2)}) %collective-permute-start.16) | collective-permute-done | bytes 49184 | tf_op jit(solution)/shard_map/ppermute | solution.py:21
  41.8 0.7 %convert_add_fusion = f32[96,256]{1,0:T(8,128)} fusion(f32[96,256]{1,0:T(8,128)S(1)} %outward.2, bf16[96,256]{1,0:T(8,128)(2,1)S(1)} %collective-permute-done.16), kind=kLoop, calls=%fused_computation | loop fusion | flops 49152 | bytes 245760 | tf_op jit(solution)/shard_map/add | solution.py:468
  (29 shorter events, 0.6 us)
Async XLA Ops:
  1.5 6.8 %collective-permute-start = (bf16[96,256]{1,0:T(8,128)(2,1)S(1)}, bf16[96,256]{1,0:T(8,128)(2,1)S(1)}, u32[]{:S(2)}, u32[]{:S(2)}) collective-permute-start(bf16[96,256]{1,0:T(8,128)(2,1)S(1)} %convert_element_type.6.after_ref.low_ref), channel_id=1, source_target_pairs={{0,8},{1,9},{2,10},{3,11},{4,12},{5,13},{6,14},{7,15},{8,0},{9,1},... | collective-permute-start | bytes 147464 | tf_op jit(solution)/shard_map/ppermute | solution.py:21
  5.6 0.8 %copy-start = (s32[8,8,32]{2,1,0:T(8,128)S(1)}, s32[8,8,32]{2,1,0:T(8,128)}, u32[]{:S(2)}) copy-start(s32[8,8,32]{2,1,0:T(8,128)} %mask_ref.3) | copy-start | bytes 24580
  8.3 3.7 %collective-permute-start.1 = (bf16[16,256]{1,0:T(8,128)(2,1)S(1)}, bf16[16,256]{1,0:T(8,128)(2,1)S(1)}, u32[]{:S(2)}, u32[]{:S(2)}) collective-permute-start(bf16[16,256]{1,0:T(8,128)(2,1)S(1)} %tails.1.after_ref), channel_id=1, source_target_pairs={{0,16},{16,0},{1,17},{17,1},{2,18},{18,2},{3,19},{19,3},{4,20},{20... | collective-permute-start | bytes 24584 | tf_op jit(solution)/shard_map/ppermute | solution.py:26
  12.1 6.2 %copy-start.1 = (s32[128]{0:T(128)S(1)}, s32[128]{0:T(128)}, u32[]{:S(2)}) copy-start(s32[128]{0:T(128)} %param.10) | copy-start | bytes 1540
  12.1 6.2 %copy-start.2 = (f32[128]{0:T(128)S(1)}, f32[128]{0:T(128)}, u32[]{:S(2)}) copy-start(f32[128]{0:T(128)} %param.11) | copy-start | bytes 1540
  12.1 6.2 %copy-start.3 = (f32[128]{0:T(128)S(1)}, f32[128]{0:T(128)}, u32[]{:S(2)}) copy-start(f32[128]{0:T(128)} %param.12) | copy-start | bytes 1540
  12.1 6.7 %collective-permute-start.5 = (bf16[208,256]{1,0:T(8,128)(2,1)S(1)}, bf16[208,256]{1,0:T(8,128)(2,1)S(1)}, u32[]{:S(2)}, u32[]{:S(2)}) collective-permute-start(bf16[208,256]{1,0:T(8,128)(2,1)S(1)} %window.1.after_ref.first_ref), channel_id=1, source_target_pairs={{0,6},{1,7},{2,4},{3,5},{4,2},{5,3},{6,0},{7,1},{8,14},{9,15},{10,... | collective-permute-start | bytes 319496 | tf_op jit(solution)/shard_map/ppermute | solution.py:21
  14.7 4.7 %collective-permute-start.4 = (bf16[208,256]{1,0:T(8,128)(2,1)S(1)}, bf16[208,256]{1,0:T(8,128)(2,1)S(1)}, u32[]{:S(2)}, u32[]{:S(2)}) collective-permute-start(bf16[208,256]{1,0:T(8,128)(2,1)S(1)} %window.1.after_ref.first_ref), channel_id=1, source_target_pairs={{0,4},{1,5},{2,6},{3,7},{4,0},{5,1},{6,2},{7,3},{8,12},{9,13},{10,... | collective-permute-start | bytes 319496 | tf_op jit(solution)/shard_map/ppermute | solution.py:21
  15.1 4.7 %collective-permute-start.3 = (bf16[208,256]{1,0:T(8,128)(2,1)S(1)}, bf16[208,256]{1,0:T(8,128)(2,1)S(1)}, u32[]{:S(2)}, u32[]{:S(2)}) collective-permute-start(bf16[208,256]{1,0:T(8,128)(2,1)S(1)} %window.1.after_ref.first_ref), channel_id=1, source_target_pairs={{0,2},{1,3},{2,0},{3,1},{4,6},{5,7},{6,4},{7,5},{8,10},{9,11},{10,... | collective-permute-start | bytes 319496 | tf_op jit(solution)/shard_map/ppermute | solution.py:21
  19.9 1.9 %collective-permute-start.6 = (bf16[624,256]{1,0:T(8,128)(2,1)S(1)}, bf16[624,256]{1,0:T(8,128)(2,1)S(1)}, u32[]{:S(2)}, u32[]{:S(2)}) collective-permute-start(bf16[624,256]{1,0:T(8,128)(2,1)S(1)} %pack.1.rest_ref), channel_id=1, source_target_pairs={{0,1},{1,0},{2,3},{3,2},{4,5},{5,4},{6,7},{7,6},{8,9},{9,8},{10,11... | collective-permute-start | bytes 958472 | tf_op jit(solution)/shard_map/ppermute | solution.py:21
  19.9 1.8 %collective-permute-start.2 = (bf16[208,256]{1,0:T(8,128)(2,1)S(1)}, bf16[208,256]{1,0:T(8,128)(2,1)S(1)}, u32[]{:S(2)}, u32[]{:S(2)}) collective-permute-start(bf16[208,256]{1,0:T(8,128)(2,1)S(1)} %window.1.after_ref.first_ref), channel_id=1, source_target_pairs={{0,1},{1,0},{2,3},{3,2},{4,5},{5,4},{6,7},{7,6},{8,9},{9,8},{10,11... | collective-permute-start | bytes 319496 | tf_op jit(solution)/shard_map/ppermute | solution.py:21
  24.1 1.3 %collective-permute-start.7 = (bf16[64,256]{1,0:T(8,128)(2,1)S(1)}, bf16[64,256]{1,0:T(8,128)(2,1)S(1)}, u32[]{:S(2)}, u32[]{:S(2)}) collective-permute-start(bf16[64,256]{1,0:T(8,128)(2,1)S(1)} %get-tuple-element.24), channel_id=1, source_target_pairs={{0,1},{1,0},{2,3},{3,2},{4,5},{5,4},{6,7},{7,6},{8,9},{9,8},{10,11... | collective-permute-start | bytes 98312 | tf_op jit(solution)/shard_map/ppermute | solution.py:21
  25.4 1.8 %collective-permute-start.8 = (bf16[8,96,256]{2,1,0:T(8,128)(2,1)S(1)}, bf16[8,96,256]{2,1,0:T(8,128)(2,1)S(1)}, u32[]{:S(2)}, u32[]{:S(2)}) collective-permute-start(bf16[8,96,256]{2,1,0:T(8,128)(2,1)S(1)} %gate.1), channel_id=1, source_target_pairs={{0,1},{1,0},{2,3},{3,2},{4,5},{5,4},{6,7},{7,6},{8,9},{9,8},{10,11... | collective-permute-start | bytes 1179656 | tf_op jit(solution)/shard_map/ppermute | solution.py:21
  25.7 3.9 %collective-permute-start.9 = (bf16[64,256]{1,0:T(8,128)(2,1)S(1)}, bf16[64,256]{1,0:T(8,128)(2,1)S(1)}, u32[]{:S(2)}, u32[]{:S(2)}) collective-permute-start(bf16[64,256]{1,0:T(8,128)(2,1)S(1)} %rims.1.after_ref), channel_id=1, source_target_pairs={{0,16},{16,0},{1,17},{17,1},{2,18},{18,2},{3,19},{19,3},{4,20},{20... | collective-permute-start | bytes 98312 | tf_op jit(solution)/shard_map/ppermute | solution.py:26
  29.6 5.8 %collective-permute-start.14 = (bf16[96,256]{1,0:T(8,128)(2,1)S(1)}, bf16[96,256]{1,0:T(8,128)(2,1)S(1)}, u32[]{:S(2)}, u32[]{:S(2)}) collective-permute-start(bf16[96,256]{1,0:T(8,128)(2,1)S(1)} %get-tuple-element.31), channel_id=1, source_target_pairs={{0,4},{1,5},{2,6},{3,7},{4,0},{5,1},{6,2},{7,3},{8,12},{9,13},{10,... | collective-permute-start | bytes 147464 | tf_op jit(solution)/shard_map/ppermute | solution.py:21
  31.2 5.5 %collective-permute-start.15 = (bf16[96,256]{1,0:T(8,128)(2,1)S(1)}, bf16[96,256]{1,0:T(8,128)(2,1)S(1)}, u32[]{:S(2)}, u32[]{:S(2)}) collective-permute-start(bf16[96,256]{1,0:T(8,128)(2,1)S(1)} %get-tuple-element.32), channel_id=1, source_target_pairs={{0,6},{1,7},{2,4},{3,5},{4,2},{5,3},{6,0},{7,1},{8,14},{9,15},{10,... | collective-permute-start | bytes 147464 | tf_op jit(solution)/shard_map/ppermute | solution.py:21
  31.7 5.0 %collective-permute-start.13 = (bf16[96,256]{1,0:T(8,128)(2,1)S(1)}, bf16[96,256]{1,0:T(8,128)(2,1)S(1)}, u32[]{:S(2)}, u32[]{:S(2)}) collective-permute-start(bf16[96,256]{1,0:T(8,128)(2,1)S(1)} %get-tuple-element.25.after_ref), channel_id=1, source_target_pairs={{0,2},{1,3},{2,0},{3,1},{4,6},{5,7},{6,4},{7,5},{8,10},{9,11},{10,... | collective-permute-start | bytes 147464 | tf_op jit(solution)/shard_map/ppermute | solution.py:21
  33.2 6.9 %collective-permute-start.10 = (bf16[96,256]{1,0:T(8,128)(2,1)S(1)}, bf16[96,256]{1,0:T(8,128)(2,1)S(1)}, u32[]{:S(2)}, u32[]{:S(2)}) collective-permute-start(bf16[96,256]{1,0:T(8,128)(2,1)S(1)} %get-tuple-element.27), channel_id=1, source_target_pairs={{0,2},{1,3},{2,0},{3,1},{4,6},{5,7},{6,4},{7,5},{8,10},{9,11},{10,... | collective-permute-start | bytes 147464 | tf_op jit(solution)/shard_map/ppermute | solution.py:21
  33.8 6.3 %collective-permute-start.11 = (bf16[96,256]{1,0:T(8,128)(2,1)S(1)}, bf16[96,256]{1,0:T(8,128)(2,1)S(1)}, u32[]{:S(2)}, u32[]{:S(2)}) collective-permute-start(bf16[96,256]{1,0:T(8,128)(2,1)S(1)} %get-tuple-element.28), channel_id=1, source_target_pairs={{0,4},{1,5},{2,6},{3,7},{4,0},{5,1},{6,2},{7,3},{8,12},{9,13},{10,... | collective-permute-start | bytes 147464 | tf_op jit(solution)/shard_map/ppermute | solution.py:21
  35.4 5.0 %collective-permute-start.12 = (bf16[96,256]{1,0:T(8,128)(2,1)S(1)}, bf16[96,256]{1,0:T(8,128)(2,1)S(1)}, u32[]{:S(2)}, u32[]{:S(2)}) collective-permute-start(bf16[96,256]{1,0:T(8,128)(2,1)S(1)} %get-tuple-element.29), channel_id=1, source_target_pairs={{0,6},{1,7},{2,4},{3,5},{4,2},{5,3},{6,0},{7,1},{8,14},{9,15},{10,... | collective-permute-start | bytes 147464 | tf_op jit(solution)/shard_map/ppermute | solution.py:21
  36.8 5.1 %collective-permute-start.16 = (bf16[96,256]{1,0:T(8,128)(2,1)S(1)}, bf16[96,256]{1,0:T(8,128)(2,1)S(1)}, u32[]{:S(2)}, u32[]{:S(2)}) collective-permute-start(bf16[96,256]{1,0:T(8,128)(2,1)S(1)} %outward.3), channel_id=1, source_target_pairs={{0,8},{1,9},{2,10},{3,11},{4,12},{5,13},{6,14},{7,15},{8,0},{9,1},... | collective-permute-start | bytes 147464 | tf_op jit(solution)/shard_map/ppermute | solution.py:21

commit v6 on v5

--- a/solution.py
+++ b/solution.py
@@ -49,14 +49,27 @@
     )(*operands)
 
 
+def masks_kernel(mask_ref, after_ref, out_ref):
+    del after_ref
+    mask = mask_ref[...].astype(F32)
+    blocks, lags, tiles = mask.shape
+    twice = jnp.broadcast_to(mask[:, None], (blocks, 2, lags, tiles))
+    out_ref[...] = twice.reshape(blocks, 2 * lags, tiles)
+
+
+def masks_of(mask, after):
+    blocks, lags, tiles = mask.shape
+    outs = [((blocks, 2 * lags, tiles), F32)]
+    return call(masks_kernel, outs, [mask, after], "va", flops=BUSY, name="masks")[0]
+
+
 def prepare_kernel(devices, first, foot_hbm, mask_ref, after_ref, masked_ref, foot_ref, sems):
     del after_ref
     me = lax.axis_index("rcpt")
-    blocks, lags, tiles = mask_ref.shape
+    blocks, group, tiles = mask_ref.shape
     depth, cells = foot_ref.shape
     own = cells // devices
     tile = cells // tiles
-    group = 2 * lags
     part = foot_hbm.shape[0] // blocks
     used = depth // part
     copies = []
@@ -65,8 +78,7 @@
         copies.append(pltpu.make_async_copy(source, foot_ref.at[pl.ds(b * part, part)], sems.at[b]))
     for copy in copies:
         copy.start()
-    mask = mask_ref[first : first + used].astype(F32)
-    twice = jnp.broadcast_to(mask[:, None], (used, 2, lags, tiles)).reshape(used * group, tiles)
+    twice = mask_ref[first : first + used].reshape(used * group, tiles)
     wide = jnp.dot(twice.astype(BF16), expander(tiles, tile, BF16), preferred_element_type=F32)
     wide = wide.astype(BF16)
     for b in range(used):
@@ -127,31 +139,44 @@
     )
 
 
-def tails_kernel(low_ref, far_ref, after_ref, out_ref):
-    del after_ref
+def edge_kernel(low_ref, out_ref):
     hours = low_ref.shape[0]
-    ends = [ref[hours - PAIR :].astype(F32)[RIM:] for ref in (low_ref, far_ref)]
-    out_ref[...] = jnp.concatenate(ends, axis=0).astype(BF16)
-
-
-def tails(low, far_low, after):
-    outs = [((PAIR, low.shape[1]), BF16)]
-    return call(tails_kernel, outs, [low, far_low, after], "vva", name="tails")[0]
-
-
-def window_kernel(low_ref, far_ref, rims_ref, after_ref, out_ref):
+    out_ref[...] = low_ref[hours - PAIR :].astype(F32)[RIM:].astype(BF16)
+
+
+def edge(low):
+    outs = [((RIM, low.shape[1]), BF16)]
+    return call(edge_kernel, outs, [low], "v", name="edge")[0]
+
+
+def block_kernel(low_ref, rim_ref, after_ref, out_ref):
     del after_ref
     hours = low_ref.shape[0]
     inside = (lax.axis_index("hour") > 0).astype(F32)
+    rim = rim_ref[...].astype(F32) * inside
     out_ref[:hours] = low_ref[...]
-    out_ref[hours : 2 * hours] = far_ref[...]
-    out_ref[2 * hours :] = (rims_ref[...].astype(F32) * inside).astype(BF16)
-
-
-def window(low, far_low, rims, after):
+    out_ref[hours:] = jnp.concatenate([rim, jnp.zeros_like(rim)], axis=0).astype(BF16)
+
+
+def block_of(low, rim, after):
     hours, columns = low.shape
-    outs = [((2 * hours + PAIR, columns), BF16)]
-    return call(window_kernel, outs, [low, far_low, rims, after], "vvva", name="window")[0]
+    outs = [((hours + PAIR, columns), BF16)]
+    return call(block_kernel, outs, [low, rim, after], "vva", name="block")[0]
+
+
+def window_kernel(near_ref, far_ref, after_ref, out_ref):
+    del after_ref
+    hours = near_ref.shape[0] - PAIR
+    out_ref[:hours] = near_ref[:hours]
+    out_ref[hours : 2 * hours] = far_ref[:hours]
+    rims = [ref[hours:].astype(F32)[:RIM] for ref in (near_ref, far_ref)]
+    out_ref[2 * hours :] = jnp.concatenate(rims, axis=0).astype(BF16)
+
+
+def window(near, far, after):
+    height, columns = near.shape
+    outs = [((2 * height - PAIR, columns), BF16)]
+    return call(window_kernel, outs, [near, far, after], "vva", name="window")[0]
 
 
 def pack_kernel(count, *refs):
@@ -426,16 +451,18 @@
     near = range(2, far, 2)
 
     low = flux.astype(BF16)
-    far_low = swap(low, far)
+    end = edge(low)
+    masks = masks_of(tile_mask, end)
+    block = block_of(low, turn(end, 1), masks)
+    far_block = swap(block, far)
     foot = footprint.reshape(rows * lags, cells)
     blocks = tile_mask.shape[0]
     head = blocks * 3 // 8
-    top = prepare(foot, tile_mask, low, devices, 0, head)
-    ends = tails(low, far_low, top)
-    first = window(low, far_low, turn(ends, 1), ends)
+    top = prepare(foot, masks, block, devices, 0, head)
+    first = window(block, far_block, top)
     parts = [swap(first, k) for k in near]
     other_first = swap(first, 1)
-    bottom = prepare(foot, tile_mask, first, devices, head, blocks - head)
+    bottom = prepare(foot, masks, first, devices, head, blocks - head)
     select, lines = choose(
         rec_hour.reshape(1, rows),
         observed.reshape(1, rows),

time: 42.7 us -> 42.5 us (level)
  waiting for transfers between devices: 6.83 us -> 5.49 us
  starting transfers between devices: 21 us -> 22.1 us
    ppermute x2, starting transfers between devices: 3.05 us -> 4.49 us  [turn(): lax.ppermute(block, 'hour', [(i, (i + distance) % size) for i in range(si...]
    ppermute x2, waiting for transfers between devices: 3.8 us -> 2.46 us  [turn(): lax.ppermute(block, 'hour', [(i, (i + distance) % size) for i in range(si...]
    pallas_call x17 -> x19, Pallas kernels: 10.8 us -> 10.9 us  [call(): pl.pallas_call(kernel, in_specs=[pl.BlockSpec(memory_space=where[c]) for...]
where the time goes in v6:
time: 42.5 us; the launch traced here: 42.2 us
  starting transfers between devices  22.1 us (52%)
  Pallas kernels  10.9 us (26%)
  waiting for transfers between devices  5.49 us (13%)
  other arithmetic  1.55 us (4%)
  between operations  1.46 us (3%)
  local copies, waits for them, and re-layouts  0.78 us (2%)
    ppermute x15, starting transfers between devices, swap(): return lax.ppermute(block, 'rcpt', [(i, i ^ bit) for i in devices])  17.6 us
    pallas_call x19, Pallas kernels, call(): pl.pallas_call(kernel, in_specs=[pl.BlockSpec(memory_space=where[c]) for...  10.9 us
    ppermute x2, starting transfers between devices, turn(): lax.ppermute(block, 'hour', [(i, (i + distance) % size) for i in range(si...  4.49 us
    ppermute x15, waiting for transfers between devices, swap(): return lax.ppermute(block, 'rcpt', [(i, i ^ bit) for i in devices])  3.03 us
    ppermute x2, waiting for transfers between devices, turn(): lax.ppermute(block, 'hour', [(i, (i + distance) % size) for i in range(si...  2.46 us
    convert_element_type x1, other arithmetic, per_device(): low = flux.astype(BF16)  0.9 us
  transfers between devices with their start and end apart: 17, of which 8 were waited for; matrix products, arithmetic and copies ran while one was open for 0% of the time, Pallas kernels for 20%

profile of v6, /device:TPU:0, one launch (start us, length us, event | category | flops | bytes accessed | tf_op | source)
XLA Modules:
  0.0 42.2 jit_solution(2988414060470598148)
XLA Ops:
  0.6 0.9 %convert_element_type.6.low_ref = bf16[96,256]{1,0:T(8,128)(2,1)S(1)} convert(f32[96,256]{1,0:T(8,128)} %param.7) | non-fusion elementwise | flops 24576 | bytes 147456 | tf_op jit(solution)/shard_map/convert_element_type | solution.py:453
  1.5 3.0 %collective-permute-start = (bf16[8,256]{1,0:T(8,128)(2,1)S(1)}, bf16[8,256]{1,0:T(8,128)(2,1)S(1)}, u32[]{:S(2)}, u32[]{:S(2)}) collective-permute-start(bf16[8,256]{1,0:T(8,128)(2,1)S(1)} %edge.1.after_ref), channel_id=1, source_target_pairs={{0,16},{16,0},{1,17},{17,1},{2,18},{18,2},{3,19},{19,3},{4,20},{20... | collective-permute-start | bytes 12296 | tf_op jit(solution)/shard_map/ppermute | solution.py:26
  4.5 0.8 %copy-done = s32[8,8,32]{2,1,0:T(8,128)S(1)} copy-done((s32[8,8,32]{2,1,0:T(8,128)S(1)}, s32[8,8,32]{2,1,0:T(8,128)}, u32[]{:S(2)}) %copy-start) | copy-done | bytes 8216
  6.1 3.2 %collective-permute-start.1 = (bf16[112,256]{1,0:T(8,128)(2,1)S(1)}, bf16[112,256]{1,0:T(8,128)(2,1)S(1)}, u32[]{:S(2)}, u32[]{:S(2)}) collective-permute-start(bf16[112,256]{1,0:T(8,128)(2,1)S(1)} %block.1.after_ref.near_ref), channel_id=1, source_target_pairs={{0,8},{1,9},{2,10},{3,11},{4,12},{5,13},{6,14},{7,15},{8,0},{9,1},... | collective-permute-start | bytes 172040 | tf_op jit(solution)/shard_map/ppermute | solution.py:21
  9.3 2.0 %prepare.2.after_ref.top_ref = bf16[16,384,256]{2,1,0:T(8,128)(2,1)S(1)} custom-call(bf16[1024,4096]{1,0:T(8,128)(2,1)} %bitcast.8, f32[8,16,32]{2,1,0:T(8,128)S(1)} %masks.1.after_ref.mask_ref, bf16[112,256]{1,0:T(8,128)(2,1)S(1)} %block.1.after_ref.near_ref), custom_call_target="tpu_custom_call" | custom-call | flops 10000000000 | bytes 6291456 | tf_op jit(solution)/shard_map/prepare/pallas_call | solution.py:40
  11.3 0.2 collective-permute-done.1.far_ref
  11.5 2.9 %collective-permute-start.5 = (bf16[208,256]{1,0:T(8,128)(2,1)S(1)}, bf16[208,256]{1,0:T(8,128)(2,1)S(1)}, u32[]{:S(2)}, u32[]{:S(2)}) collective-permute-start(bf16[208,256]{1,0:T(8,128)(2,1)S(1)} %window.1.after_ref.first_ref), channel_id=1, source_target_pairs={{0,6},{1,7},{2,4},{3,5},{4,2},{5,3},{6,0},{7,1},{8,14},{9,15},{10,... | collective-permute-start | bytes 319496 | tf_op jit(solution)/shard_map/ppermute | solution.py:21
  14.4 0.4 %collective-permute-start.4 = (bf16[208,256]{1,0:T(8,128)(2,1)S(1)}, bf16[208,256]{1,0:T(8,128)(2,1)S(1)}, u32[]{:S(2)}, u32[]{:S(2)}) collective-permute-start(bf16[208,256]{1,0:T(8,128)(2,1)S(1)} %window.1.after_ref.first_ref), channel_id=1, source_target_pairs={{0,4},{1,5},{2,6},{3,7},{4,0},{5,1},{6,2},{7,3},{8,12},{9,13},{10,... | collective-permute-start | bytes 319496 | tf_op jit(solution)/shard_map/ppermute | solution.py:21
  14.9 0.2 collective-permute-start.3
  15.1 2.6 %prepare.3.refs_4_.low_ref = bf16[16,640,256]{2,1,0:T(8,128)(2,1)S(1)} custom-call(bf16[1024,4096]{1,0:T(8,128)(2,1)} %bitcast.9, f32[8,16,32]{2,1,0:T(8,128)S(1)} %masks.1.after_ref.mask_ref, bf16[208,256]{1,0:T(8,128)(2,1)S(1)} %window.1.after_ref.first_ref), custom_call_target="tpu_custom_call" | custom-call | flops 10000000000 | bytes 10485760 | tf_op jit(solution)/shard_map/prepare/pallas_call | solution.py:40
  17.7 0.5 %choose.1 = (f32[112,1024]{1,0:T(8,128)S(1)}, f32[16,1024]{1,0:T(8,128)S(1)}) custom-call(s32[1,128]{1,0:T(1,128)S(1)} %bitcast.5, f32[1,128]{1,0:T(1,128)S(1)} %bitcast.6, f32[1,128]{1,0:T(1,128)S(1)} %bitcast.7, s32[1]{0:T(128)S(6)} %copy.9.count_ref, bf16[208,256]{1,0:T(8,128)(2,1)S(1)} %window.1.after_ref.first_ref), custom_call_target="tpu_custom_call" | custom-call | flops 10000000000 | tf_op jit(solution)/shard_map/choose/pallas_call | solution.py:40
  18.3 0.9 %collective-permute-done.4.refs_1_ = bf16[208,256]{1,0:T(8,128)(2,1)S(1)} collective-permute-done((bf16[208,256]{1,0:T(8,128)(2,1)S(1)}, bf16[208,256]{1,0:T(8,128)(2,1)S(1)}, u32[]{:S(2)}, u32[]{:S(2)}) %collective-permute-start.4) | collective-permute-done | bytes 106528 | tf_op jit(solution)/shard_map/ppermute | solution.py:21
  19.2 0.4 %collective-permute-done.3.refs_0_ = bf16[208,256]{1,0:T(8,128)(2,1)S(1)} collective-permute-done((bf16[208,256]{1,0:T(8,128)(2,1)S(1)}, bf16[208,256]{1,0:T(8,128)(2,1)S(1)}, u32[]{:S(2)}, u32[]{:S(2)}) %collective-permute-start.3) | collective-permute-done | bytes 106528 | tf_op jit(solution)/shard_map/ppermute | solution.py:21
  19.7 0.5 %collective-permute-start.2 = (bf16[208,256]{1,0:T(8,128)(2,1)S(1)}, bf16[208,256]{1,0:T(8,128)(2,1)S(1)}, u32[]{:S(2)}, u32[]{:S(2)}) collective-permute-start(bf16[208,256]{1,0:T(8,128)(2,1)S(1)} %window.1.after_ref.first_ref), channel_id=1, source_target_pairs={{0,1},{1,0},{2,3},{3,2},{4,5},{5,4},{6,7},{7,6},{8,9},{9,8},{10,11... | collective-permute-start | bytes 319496 | tf_op jit(solution)/shard_map/ppermute | solution.py:21
  20.2 1.3 %score.1.begun_ref = f32[112,1024]{1,0:T(8,128)S(1)} custom-call(bf16[208,256]{1,0:T(8,128)(2,1)S(1)} %window.1.after_ref.first_ref, bf16[624,256]{1,0:T(8,128)(2,1)S(1)} %pack.1.rest_ref, bf16[16,384,256]{2,1,0:T(8,128)(2,1)S(1)} %prepare.2.after_ref.top_ref, bf16[16,640,256]{2,1,0:T(8,128)(2,1)S(1)} %prepare.3.refs_4_.low_ref), custom_call_target="tpu_custom_call" | custom-call | flops 469762048 | bytes 4194304 | tf_op jit(solution)/shard_map/score/pallas_call | solution.py:40
  21.5 2.4 %adjoint.1 = (f32[8,1024]{1,0:T(8,128)S(1)}, bf16[112,1024]{1,0:T(8,128)(2,1)S(1)}, bf16[8,96,256]{2,1,0:T(8,128)(2,1)S(1)}, bf16[64,256]{1,0:T(8,128)(2,1)S(1)}) custom-call(bf16[208,256]{1,0:T(8,128)(2,1)S(1)} %collective-permute-done.2.first_ref, bf16[624,256]{1,0:T(8,128)(2,1)S(1)} %collective-permute-done.6.rest_ref, ...), custom_call_target="tpu_custom_call" | custom-call | flops 939524096 | bytes 4194304 | tf_op jit(solution)/shard_map/adjoint/pallas_call | solution.py:40
  23.9 0.2 collective-permute-start.7
  24.0 0.8 %mine.1 = (f32[8,96,256]{2,1,0:T(8,128)S(1)}, f32[64,256]{1,0:T(8,128)S(1)}) custom-call(bf16[112,1024]{1,0:T(8,128)(2,1)S(1)} %get-tuple-element.20.spread_ref, bf16[16,384,256]{2,1,0:T(8,128)(2,1)S(1)} %prepare.2.after_ref.top_ref, bf16[16,640,256]{2,1,0:T(8,128)(2,1)S(1)} %prepare.3.refs_4_.low_ref), custom_call_target="tpu_custom_call" | custom-call | flops 469762048 | bytes 4194304 | tf_op jit(solution)/shard_map/mine/pallas_call | solution.py:40
  24.9 0.2 collective-permute-done.7.came_ref
  25.2 0.2 collective-permute-start.8
  25.4 1.5 %collective-permute-start.9 = (bf16[64,256]{1,0:T(8,128)(2,1)S(1)}, bf16[64,256]{1,0:T(8,128)(2,1)S(1)}, u32[]{:S(2)}, u32[]{:S(2)}) collective-permute-start(bf16[64,256]{1,0:T(8,128)(2,1)S(1)} %rims.1.after_ref), channel_id=1, source_target_pairs={{0,16},{16,0},{1,17},{17,1},{2,18},{18,2},{3,19},{19,3},{4,20},{20... | collective-permute-start | bytes 98312 | tf_op jit(solution)/shard_map/ppermute | solution.py:26
  27.0 2.3 %collective-permute-done.9.rims_ref = bf16[64,256]{1,0:T(8,128)(2,1)S(1)} collective-permute-done((bf16[64,256]{1,0:T(8,128)(2,1)S(1)}, bf16[64,256]{1,0:T(8,128)(2,1)S(1)}, u32[]{:S(2)}, u32[]{:S(2)}) %collective-permute-start.9) | collective-permute-done | bytes 32800 | tf_op jit(solution)/shard_map/ppermute | solution.py:26
  29.4 1.6 %collective-permute-start.14 = (bf16[96,256]{1,0:T(8,128)(2,1)S(1)}, bf16[96,256]{1,0:T(8,128)(2,1)S(1)}, u32[]{:S(2)}, u32[]{:S(2)}) collective-permute-start(bf16[96,256]{1,0:T(8,128)(2,1)S(1)} %get-tuple-element.31), channel_id=1, source_target_pairs={{0,4},{1,5},{2,6},{3,7},{4,0},{5,1},{6,2},{7,3},{8,12},{9,13},{10,... | collective-permute-start | bytes 147464 | tf_op jit(solution)/shard_map/ppermute | solution.py:21
  31.0 0.5 %collective-permute-start.15 = (bf16[96,256]{1,0:T(8,128)(2,1)S(1)}, bf16[96,256]{1,0:T(8,128)(2,1)S(1)}, u32[]{:S(2)}, u32[]{:S(2)}) collective-permute-start(bf16[96,256]{1,0:T(8,128)(2,1)S(1)} %get-tuple-element.32), channel_id=1, source_target_pairs={{0,6},{1,7},{2,4},{3,5},{4,2},{5,3},{6,0},{7,1},{8,14},{9,15},{10,... | collective-permute-start | bytes 147464 | tf_op jit(solution)/shard_map/ppermute | solution.py:21
  31.5 1.5 %collective-permute-start.13 = (bf16[96,256]{1,0:T(8,128)(2,1)S(1)}, bf16[96,256]{1,0:T(8,128)(2,1)S(1)}, u32[]{:S(2)}, u32[]{:S(2)}) collective-permute-start(bf16[96,256]{1,0:T(8,128)(2,1)S(1)} %get-tuple-element.25.after_ref), channel_id=1, source_target_pairs={{0,2},{1,3},{2,0},{3,1},{4,6},{5,7},{6,4},{7,5},{8,10},{9,11},{10,... | collective-permute-start | bytes 147464 | tf_op jit(solution)/shard_map/ppermute | solution.py:21
  32.9 0.6 %collective-permute-start.10 = (bf16[96,256]{1,0:T(8,128)(2,1)S(1)}, bf16[96,256]{1,0:T(8,128)(2,1)S(1)}, u32[]{:S(2)}, u32[]{:S(2)}) collective-permute-start(bf16[96,256]{1,0:T(8,128)(2,1)S(1)} %get-tuple-element.27), channel_id=1, source_target_pairs={{0,2},{1,3},{2,0},{3,1},{4,6},{5,7},{6,4},{7,5},{8,10},{9,11},{10,... | collective-permute-start | bytes 147464 | tf_op jit(solution)/shard_map/ppermute | solution.py:21
  33.6 1.6 %collective-permute-start.11 = (bf16[96,256]{1,0:T(8,128)(2,1)S(1)}, bf16[96,256]{1,0:T(8,128)(2,1)S(1)}, u32[]{:S(2)}, u32[]{:S(2)}) collective-permute-start(bf16[96,256]{1,0:T(8,128)(2,1)S(1)} %get-tuple-element.28), channel_id=1, source_target_pairs={{0,4},{1,5},{2,6},{3,7},{4,0},{5,1},{6,2},{7,3},{8,12},{9,13},{10,... | collective-permute-start | bytes 147464 | tf_op jit(solution)/shard_map/ppermute | solution.py:21
  35.2 1.3 %collective-permute-start.12 = (bf16[96,256]{1,0:T(8,128)(2,1)S(1)}, bf16[96,256]{1,0:T(8,128)(2,1)S(1)}, u32[]{:S(2)}, u32[]{:S(2)}) collective-permute-start(bf16[96,256]{1,0:T(8,128)(2,1)S(1)} %get-tuple-element.29), channel_id=1, source_target_pairs={{0,6},{1,7},{2,4},{3,5},{4,2},{5,3},{6,0},{7,1},{8,14},{9,15},{10,... | collective-permute-start | bytes 147464 | tf_op jit(solution)/shard_map/ppermute | solution.py:21
  36.5 2.8 %collective-permute-start.16 = (bf16[96,256]{1,0:T(8,128)(2,1)S(1)}, bf16[96,256]{1,0:T(8,128)(2,1)S(1)}, u32[]{:S(2)}, u32[]{:S(2)}) collective-permute-start(bf16[96,256]{1,0:T(8,128)(2,1)S(1)} %outward.3), channel_id=1, source_target_pairs={{0,8},{1,9},{2,10},{3,11},{4,12},{5,13},{6,14},{7,15},{8,0},{9,1},... | collective-permute-start | bytes 147464 | tf_op jit(solution)/shard_map/ppermute | solution.py:21
  39.3 1.0 %narrow.1 = f32[1,128]{1,0:T(1,128)} custom-call(f32[8,1024]{1,0:T(8,128)S(1)} %get-tuple-element.33.mism_ref, f32[96,256]{1,0:T(8,128)S(1)} %get-tuple-element.30.first_ref.after_ref), custom_call_target="tpu_custom_call" | custom-call | flops 10000000000 | tf_op jit(solution)/shard_map/narrow/pallas_call | solution.py:40
  40.4 1.2 %collective-permute-done.16 = bf16[96,256]{1,0:T(8,128)(2,1)S(1)} collective-permute-done((bf16[96,256]{1,0:T(8,128)(2,1)S(1)}, bf16[96,256]{1,0:T(8,128)(2,1)S(1)}, u32[]{:S(2)}, u32[]{:S(2)}) %collective-permute-start.16) | collective-permute-done | bytes 49184 | tf_op jit(solution)/shard_map/ppermute | solution.py:21
  41.6 0.7 %convert_add_fusion = f32[96,256]{1,0:T(8,128)} fusion(f32[96,256]{1,0:T(8,128)S(1)} %outward.2, bf16[96,256]{1,0:T(8,128)(2,1)S(1)} %collective-permute-done.16), kind=kLoop, calls=%fused_computation | loop fusion | flops 49152 | bytes 245760 | tf_op jit(solution)/shard_map/add | solution.py:495
  (31 shorter events, 0.6 us)
Async XLA Ops:
  1.5 4.6 %collective-permute-start = (bf16[8,256]{1,0:T(8,128)(2,1)S(1)}, bf16[8,256]{1,0:T(8,128)(2,1)S(1)}, u32[]{:S(2)}, u32[]{:S(2)}) collective-permute-start(bf16[8,256]{1,0:T(8,128)(2,1)S(1)} %edge.1.after_ref), channel_id=1, source_target_pairs={{0,16},{16,0},{1,17},{17,1},{2,18},{18,2},{3,19},{19,3},{4,20},{20... | collective-permute-start | bytes 12296 | tf_op jit(solution)/shard_map/ppermute | solution.py:26
  4.5 0.8 %copy-start = (s32[8,8,32]{2,1,0:T(8,128)S(1)}, s32[8,8,32]{2,1,0:T(8,128)}, u32[]{:S(2)}) copy-start(s32[8,8,32]{2,1,0:T(8,128)} %mask_ref.1) | copy-start | bytes 24580
  6.1 5.3 %collective-permute-start.1 = (bf16[112,256]{1,0:T(8,128)(2,1)S(1)}, bf16[112,256]{1,0:T(8,128)(2,1)S(1)}, u32[]{:S(2)}, u32[]{:S(2)}) collective-permute-start(bf16[112,256]{1,0:T(8,128)(2,1)S(1)} %block.1.after_ref.near_ref), channel_id=1, source_target_pairs={{0,8},{1,9},{2,10},{3,11},{4,12},{5,13},{6,14},{7,15},{8,0},{9,1},... | collective-permute-start | bytes 172040 | tf_op jit(solution)/shard_map/ppermute | solution.py:21
  11.5 6.2 %copy-start.1 = (s32[128]{0:T(128)S(1)}, s32[128]{0:T(128)}, u32[]{:S(2)}) copy-start(s32[128]{0:T(128)} %param.10) | copy-start | bytes 1540
  11.5 6.2 %copy-start.2 = (f32[128]{0:T(128)S(1)}, f32[128]{0:T(128)}, u32[]{:S(2)}) copy-start(f32[128]{0:T(128)} %param.11) | copy-start | bytes 1540
  11.5 6.2 %copy-start.3 = (f32[128]{0:T(128)S(1)}, f32[128]{0:T(128)}, u32[]{:S(2)}) copy-start(f32[128]{0:T(128)} %param.12) | copy-start | bytes 1540
  11.5 6.7 %collective-permute-start.5 = (bf16[208,256]{1,0:T(8,128)(2,1)S(1)}, bf16[208,256]{1,0:T(8,128)(2,1)S(1)}, u32[]{:S(2)}, u32[]{:S(2)}) collective-permute-start(bf16[208,256]{1,0:T(8,128)(2,1)S(1)} %window.1.after_ref.first_ref), channel_id=1, source_target_pairs={{0,6},{1,7},{2,4},{3,5},{4,2},{5,3},{6,0},{7,1},{8,14},{9,15},{10,... | collective-permute-start | bytes 319496 | tf_op jit(solution)/shard_map/ppermute | solution.py:21
  14.4 4.7 %collective-permute-start.4 = (bf16[208,256]{1,0:T(8,128)(2,1)S(1)}, bf16[208,256]{1,0:T(8,128)(2,1)S(1)}, u32[]{:S(2)}, u32[]{:S(2)}) collective-permute-start(bf16[208,256]{1,0:T(8,128)(2,1)S(1)} %window.1.after_ref.first_ref), channel_id=1, source_target_pairs={{0,4},{1,5},{2,6},{3,7},{4,0},{5,1},{6,2},{7,3},{8,12},{9,13},{10,... | collective-permute-start | bytes 319496 | tf_op jit(solution)/shard_map/ppermute | solution.py:21
  14.9 4.7 %collective-permute-start.3 = (bf16[208,256]{1,0:T(8,128)(2,1)S(1)}, bf16[208,256]{1,0:T(8,128)(2,1)S(1)}, u32[]{:S(2)}, u32[]{:S(2)}) collective-permute-start(bf16[208,256]{1,0:T(8,128)(2,1)S(1)} %window.1.after_ref.first_ref), channel_id=1, source_target_pairs={{0,2},{1,3},{2,0},{3,1},{4,6},{5,7},{6,4},{7,5},{8,10},{9,11},{10,... | collective-permute-start | bytes 319496 | tf_op jit(solution)/shard_map/ppermute | solution.py:21
  19.6 1.9 %collective-permute-start.6 = (bf16[624,256]{1,0:T(8,128)(2,1)S(1)}, bf16[624,256]{1,0:T(8,128)(2,1)S(1)}, u32[]{:S(2)}, u32[]{:S(2)}) collective-permute-start(bf16[624,256]{1,0:T(8,128)(2,1)S(1)} %pack.1.rest_ref), channel_id=1, source_target_pairs={{0,1},{1,0},{2,3},{3,2},{4,5},{5,4},{6,7},{7,6},{8,9},{9,8},{10,11... | collective-permute-start | bytes 958472 | tf_op jit(solution)/shard_map/ppermute | solution.py:21
  19.7 1.8 %collective-permute-start.2 = (bf16[208,256]{1,0:T(8,128)(2,1)S(1)}, bf16[208,256]{1,0:T(8,128)(2,1)S(1)}, u32[]{:S(2)}, u32[]{:S(2)}) collective-permute-start(bf16[208,256]{1,0:T(8,128)(2,1)S(1)} %window.1.after_ref.first_ref), channel_id=1, source_target_pairs={{0,1},{1,0},{2,3},{3,2},{4,5},{5,4},{6,7},{7,6},{8,9},{9,8},{10,11... | collective-permute-start | bytes 319496 | tf_op jit(solution)/shard_map/ppermute | solution.py:21
  23.9 1.3 %collective-permute-start.7 = (bf16[64,256]{1,0:T(8,128)(2,1)S(1)}, bf16[64,256]{1,0:T(8,128)(2,1)S(1)}, u32[]{:S(2)}, u32[]{:S(2)}) collective-permute-start(bf16[64,256]{1,0:T(8,128)(2,1)S(1)} %get-tuple-element.24), channel_id=1, source_target_pairs={{0,1},{1,0},{2,3},{3,2},{4,5},{5,4},{6,7},{7,6},{8,9},{9,8},{10,11... | collective-permute-start | bytes 98312 | tf_op jit(solution)/shard_map/ppermute | solution.py:21
  25.2 1.8 %collective-permute-start.8 = (bf16[8,96,256]{2,1,0:T(8,128)(2,1)S(1)}, bf16[8,96,256]{2,1,0:T(8,128)(2,1)S(1)}, u32[]{:S(2)}, u32[]{:S(2)}) collective-permute-start(bf16[8,96,256]{2,1,0:T(8,128)(2,1)S(1)} %gate.1), channel_id=1, source_target_pairs={{0,1},{1,0},{2,3},{3,2},{4,5},{5,4},{6,7},{7,6},{8,9},{9,8},{10,11... | collective-permute-start | bytes 1179656 | tf_op jit(solution)/shard_map/ppermute | solution.py:21
  25.4 3.9 %collective-permute-start.9 = (bf16[64,256]{1,0:T(8,128)(2,1)S(1)}, bf16[64,256]{1,0:T(8,128)(2,1)S(1)}, u32[]{:S(2)}, u32[]{:S(2)}) collective-permute-start(bf16[64,256]{1,0:T(8,128)(2,1)S(1)} %rims.1.after_ref), channel_id=1, source_target_pairs={{0,16},{16,0},{1,17},{17,1},{2,18},{18,2},{3,19},{19,3},{4,20},{20... | collective-permute-start | bytes 98312 | tf_op jit(solution)/shard_map/ppermute | solution.py:26
  29.4 5.8 %collective-permute-start.14 = (bf16[96,256]{1,0:T(8,128)(2,1)S(1)}, bf16[96,256]{1,0:T(8,128)(2,1)S(1)}, u32[]{:S(2)}, u32[]{:S(2)}) collective-permute-start(bf16[96,256]{1,0:T(8,128)(2,1)S(1)} %get-tuple-element.31), channel_id=1, source_target_pairs={{0,4},{1,5},{2,6},{3,7},{4,0},{5,1},{6,2},{7,3},{8,12},{9,13},{10,... | collective-permute-start | bytes 147464 | tf_op jit(solution)/shard_map/ppermute | solution.py:21
  31.0 5.5 %collective-permute-start.15 = (bf16[96,256]{1,0:T(8,128)(2,1)S(1)}, bf16[96,256]{1,0:T(8,128)(2,1)S(1)}, u32[]{:S(2)}, u32[]{:S(2)}) collective-permute-start(bf16[96,256]{1,0:T(8,128)(2,1)S(1)} %get-tuple-element.32), channel_id=1, source_target_pairs={{0,6},{1,7},{2,4},{3,5},{4,2},{5,3},{6,0},{7,1},{8,14},{9,15},{10,... | collective-permute-start | bytes 147464 | tf_op jit(solution)/shard_map/ppermute | solution.py:21
  31.5 5.0 %collective-permute-start.13 = (bf16[96,256]{1,0:T(8,128)(2,1)S(1)}, bf16[96,256]{1,0:T(8,128)(2,1)S(1)}, u32[]{:S(2)}, u32[]{:S(2)}) collective-permute-start(bf16[96,256]{1,0:T(8,128)(2,1)S(1)} %get-tuple-element.25.after_ref), channel_id=1, source_target_pairs={{0,2},{1,3},{2,0},{3,1},{4,6},{5,7},{6,4},{7,5},{8,10},{9,11},{10,... | collective-permute-start | bytes 147464 | tf_op jit(solution)/shard_map/ppermute | solution.py:21
  32.9 7.4 %collective-permute-start.10 = (bf16[96,256]{1,0:T(8,128)(2,1)S(1)}, bf16[96,256]{1,0:T(8,128)(2,1)S(1)}, u32[]{:S(2)}, u32[]{:S(2)}) collective-permute-start(bf16[96,256]{1,0:T(8,128)(2,1)S(1)} %get-tuple-element.27), channel_id=1, source_target_pairs={{0,2},{1,3},{2,0},{3,1},{4,6},{5,7},{6,4},{7,5},{8,10},{9,11},{10,... | collective-permute-start | bytes 147464 | tf_op jit(solution)/shard_map/ppermute | solution.py:21
  33.6 6.8 %collective-permute-start.11 = (bf16[96,256]{1,0:T(8,128)(2,1)S(1)}, bf16[96,256]{1,0:T(8,128)(2,1)S(1)}, u32[]{:S(2)}, u32[]{:S(2)}) collective-permute-start(bf16[96,256]{1,0:T(8,128)(2,1)S(1)} %get-tuple-element.28), channel_id=1, source_target_pairs={{0,4},{1,5},{2,6},{3,7},{4,0},{5,1},{6,2},{7,3},{8,12},{9,13},{10,... | collective-permute-start | bytes 147464 | tf_op jit(solution)/shard_map/ppermute | solution.py:21
  35.2 5.2 %collective-permute-start.12 = (bf16[96,256]{1,0:T(8,128)(2,1)S(1)}, bf16[96,256]{1,0:T(8,128)(2,1)S(1)}, u32[]{:S(2)}, u32[]{:S(2)}) collective-permute-start(bf16[96,256]{1,0:T(8,128)(2,1)S(1)} %get-tuple-element.29), channel_id=1, source_target_pairs={{0,6},{1,7},{2,4},{3,5},{4,2},{5,3},{6,0},{7,1},{8,14},{9,15},{10,... | collective-permute-start | bytes 147464 | tf_op jit(solution)/shard_map/ppermute | solution.py:21
  36.5 5.1 %collective-permute-start.16 = (bf16[96,256]{1,0:T(8,128)(2,1)S(1)}, bf16[96,256]{1,0:T(8,128)(2,1)S(1)}, u32[]{:S(2)}, u32[]{:S(2)}) collective-permute-start(bf16[96,256]{1,0:T(8,128)(2,1)S(1)} %outward.3), channel_id=1, source_target_pairs={{0,8},{1,9},{2,10},{3,11},{4,12},{5,13},{6,14},{7,15},{8,0},{9,1},... | collective-permute-start | bytes 147464 | tf_op jit(solution)/shard_map/ppermute | solution.py:21

commit v7 on v6

--- a/solution.py
+++ b/solution.py
@@ -225,31 +225,27 @@
                     score_ref[:, at] += term
 
 
-def readers(first_ref, rest_ref):
-    height = first_ref.shape[0]
-
+def readers(rest_ref, height):
     def read(i, rows):
-        if i == 0:
-            return first_ref[rows]
-        return rest_ref[(i - 1) * height + rows.start : (i - 1) * height + rows.stop]
-
-    count = 1 + rest_ref.shape[0] // height
-    return [functools.partial(read, i) for i in range(count)]
-
-
-def score_kernel(first_ref, rest_ref, top_ref, low_ref, score_ref, window_ref):
-    add_scores(readers(first_ref, rest_ref), (top_ref, low_ref), 0, score_ref, window_ref)
-
-
-def score(first, rest, masked):
+        return rest_ref[i * height + rows.start : i * height + rows.stop]
+
+    return [functools.partial(read, i) for i in range(rest_ref.shape[0] // height)]
+
+
+def score_kernel(rest_ref, top_ref, low_ref, score_ref, window_ref):
+    height = 2 * window_ref.shape[0] - PAIR
+    add_scores(readers(rest_ref, height), (top_ref, low_ref), 0, score_ref, window_ref)
+
+
+def score(rest, masked):
     devices, _, own = masked[0].shape
     depth = sum(part.shape[1] for part in masked)
-    width = first.shape[0] // 2 - RIM + PAIR
+    width = rest.shape[0] // (devices // 4) // 2 - RIM + PAIR
     return call(
         score_kernel,
         [((width, depth), F32)],
-        [first, rest, *masked],
-        "vvvv",
+        [rest, *masked],
+        "vvv",
         [pltpu.VMEM((width, own), BF16)],
         flops=width * depth * own * devices,
         moved=depth * own * devices,
@@ -277,13 +273,14 @@
 
 
 def adjoint_kernel(
-    lags, first_ref, rest_ref, top_ref, low_ref, begun_ref, select_ref, line_ref,
+    lags, rest_ref, top_ref, low_ref, begun_ref, select_ref, line_ref,
     mism_ref, spread_ref, other_ref, rims_ref, score_ref, window_ref,
 ):
     width, depth = score_ref.shape
     hours = other_ref.shape[1]
     score_ref[...] = begun_ref[...]
-    add_scores(readers(first_ref, rest_ref), (top_ref, low_ref), 1, score_ref, window_ref)
+    height = 2 * window_ref.shape[0] - PAIR
+    add_scores(readers(rest_ref, height), (top_ref, low_ref), 1, score_ref, window_ref)
     line = jnp.sum(score_ref[...] * select_ref[...], axis=0, keepdims=True)
     model = group_sums(jnp.broadcast_to(line, (8, depth)), lags)
     mism = line_ref[:8] * (model - line_ref[8:])
@@ -302,7 +299,7 @@
         rims_ref[i * PAIR : (i + 1) * PAIR] = jnp.concatenate(edges, axis=0).astype(BF16)
 
 
-def adjoint(first, rest, masked, begun, select, lines, lags):
+def adjoint(rest, masked, begun, select, lines, lags):
     devices, _, own = masked[0].shape
     depth = sum(part.shape[1] for part in masked)
     width = begun.shape[0]
@@ -314,8 +311,8 @@
             ((devices // 2, width - PAIR, own), BF16),
             ((devices // 4 * PAIR, own), BF16),
         ],
-        [first, rest, *masked, begun, select, lines],
-        "v" * 7,
+        [rest, *masked, begun, select, lines],
+        "v" * 6,
         [pltpu.VMEM((width, depth), F32), pltpu.VMEM((width, own), BF16)],
         flops=2 * width * depth * own * devices,
         moved=depth * own * devices,
@@ -461,7 +458,6 @@
     top = prepare(foot, masks, block, devices, 0, head)
     first = window(block, far_block, top)
     parts = [swap(first, k) for k in near]
-    other_first = swap(first, 1)
     bottom = prepare(foot, masks, first, devices, head, blocks - head)
     select, lines = choose(
         rec_hour.reshape(1, rows),
@@ -472,11 +468,11 @@
         lags,
         hours,
     )
-    rest = pack(parts, lines, bottom)
+    rest = pack([first, *parts], lines, bottom)
     masked = (top, bottom)
-    begun = score(first, rest, masked)
+    begun = score(rest, masked)
     mism, spread, other, other_rims = adjoint(
-        other_first, swap(rest, 1), masked, begun, select, lines, lags
+        swap(rest, 1), masked, begun, select, lines, lags
     )
 
     came_rims = swap(other_rims, 1)

time: 42.5 us -> 42.4 us (level)
  starting transfers between devices: 22.1 us -> 21.6 us
  waiting for transfers between devices: 5.49 us -> 5.95 us
    ppermute x15 -> x14, starting transfers between devices: 17.6 us -> 17.1 us  [swap(): return lax.ppermute(block, 'rcpt', [(i, i ^ bit) for i in devices])]
    ppermute x15 -> x14, waiting for transfers between devices: 3.03 us -> 3.48 us  [swap(): return lax.ppermute(block, 'rcpt', [(i, i ^ bit) for i in devices])]
  transfers between devices with their start and end apart: 17 -> 16, of which waited for: 8 -> 9; matrix products, arithmetic and copies ran while one was open for 0% -> 0% of each run, Pallas kernels for 20% -> 20%
where the time goes in v7:
time: 42.4 us; the launch traced here: 42.2 us
  starting transfers between devices  21.6 us (51%)
  Pallas kernels  10.9 us (26%)
  waiting for transfers between devices  5.95 us (14%)
  other arithmetic  1.55 us (4%)
  between operations  1.45 us (3%)
  local copies, waits for them, and re-layouts  0.78 us (2%)
    ppermute x14, starting transfers between devices, swap(): return lax.ppermute(block, 'rcpt', [(i, i ^ bit) for i in devices])  17.1 us
    pallas_call x19, Pallas kernels, call(): pl.pallas_call(kernel, in_specs=[pl.BlockSpec(memory_space=where[c]) for...  10.9 us
    ppermute x2, starting transfers between devices, turn(): lax.ppermute(block, 'hour', [(i, (i + distance) % size) for i in range(si...  4.49 us
    ppermute x14, waiting for transfers between devices, swap(): return lax.ppermute(block, 'rcpt', [(i, i ^ bit) for i in devices])  3.48 us
    ppermute x2, waiting for transfers between devices, turn(): lax.ppermute(block, 'hour', [(i, (i + distance) % size) for i in range(si...  2.46 us
    convert_element_type x1, other arithmetic, per_device(): low = flux.astype(BF16)  0.9 us
  transfers between devices with their start and end apart: 16, of which 9 were waited for; matrix products, arithmetic and copies ran while one was open for 0% of the time, Pallas kernels for 20%

profile of v7, /device:TPU:0, one launch (start us, length us, event | category | flops | bytes accessed | tf_op | source)
XLA Modules:
  0.0 42.2 jit_solution(1028565812389987840)
XLA Ops:
  0.6 0.9 %convert_element_type.6.low_ref = bf16[96,256]{1,0:T(8,128)(2,1)S(1)} convert(f32[96,256]{1,0:T(8,128)} %param.7) | non-fusion elementwise | flops 24576 | bytes 147456 | tf_op jit(solution)/shard_map/convert_element_type | solution.py:450
  1.5 3.0 %collective-permute-start = (bf16[8,256]{1,0:T(8,128)(2,1)S(1)}, bf16[8,256]{1,0:T(8,128)(2,1)S(1)}, u32[]{:S(2)}, u32[]{:S(2)}) collective-permute-start(bf16[8,256]{1,0:T(8,128)(2,1)S(1)} %edge.1.after_ref), channel_id=1, source_target_pairs={{0,16},{16,0},{1,17},{17,1},{2,18},{18,2},{3,19},{19,3},{4,20},{20... | collective-permute-start | bytes 12296 | tf_op jit(solution)/shard_map/ppermute | solution.py:26
  4.5 0.8 %copy-done = s32[8,8,32]{2,1,0:T(8,128)S(1)} copy-done((s32[8,8,32]{2,1,0:T(8,128)S(1)}, s32[8,8,32]{2,1,0:T(8,128)}, u32[]{:S(2)}) %copy-start) | copy-done | bytes 8216
  6.1 3.2 %collective-permute-start.1 = (bf16[112,256]{1,0:T(8,128)(2,1)S(1)}, bf16[112,256]{1,0:T(8,128)(2,1)S(1)}, u32[]{:S(2)}, u32[]{:S(2)}) collective-permute-start(bf16[112,256]{1,0:T(8,128)(2,1)S(1)} %block.1.after_ref.near_ref), channel_id=1, source_target_pairs={{0,8},{1,9},{2,10},{3,11},{4,12},{5,13},{6,14},{7,15},{8,0},{9,1},... | collective-permute-start | bytes 172040 | tf_op jit(solution)/shard_map/ppermute | solution.py:21
  9.3 2.0 %prepare.2.after_ref.top_ref = bf16[16,384,256]{2,1,0:T(8,128)(2,1)S(1)} custom-call(bf16[1024,4096]{1,0:T(8,128)(2,1)} %bitcast.8, f32[8,16,32]{2,1,0:T(8,128)S(1)} %masks.1.after_ref.mask_ref, bf16[112,256]{1,0:T(8,128)(2,1)S(1)} %block.1.after_ref.near_ref), custom_call_target="tpu_custom_call" | custom-call | flops 10000000000 | bytes 6291456 | tf_op jit(solution)/shard_map/prepare/pallas_call | solution.py:40
  11.3 0.2 collective-permute-done.1.far_ref
  11.5 2.9 %collective-permute-start.4 = (bf16[208,256]{1,0:T(8,128)(2,1)S(1)}, bf16[208,256]{1,0:T(8,128)(2,1)S(1)}, u32[]{:S(2)}, u32[]{:S(2)}) collective-permute-start(bf16[208,256]{1,0:T(8,128)(2,1)S(1)} %window.1.after_ref.refs_0_), channel_id=1, source_target_pairs={{0,6},{1,7},{2,4},{3,5},{4,2},{5,3},{6,0},{7,1},{8,14},{9,15},{10,... | collective-permute-start | bytes 319496 | tf_op jit(solution)/shard_map/ppermute | solution.py:21
  14.4 0.4 %collective-permute-start.3 = (bf16[208,256]{1,0:T(8,128)(2,1)S(1)}, bf16[208,256]{1,0:T(8,128)(2,1)S(1)}, u32[]{:S(2)}, u32[]{:S(2)}) collective-permute-start(bf16[208,256]{1,0:T(8,128)(2,1)S(1)} %window.1.after_ref.refs_0_), channel_id=1, source_target_pairs={{0,4},{1,5},{2,6},{3,7},{4,0},{5,1},{6,2},{7,3},{8,12},{9,13},{10,... | collective-permute-start | bytes 319496 | tf_op jit(solution)/shard_map/ppermute | solution.py:21
  14.9 0.2 collective-permute-start.2
  15.1 2.6 %prepare.3.refs_5_.low_ref = bf16[16,640,256]{2,1,0:T(8,128)(2,1)S(1)} custom-call(bf16[1024,4096]{1,0:T(8,128)(2,1)} %bitcast.9, f32[8,16,32]{2,1,0:T(8,128)S(1)} %masks.1.after_ref.mask_ref, bf16[208,256]{1,0:T(8,128)(2,1)S(1)} %window.1.after_ref.refs_0_), custom_call_target="tpu_custom_call" | custom-call | flops 10000000000 | bytes 10485760 | tf_op jit(solution)/shard_map/prepare/pallas_call | solution.py:40
  17.7 0.5 %choose.1 = (f32[112,1024]{1,0:T(8,128)S(1)}, f32[16,1024]{1,0:T(8,128)S(1)}) custom-call(s32[1,128]{1,0:T(1,128)S(1)} %bitcast.5, f32[1,128]{1,0:T(1,128)S(1)} %bitcast.6, f32[1,128]{1,0:T(1,128)S(1)} %bitcast.7, s32[1]{0:T(128)S(6)} %copy.9.count_ref, bf16[208,256]{1,0:T(8,128)(2,1)S(1)} %window.1.after_ref.refs_0_), custom_call_target="tpu_custom_call" | custom-call | flops 10000000000 | tf_op jit(solution)/shard_map/choose/pallas_call | solution.py:40
  18.3 0.9 %collective-permute-done.3.refs_2_ = bf16[208,256]{1,0:T(8,128)(2,1)S(1)} collective-permute-done((bf16[208,256]{1,0:T(8,128)(2,1)S(1)}, bf16[208,256]{1,0:T(8,128)(2,1)S(1)}, u32[]{:S(2)}, u32[]{:S(2)}) %collective-permute-start.3) | collective-permute-done | bytes 106528 | tf_op jit(solution)/shard_map/ppermute | solution.py:21
  19.2 0.4 %collective-permute-done.2.refs_1_ = bf16[208,256]{1,0:T(8,128)(2,1)S(1)} collective-permute-done((bf16[208,256]{1,0:T(8,128)(2,1)S(1)}, bf16[208,256]{1,0:T(8,128)(2,1)S(1)}, u32[]{:S(2)}, u32[]{:S(2)}) %collective-permute-start.2) | collective-permute-done | bytes 106528 | tf_op jit(solution)/shard_map/ppermute | solution.py:21
  19.7 1.3 %score.1.begun_ref = f32[112,1024]{1,0:T(8,128)S(1)} custom-call(bf16[832,256]{1,0:T(8,128)(2,1)S(1)} %pack.1.rest_ref, bf16[16,384,256]{2,1,0:T(8,128)(2,1)S(1)} %prepare.2.after_ref.top_ref, bf16[16,640,256]{2,1,0:T(8,128)(2,1)S(1)} %prepare.3.refs_5_.low_ref), custom_call_target="tpu_custom_call" | custom-call | flops 469762048 | bytes 4194304 | tf_op jit(solution)/shard_map/score/pallas_call | solution.py:40
  21.0 0.5 %collective-permute-done.5.rest_ref = bf16[832,256]{1,0:T(8,128)(2,1)S(1)} collective-permute-done((bf16[832,256]{1,0:T(8,128)(2,1)S(1)}, bf16[832,256]{1,0:T(8,128)(2,1)S(1)}, u32[]{:S(2)}, u32[]{:S(2)}) %collective-permute-start.5) | collective-permute-done | bytes 426016 | tf_op jit(solution)/shard_map/ppermute | solution.py:21
  21.5 2.3 %adjoint.1 = (f32[8,1024]{1,0:T(8,128)S(1)}, bf16[112,1024]{1,0:T(8,128)(2,1)S(1)}, bf16[8,96,256]{2,1,0:T(8,128)(2,1)S(1)}, bf16[64,256]{1,0:T(8,128)(2,1)S(1)}) custom-call(bf16[832,256]{1,0:T(8,128)(2,1)S(1)} %collective-permute-done.5.rest_ref, bf16[16,384,256]{2,1,0:T(8,128)(2,1)S(1)} %prepare.2.after_ref.top_ref, ...), custom_call_target="tpu_custom_call" | custom-call | flops 939524096 | bytes 4194304 | tf_op jit(solution)/shard_map/adjoint/pallas_call | solution.py:40
  23.8 0.2 collective-permute-start.6
  24.0 0.8 %mine.1 = (f32[8,96,256]{2,1,0:T(8,128)S(1)}, f32[64,256]{1,0:T(8,128)S(1)}) custom-call(bf16[112,1024]{1,0:T(8,128)(2,1)S(1)} %get-tuple-element.20.spread_ref, bf16[16,384,256]{2,1,0:T(8,128)(2,1)S(1)} %prepare.2.after_ref.top_ref, bf16[16,640,256]{2,1,0:T(8,128)(2,1)S(1)} %prepare.3.refs_5_.low_ref), custom_call_target="tpu_custom_call" | custom-call | flops 469762048 | bytes 4194304 | tf_op jit(solution)/shard_map/mine/pallas_call | solution.py:40
  24.9 0.2 collective-permute-done.6.came_ref
  25.1 0.2 collective-permute-start.7
  25.4 1.5 %collective-permute-start.8 = (bf16[64,256]{1,0:T(8,128)(2,1)S(1)}, bf16[64,256]{1,0:T(8,128)(2,1)S(1)}, u32[]{:S(2)}, u32[]{:S(2)}) collective-permute-start(bf16[64,256]{1,0:T(8,128)(2,1)S(1)} %rims.1.after_ref), channel_id=1, source_target_pairs={{0,16},{16,0},{1,17},{17,1},{2,18},{18,2},{3,19},{19,3},{4,20},{20... | collective-permute-start | bytes 98312 | tf_op jit(solution)/shard_map/ppermute | solution.py:26
  27.0 2.3 %collective-permute-done.8.rims_ref = bf16[64,256]{1,0:T(8,128)(2,1)S(1)} collective-permute-done((bf16[64,256]{1,0:T(8,128)(2,1)S(1)}, bf16[64,256]{1,0:T(8,128)(2,1)S(1)}, u32[]{:S(2)}, u32[]{:S(2)}) %collective-permute-start.8) | collective-permute-done | bytes 32800 | tf_op jit(solution)/shard_map/ppermute | solution.py:26
  29.3 1.6 %collective-permute-start.13 = (bf16[96,256]{1,0:T(8,128)(2,1)S(1)}, bf16[96,256]{1,0:T(8,128)(2,1)S(1)}, u32[]{:S(2)}, u32[]{:S(2)}) collective-permute-start(bf16[96,256]{1,0:T(8,128)(2,1)S(1)} %get-tuple-element.31), channel_id=1, source_target_pairs={{0,4},{1,5},{2,6},{3,7},{4,0},{5,1},{6,2},{7,3},{8,12},{9,13},{10,... | collective-permute-start | bytes 147464 | tf_op jit(solution)/shard_map/ppermute | solution.py:21
  31.0 0.5 %collective-permute-start.14 = (bf16[96,256]{1,0:T(8,128)(2,1)S(1)}, bf16[96,256]{1,0:T(8,128)(2,1)S(1)}, u32[]{:S(2)}, u32[]{:S(2)}) collective-permute-start(bf16[96,256]{1,0:T(8,128)(2,1)S(1)} %get-tuple-element.32), channel_id=1, source_target_pairs={{0,6},{1,7},{2,4},{3,5},{4,2},{5,3},{6,0},{7,1},{8,14},{9,15},{10,... | collective-permute-start | bytes 147464 | tf_op jit(solution)/shard_map/ppermute | solution.py:21
  31.4 1.4 %collective-permute-start.12 = (bf16[96,256]{1,0:T(8,128)(2,1)S(1)}, bf16[96,256]{1,0:T(8,128)(2,1)S(1)}, u32[]{:S(2)}, u32[]{:S(2)}) collective-permute-start(bf16[96,256]{1,0:T(8,128)(2,1)S(1)} %get-tuple-element.25.after_ref), channel_id=1, source_target_pairs={{0,2},{1,3},{2,0},{3,1},{4,6},{5,7},{6,4},{7,5},{8,10},{9,11},{10,... | collective-permute-start | bytes 147464 | tf_op jit(solution)/shard_map/ppermute | solution.py:21
  32.9 0.6 %collective-permute-start.9 = (bf16[96,256]{1,0:T(8,128)(2,1)S(1)}, bf16[96,256]{1,0:T(8,128)(2,1)S(1)}, u32[]{:S(2)}, u32[]{:S(2)}) collective-permute-start(bf16[96,256]{1,0:T(8,128)(2,1)S(1)} %get-tuple-element.27), channel_id=1, source_target_pairs={{0,2},{1,3},{2,0},{3,1},{4,6},{5,7},{6,4},{7,5},{8,10},{9,11},{10,... | collective-permute-start | bytes 147464 | tf_op jit(solution)/shard_map/ppermute | solution.py:21
  33.5 1.6 %collective-permute-start.10 = (bf16[96,256]{1,0:T(8,128)(2,1)S(1)}, bf16[96,256]{1,0:T(8,128)(2,1)S(1)}, u32[]{:S(2)}, u32[]{:S(2)}) collective-permute-start(bf16[96,256]{1,0:T(8,128)(2,1)S(1)} %get-tuple-element.28), channel_id=1, source_target_pairs={{0,4},{1,5},{2,6},{3,7},{4,0},{5,1},{6,2},{7,3},{8,12},{9,13},{10,... | collective-permute-start | bytes 147464 | tf_op jit(solution)/shard_map/ppermute | solution.py:21
  35.1 1.3 %collective-permute-start.11 = (bf16[96,256]{1,0:T(8,128)(2,1)S(1)}, bf16[96,256]{1,0:T(8,128)(2,1)S(1)}, u32[]{:S(2)}, u32[]{:S(2)}) collective-permute-start(bf16[96,256]{1,0:T(8,128)(2,1)S(1)} %get-tuple-element.29), channel_id=1, source_target_pairs={{0,6},{1,7},{2,4},{3,5},{4,2},{5,3},{6,0},{7,1},{8,14},{9,15},{10,... | collective-permute-start | bytes 147464 | tf_op jit(solution)/shard_map/ppermute | solution.py:21
  36.5 2.8 %collective-permute-start.15 = (bf16[96,256]{1,0:T(8,128)(2,1)S(1)}, bf16[96,256]{1,0:T(8,128)(2,1)S(1)}, u32[]{:S(2)}, u32[]{:S(2)}) collective-permute-start(bf16[96,256]{1,0:T(8,128)(2,1)S(1)} %outward.3), channel_id=1, source_target_pairs={{0,8},{1,9},{2,10},{3,11},{4,12},{5,13},{6,14},{7,15},{8,0},{9,1},... | collective-permute-start | bytes 147464 | tf_op jit(solution)/shard_map/ppermute | solution.py:21
  39.3 1.0 %narrow.1 = f32[1,128]{1,0:T(1,128)} custom-call(f32[8,1024]{1,0:T(8,128)S(1)} %get-tuple-element.33.mism_ref, f32[96,256]{1,0:T(8,128)S(1)} %get-tuple-element.30.first_ref.after_ref), custom_call_target="tpu_custom_call" | custom-call | flops 10000000000 | tf_op jit(solution)/shard_map/narrow/pallas_call | solution.py:40
  40.4 1.2 %collective-permute-done.15 = bf16[96,256]{1,0:T(8,128)(2,1)S(1)} collective-permute-done((bf16[96,256]{1,0:T(8,128)(2,1)S(1)}, bf16[96,256]{1,0:T(8,128)(2,1)S(1)}, u32[]{:S(2)}, u32[]{:S(2)}) %collective-permute-start.15) | collective-permute-done | bytes 49184 | tf_op jit(solution)/shard_map/ppermute | solution.py:21
  41.6 0.7 %convert_add_fusion = f32[96,256]{1,0:T(8,128)} fusion(f32[96,256]{1,0:T(8,128)S(1)} %outward.2, bf16[96,256]{1,0:T(8,128)(2,1)S(1)} %collective-permute-done.15), kind=kLoop, calls=%fused_computation | loop fusion | flops 49152 | bytes 245760 | tf_op jit(solution)/shard_map/add | solution.py:491
  (29 shorter events, 0.6 us)
Async XLA Ops:
  1.5 4.6 %collective-permute-start = (bf16[8,256]{1,0:T(8,128)(2,1)S(1)}, bf16[8,256]{1,0:T(8,128)(2,1)S(1)}, u32[]{:S(2)}, u32[]{:S(2)}) collective-permute-start(bf16[8,256]{1,0:T(8,128)(2,1)S(1)} %edge.1.after_ref), channel_id=1, source_target_pairs={{0,16},{16,0},{1,17},{17,1},{2,18},{18,2},{3,19},{19,3},{4,20},{20... | collective-permute-start | bytes 12296 | tf_op jit(solution)/shard_map/ppermute | solution.py:26
  4.5 0.8 %copy-start = (s32[8,8,32]{2,1,0:T(8,128)S(1)}, s32[8,8,32]{2,1,0:T(8,128)}, u32[]{:S(2)}) copy-start(s32[8,8,32]{2,1,0:T(8,128)} %mask_ref.1) | copy-start | bytes 24580
  6.1 5.3 %collective-permute-start.1 = (bf16[112,256]{1,0:T(8,128)(2,1)S(1)}, bf16[112,256]{1,0:T(8,128)(2,1)S(1)}, u32[]{:S(2)}, u32[]{:S(2)}) collective-permute-start(bf16[112,256]{1,0:T(8,128)(2,1)S(1)} %block.1.after_ref.near_ref), channel_id=1, source_target_pairs={{0,8},{1,9},{2,10},{3,11},{4,12},{5,13},{6,14},{7,15},{8,0},{9,1},... | collective-permute-start | bytes 172040 | tf_op jit(solution)/shard_map/ppermute | solution.py:21
  11.5 6.2 %copy-start.1 = (s32[128]{0:T(128)S(1)}, s32[128]{0:T(128)}, u32[]{:S(2)}) copy-start(s32[128]{0:T(128)} %param.10) | copy-start | bytes 1540
  11.5 6.2 %copy-start.2 = (f32[128]{0:T(128)S(1)}, f32[128]{0:T(128)}, u32[]{:S(2)}) copy-start(f32[128]{0:T(128)} %param.11) | copy-start | bytes 1540
  11.5 6.2 %copy-start.3 = (f32[128]{0:T(128)S(1)}, f32[128]{0:T(128)}, u32[]{:S(2)}) copy-start(f32[128]{0:T(128)} %param.12) | copy-start | bytes 1540
  11.5 6.7 %collective-permute-start.4 = (bf16[208,256]{1,0:T(8,128)(2,1)S(1)}, bf16[208,256]{1,0:T(8,128)(2,1)S(1)}, u32[]{:S(2)}, u32[]{:S(2)}) collective-permute-start(bf16[208,256]{1,0:T(8,128)(2,1)S(1)} %window.1.after_ref.refs_0_), channel_id=1, source_target_pairs={{0,6},{1,7},{2,4},{3,5},{4,2},{5,3},{6,0},{7,1},{8,14},{9,15},{10,... | collective-permute-start | bytes 319496 | tf_op jit(solution)/shard_map/ppermute | solution.py:21
  14.4 4.7 %collective-permute-start.3 = (bf16[208,256]{1,0:T(8,128)(2,1)S(1)}, bf16[208,256]{1,0:T(8,128)(2,1)S(1)}, u32[]{:S(2)}, u32[]{:S(2)}) collective-permute-start(bf16[208,256]{1,0:T(8,128)(2,1)S(1)} %window.1.after_ref.refs_0_), channel_id=1, source_target_pairs={{0,4},{1,5},{2,6},{3,7},{4,0},{5,1},{6,2},{7,3},{8,12},{9,13},{10,... | collective-permute-start | bytes 319496 | tf_op jit(solution)/shard_map/ppermute | solution.py:21
  14.9 4.7 %collective-permute-start.2 = (bf16[208,256]{1,0:T(8,128)(2,1)S(1)}, bf16[208,256]{1,0:T(8,128)(2,1)S(1)}, u32[]{:S(2)}, u32[]{:S(2)}) collective-permute-start(bf16[208,256]{1,0:T(8,128)(2,1)S(1)} %window.1.after_ref.refs_0_), channel_id=1, source_target_pairs={{0,2},{1,3},{2,0},{3,1},{4,6},{5,7},{6,4},{7,5},{8,10},{9,11},{10,... | collective-permute-start | bytes 319496 | tf_op jit(solution)/shard_map/ppermute | solution.py:21
  19.6 1.8 %collective-permute-start.5 = (bf16[832,256]{1,0:T(8,128)(2,1)S(1)}, bf16[832,256]{1,0:T(8,128)(2,1)S(1)}, u32[]{:S(2)}, u32[]{:S(2)}) collective-permute-start(bf16[832,256]{1,0:T(8,128)(2,1)S(1)} %pack.1.rest_ref), channel_id=1, source_target_pairs={{0,1},{1,0},{2,3},{3,2},{4,5},{5,4},{6,7},{7,6},{8,9},{9,8},{10,11... | collective-permute-start | bytes 1277960 | tf_op jit(solution)/shard_map/ppermute | solution.py:21
  23.8 1.3 %collective-permute-start.6 = (bf16[64,256]{1,0:T(8,128)(2,1)S(1)}, bf16[64,256]{1,0:T(8,128)(2,1)S(1)}, u32[]{:S(2)}, u32[]{:S(2)}) collective-permute-start(bf16[64,256]{1,0:T(8,128)(2,1)S(1)} %get-tuple-element.24), channel_id=1, source_target_pairs={{0,1},{1,0},{2,3},{3,2},{4,5},{5,4},{6,7},{7,6},{8,9},{9,8},{10,11... | collective-permute-start | bytes 98312 | tf_op jit(solution)/shard_map/ppermute | solution.py:21
  25.1 1.8 %collective-permute-start.7 = (bf16[8,96,256]{2,1,0:T(8,128)(2,1)S(1)}, bf16[8,96,256]{2,1,0:T(8,128)(2,1)S(1)}, u32[]{:S(2)}, u32[]{:S(2)}) collective-permute-start(bf16[8,96,256]{2,1,0:T(8,128)(2,1)S(1)} %gate.1), channel_id=1, source_target_pairs={{0,1},{1,0},{2,3},{3,2},{4,5},{5,4},{6,7},{7,6},{8,9},{9,8},{10,11... | collective-permute-start | bytes 1179656 | tf_op jit(solution)/shard_map/ppermute | solution.py:21
  25.4 3.9 %collective-permute-start.8 = (bf16[64,256]{1,0:T(8,128)(2,1)S(1)}, bf16[64,256]{1,0:T(8,128)(2,1)S(1)}, u32[]{:S(2)}, u32[]{:S(2)}) collective-permute-start(bf16[64,256]{1,0:T(8,128)(2,1)S(1)} %rims.1.after_ref), channel_id=1, source_target_pairs={{0,16},{16,0},{1,17},{17,1},{2,18},{18,2},{3,19},{19,3},{4,20},{20... | collective-permute-start | bytes 98312 | tf_op jit(solution)/shard_map/ppermute | solution.py:26
  29.3 5.8 %collective-permute-start.13 = (bf16[96,256]{1,0:T(8,128)(2,1)S(1)}, bf16[96,256]{1,0:T(8,128)(2,1)S(1)}, u32[]{:S(2)}, u32[]{:S(2)}) collective-permute-start(bf16[96,256]{1,0:T(8,128)(2,1)S(1)} %get-tuple-element.31), channel_id=1, source_target_pairs={{0,4},{1,5},{2,6},{3,7},{4,0},{5,1},{6,2},{7,3},{8,12},{9,13},{10,... | collective-permute-start | bytes 147464 | tf_op jit(solution)/shard_map/ppermute | solution.py:21
  31.0 5.5 %collective-permute-start.14 = (bf16[96,256]{1,0:T(8,128)(2,1)S(1)}, bf16[96,256]{1,0:T(8,128)(2,1)S(1)}, u32[]{:S(2)}, u32[]{:S(2)}) collective-permute-start(bf16[96,256]{1,0:T(8,128)(2,1)S(1)} %get-tuple-element.32), channel_id=1, source_target_pairs={{0,6},{1,7},{2,4},{3,5},{4,2},{5,3},{6,0},{7,1},{8,14},{9,15},{10,... | collective-permute-start | bytes 147464 | tf_op jit(solution)/shard_map/ppermute | solution.py:21
  31.4 5.0 %collective-permute-start.12 = (bf16[96,256]{1,0:T(8,128)(2,1)S(1)}, bf16[96,256]{1,0:T(8,128)(2,1)S(1)}, u32[]{:S(2)}, u32[]{:S(2)}) collective-permute-start(bf16[96,256]{1,0:T(8,128)(2,1)S(1)} %get-tuple-element.25.after_ref), channel_id=1, source_target_pairs={{0,2},{1,3},{2,0},{3,1},{4,6},{5,7},{6,4},{7,5},{8,10},{9,11},{10,... | collective-permute-start | bytes 147464 | tf_op jit(solution)/shard_map/ppermute | solution.py:21
  32.9 7.4 %collective-permute-start.9 = (bf16[96,256]{1,0:T(8,128)(2,1)S(1)}, bf16[96,256]{1,0:T(8,128)(2,1)S(1)}, u32[]{:S(2)}, u32[]{:S(2)}) collective-permute-start(bf16[96,256]{1,0:T(8,128)(2,1)S(1)} %get-tuple-element.27), channel_id=1, source_target_pairs={{0,2},{1,3},{2,0},{3,1},{4,6},{5,7},{6,4},{7,5},{8,10},{9,11},{10,... | collective-permute-start | bytes 147464 | tf_op jit(solution)/shard_map/ppermute | solution.py:21
  33.5 6.8 %collective-permute-start.10 = (bf16[96,256]{1,0:T(8,128)(2,1)S(1)}, bf16[96,256]{1,0:T(8,128)(2,1)S(1)}, u32[]{:S(2)}, u32[]{:S(2)}) collective-permute-start(bf16[96,256]{1,0:T(8,128)(2,1)S(1)} %get-tuple-element.28), channel_id=1, source_target_pairs={{0,4},{1,5},{2,6},{3,7},{4,0},{5,1},{6,2},{7,3},{8,12},{9,13},{10,... | collective-permute-start | bytes 147464 | tf_op jit(solution)/shard_map/ppermute | solution.py:21
  35.1 5.2 %collective-permute-start.11 = (bf16[96,256]{1,0:T(8,128)(2,1)S(1)}, bf16[96,256]{1,0:T(8,128)(2,1)S(1)}, u32[]{:S(2)}, u32[]{:S(2)}) collective-permute-start(bf16[96,256]{1,0:T(8,128)(2,1)S(1)} %get-tuple-element.29), channel_id=1, source_target_pairs={{0,6},{1,7},{2,4},{3,5},{4,2},{5,3},{6,0},{7,1},{8,14},{9,15},{10,... | collective-permute-start | bytes 147464 | tf_op jit(solution)/shard_map/ppermute | solution.py:21
  36.5 5.1 %collective-permute-start.15 = (bf16[96,256]{1,0:T(8,128)(2,1)S(1)}, bf16[96,256]{1,0:T(8,128)(2,1)S(1)}, u32[]{:S(2)}, u32[]{:S(2)}) collective-permute-start(bf16[96,256]{1,0:T(8,128)(2,1)S(1)} %outward.3), channel_id=1, source_target_pairs={{0,8},{1,9},{2,10},{3,11},{4,12},{5,13},{6,14},{7,15},{8,0},{9,1},... | collective-permute-start | bytes 147464 | tf_op jit(solution)/shard_map/ppermute | solution.py:21

commit v8 on v7

--- a/solution.py
+++ b/solution.py
@@ -482,7 +482,10 @@
     back = turn(rims, -1)
     main = join(own_part, came, rims)
     far_sum, parts = shares(main, back, 1, rims)
-    passed = [swap(part, k) for part, k in zip(parts, near)]
+    middle = len(near) // 2
+    order = [middle, *range(middle), *range(middle + 1, len(near))]
+    passed = {i: swap(parts[i], near[i]) for i in order}
+    passed = [passed[i] for i in range(len(near))]
     near_sum, others = shares(main, back, 0, parts[0])
     arrived = [swap(part, k) for part, k in zip(others, near)]
     mism = narrow(mism, far_sum, rows)

time: 42.4 us -> 42.4 us (level)
  no operation moved by 1% of the time
where the time goes in v8:
time: 42.4 us; the launch traced here: 42.2 us
  starting transfers between devices  21.6 us (51%)
  Pallas kernels  10.9 us (26%)
  waiting for transfers between devices  5.95 us (14%)
  other arithmetic  1.55 us (4%)
  between operations  1.45 us (3%)
  local copies, waits for them, and re-layouts  0.78 us (2%)
    ppermute x14, starting transfers between devices, swap(): return lax.ppermute(block, 'rcpt', [(i, i ^ bit) for i in devices])  17.1 us
    pallas_call x19, Pallas kernels, call(): pl.pallas_call(kernel, in_specs=[pl.BlockSpec(memory_space=where[c]) for...  10.9 us
    ppermute x2, starting transfers between devices, turn(): lax.ppermute(block, 'hour', [(i, (i + distance) % size) for i in range(si...  4.49 us
    ppermute x14, waiting for transfers between devices, swap(): return lax.ppermute(block, 'rcpt', [(i, i ^ bit) for i in devices])  3.48 us
    ppermute x2, waiting for transfers between devices, turn(): lax.ppermute(block, 'hour', [(i, (i + distance) % size) for i in range(si...  2.46 us
    convert_element_type x1, other arithmetic, per_device(): low = flux.astype(BF16)  0.9 us
  transfers between devices with their start and end apart: 16, of which 9 were waited for; matrix products, arithmetic and copies ran while one was open for 0% of the time, Pallas kernels for 20%

profile of v8, /device:TPU:0, one launch (start us, length us, event | category | flops | bytes accessed | tf_op | source)
XLA Modules:
  0.0 42.2 jit_solution(1028565812389987840)
XLA Ops:
  0.6 0.9 %convert_element_type.6.low_ref = bf16[96,256]{1,0:T(8,128)(2,1)S(1)} convert(f32[96,256]{1,0:T(8,128)} %param.7) | non-fusion elementwise | flops 24576 | bytes 147456 | tf_op jit(solution)/shard_map/convert_element_type | solution.py:450
  1.5 3.0 %collective-permute-start = (bf16[8,256]{1,0:T(8,128)(2,1)S(1)}, bf16[8,256]{1,0:T(8,128)(2,1)S(1)}, u32[]{:S(2)}, u32[]{:S(2)}) collective-permute-start(bf16[8,256]{1,0:T(8,128)(2,1)S(1)} %edge.1.after_ref), channel_id=1, source_target_pairs={{0,16},{16,0},{1,17},{17,1},{2,18},{18,2},{3,19},{19,3},{4,20},{20... | collective-permute-start | bytes 12296 | tf_op jit(solution)/shard_map/ppermute | solution.py:26
  4.5 0.8 %copy-done = s32[8,8,32]{2,1,0:T(8,128)S(1)} copy-done((s32[8,8,32]{2,1,0:T(8,128)S(1)}, s32[8,8,32]{2,1,0:T(8,128)}, u32[]{:S(2)}) %copy-start) | copy-done | bytes 8216
  6.1 3.2 %collective-permute-start.1 = (bf16[112,256]{1,0:T(8,128)(2,1)S(1)}, bf16[112,256]{1,0:T(8,128)(2,1)S(1)}, u32[]{:S(2)}, u32[]{:S(2)}) collective-permute-start(bf16[112,256]{1,0:T(8,128)(2,1)S(1)} %block.1.after_ref.near_ref), channel_id=1, source_target_pairs={{0,8},{1,9},{2,10},{3,11},{4,12},{5,13},{6,14},{7,15},{8,0},{9,1},... | collective-permute-start | bytes 172040 | tf_op jit(solution)/shard_map/ppermute | solution.py:21
  9.3 2.0 %prepare.2.after_ref.top_ref = bf16[16,384,256]{2,1,0:T(8,128)(2,1)S(1)} custom-call(bf16[1024,4096]{1,0:T(8,128)(2,1)} %bitcast.8, f32[8,16,32]{2,1,0:T(8,128)S(1)} %masks.1.after_ref.mask_ref, bf16[112,256]{1,0:T(8,128)(2,1)S(1)} %block.1.after_ref.near_ref), custom_call_target="tpu_custom_call" | custom-call | flops 10000000000 | bytes 6291456 | tf_op jit(solution)/shard_map/prepare/pallas_call | solution.py:40
  11.3 0.2 collective-permute-done.1.far_ref
  11.5 2.9 %collective-permute-start.4 = (bf16[208,256]{1,0:T(8,128)(2,1)S(1)}, bf16[208,256]{1,0:T(8,128)(2,1)S(1)}, u32[]{:S(2)}, u32[]{:S(2)}) collective-permute-start(bf16[208,256]{1,0:T(8,128)(2,1)S(1)} %window.1.after_ref.refs_0_), channel_id=1, source_target_pairs={{0,6},{1,7},{2,4},{3,5},{4,2},{5,3},{6,0},{7,1},{8,14},{9,15},{10,... | collective-permute-start | bytes 319496 | tf_op jit(solution)/shard_map/ppermute | solution.py:21
  14.4 0.4 %collective-permute-start.3 = (bf16[208,256]{1,0:T(8,128)(2,1)S(1)}, bf16[208,256]{1,0:T(8,128)(2,1)S(1)}, u32[]{:S(2)}, u32[]{:S(2)}) collective-permute-start(bf16[208,256]{1,0:T(8,128)(2,1)S(1)} %window.1.after_ref.refs_0_), channel_id=1, source_target_pairs={{0,4},{1,5},{2,6},{3,7},{4,0},{5,1},{6,2},{7,3},{8,12},{9,13},{10,... | collective-permute-start | bytes 319496 | tf_op jit(solution)/shard_map/ppermute | solution.py:21
  14.9 0.2 collective-permute-start.2
  15.1 2.6 %prepare.3.refs_5_.low_ref = bf16[16,640,256]{2,1,0:T(8,128)(2,1)S(1)} custom-call(bf16[1024,4096]{1,0:T(8,128)(2,1)} %bitcast.9, f32[8,16,32]{2,1,0:T(8,128)S(1)} %masks.1.after_ref.mask_ref, bf16[208,256]{1,0:T(8,128)(2,1)S(1)} %window.1.after_ref.refs_0_), custom_call_target="tpu_custom_call" | custom-call | flops 10000000000 | bytes 10485760 | tf_op jit(solution)/shard_map/prepare/pallas_call | solution.py:40
  17.7 0.5 %choose.1 = (f32[112,1024]{1,0:T(8,128)S(1)}, f32[16,1024]{1,0:T(8,128)S(1)}) custom-call(s32[1,128]{1,0:T(1,128)S(1)} %bitcast.5, f32[1,128]{1,0:T(1,128)S(1)} %bitcast.6, f32[1,128]{1,0:T(1,128)S(1)} %bitcast.7, s32[1]{0:T(128)S(6)} %copy.9.count_ref, bf16[208,256]{1,0:T(8,128)(2,1)S(1)} %window.1.after_ref.refs_0_), custom_call_target="tpu_custom_call" | custom-call | flops 10000000000 | tf_op jit(solution)/shard_map/choose/pallas_call | solution.py:40
  18.3 0.9 %collective-permute-done.3.refs_2_ = bf16[208,256]{1,0:T(8,128)(2,1)S(1)} collective-permute-done((bf16[208,256]{1,0:T(8,128)(2,1)S(1)}, bf16[208,256]{1,0:T(8,128)(2,1)S(1)}, u32[]{:S(2)}, u32[]{:S(2)}) %collective-permute-start.3) | collective-permute-done | bytes 106528 | tf_op jit(solution)/shard_map/ppermute | solution.py:21
  19.2 0.4 %collective-permute-done.2.refs_1_ = bf16[208,256]{1,0:T(8,128)(2,1)S(1)} collective-permute-done((bf16[208,256]{1,0:T(8,128)(2,1)S(1)}, bf16[208,256]{1,0:T(8,128)(2,1)S(1)}, u32[]{:S(2)}, u32[]{:S(2)}) %collective-permute-start.2) | collective-permute-done | bytes 106528 | tf_op jit(solution)/shard_map/ppermute | solution.py:21
  19.7 1.3 %score.1.begun_ref = f32[112,1024]{1,0:T(8,128)S(1)} custom-call(bf16[832,256]{1,0:T(8,128)(2,1)S(1)} %pack.1.rest_ref, bf16[16,384,256]{2,1,0:T(8,128)(2,1)S(1)} %prepare.2.after_ref.top_ref, bf16[16,640,256]{2,1,0:T(8,128)(2,1)S(1)} %prepare.3.refs_5_.low_ref), custom_call_target="tpu_custom_call" | custom-call | flops 469762048 | bytes 4194304 | tf_op jit(solution)/shard_map/score/pallas_call | solution.py:40
  21.0 0.5 %collective-permute-done.5.rest_ref = bf16[832,256]{1,0:T(8,128)(2,1)S(1)} collective-permute-done((bf16[832,256]{1,0:T(8,128)(2,1)S(1)}, bf16[832,256]{1,0:T(8,128)(2,1)S(1)}, u32[]{:S(2)}, u32[]{:S(2)}) %collective-permute-start.5) | collective-permute-done | bytes 426016 | tf_op jit(solution)/shard_map/ppermute | solution.py:21
  21.5 2.3 %adjoint.1 = (f32[8,1024]{1,0:T(8,128)S(1)}, bf16[112,1024]{1,0:T(8,128)(2,1)S(1)}, bf16[8,96,256]{2,1,0:T(8,128)(2,1)S(1)}, bf16[64,256]{1,0:T(8,128)(2,1)S(1)}) custom-call(bf16[832,256]{1,0:T(8,128)(2,1)S(1)} %collective-permute-done.5.rest_ref, bf16[16,384,256]{2,1,0:T(8,128)(2,1)S(1)} %prepare.2.after_ref.top_ref, ...), custom_call_target="tpu_custom_call" | custom-call | flops 939524096 | bytes 4194304 | tf_op jit(solution)/shard_map/adjoint/pallas_call | solution.py:40
  23.8 0.2 collective-permute-start.6
  24.0 0.8 %mine.1 = (f32[8,96,256]{2,1,0:T(8,128)S(1)}, f32[64,256]{1,0:T(8,128)S(1)}) custom-call(bf16[112,1024]{1,0:T(8,128)(2,1)S(1)} %get-tuple-element.20.spread_ref, bf16[16,384,256]{2,1,0:T(8,128)(2,1)S(1)} %prepare.2.after_ref.top_ref, bf16[16,640,256]{2,1,0:T(8,128)(2,1)S(1)} %prepare.3.refs_5_.low_ref), custom_call_target="tpu_custom_call" | custom-call | flops 469762048 | bytes 4194304 | tf_op jit(solution)/shard_map/mine/pallas_call | solution.py:40
  24.9 0.2 collective-permute-done.6.came_ref
  25.1 0.2 collective-permute-start.7
  25.4 1.5 %collective-permute-start.8 = (bf16[64,256]{1,0:T(8,128)(2,1)S(1)}, bf16[64,256]{1,0:T(8,128)(2,1)S(1)}, u32[]{:S(2)}, u32[]{:S(2)}) collective-permute-start(bf16[64,256]{1,0:T(8,128)(2,1)S(1)} %rims.1.after_ref), channel_id=1, source_target_pairs={{0,16},{16,0},{1,17},{17,1},{2,18},{18,2},{3,19},{19,3},{4,20},{20... | collective-permute-start | bytes 98312 | tf_op jit(solution)/shard_map/ppermute | solution.py:26
  27.0 2.3 %collective-permute-done.8.rims_ref = bf16[64,256]{1,0:T(8,128)(2,1)S(1)} collective-permute-done((bf16[64,256]{1,0:T(8,128)(2,1)S(1)}, bf16[64,256]{1,0:T(8,128)(2,1)S(1)}, u32[]{:S(2)}, u32[]{:S(2)}) %collective-permute-start.8) | collective-permute-done | bytes 32800 | tf_op jit(solution)/shard_map/ppermute | solution.py:26
  29.3 1.6 %collective-permute-start.13 = (bf16[96,256]{1,0:T(8,128)(2,1)S(1)}, bf16[96,256]{1,0:T(8,128)(2,1)S(1)}, u32[]{:S(2)}, u32[]{:S(2)}) collective-permute-start(bf16[96,256]{1,0:T(8,128)(2,1)S(1)} %get-tuple-element.31), channel_id=1, source_target_pairs={{0,4},{1,5},{2,6},{3,7},{4,0},{5,1},{6,2},{7,3},{8,12},{9,13},{10,... | collective-permute-start | bytes 147464 | tf_op jit(solution)/shard_map/ppermute | solution.py:21
  31.0 0.5 %collective-permute-start.14 = (bf16[96,256]{1,0:T(8,128)(2,1)S(1)}, bf16[96,256]{1,0:T(8,128)(2,1)S(1)}, u32[]{:S(2)}, u32[]{:S(2)}) collective-permute-start(bf16[96,256]{1,0:T(8,128)(2,1)S(1)} %get-tuple-element.32), channel_id=1, source_target_pairs={{0,6},{1,7},{2,4},{3,5},{4,2},{5,3},{6,0},{7,1},{8,14},{9,15},{10,... | collective-permute-start | bytes 147464 | tf_op jit(solution)/shard_map/ppermute | solution.py:21
  31.4 1.4 %collective-permute-start.12 = (bf16[96,256]{1,0:T(8,128)(2,1)S(1)}, bf16[96,256]{1,0:T(8,128)(2,1)S(1)}, u32[]{:S(2)}, u32[]{:S(2)}) collective-permute-start(bf16[96,256]{1,0:T(8,128)(2,1)S(1)} %get-tuple-element.25.after_ref), channel_id=1, source_target_pairs={{0,2},{1,3},{2,0},{3,1},{4,6},{5,7},{6,4},{7,5},{8,10},{9,11},{10,... | collective-permute-start | bytes 147464 | tf_op jit(solution)/shard_map/ppermute | solution.py:21
  32.9 0.6 %collective-permute-start.9 = (bf16[96,256]{1,0:T(8,128)(2,1)S(1)}, bf16[96,256]{1,0:T(8,128)(2,1)S(1)}, u32[]{:S(2)}, u32[]{:S(2)}) collective-permute-start(bf16[96,256]{1,0:T(8,128)(2,1)S(1)} %get-tuple-element.27), channel_id=1, source_target_pairs={{0,2},{1,3},{2,0},{3,1},{4,6},{5,7},{6,4},{7,5},{8,10},{9,11},{10,... | collective-permute-start | bytes 147464 | tf_op jit(solution)/shard_map/ppermute | solution.py:21
  33.5 1.6 %collective-permute-start.10 = (bf16[96,256]{1,0:T(8,128)(2,1)S(1)}, bf16[96,256]{1,0:T(8,128)(2,1)S(1)}, u32[]{:S(2)}, u32[]{:S(2)}) collective-permute-start(bf16[96,256]{1,0:T(8,128)(2,1)S(1)} %get-tuple-element.28), channel_id=1, source_target_pairs={{0,4},{1,5},{2,6},{3,7},{4,0},{5,1},{6,2},{7,3},{8,12},{9,13},{10,... | collective-permute-start | bytes 147464 | tf_op jit(solution)/shard_map/ppermute | solution.py:21
  35.1 1.3 %collective-permute-start.11 = (bf16[96,256]{1,0:T(8,128)(2,1)S(1)}, bf16[96,256]{1,0:T(8,128)(2,1)S(1)}, u32[]{:S(2)}, u32[]{:S(2)}) collective-permute-start(bf16[96,256]{1,0:T(8,128)(2,1)S(1)} %get-tuple-element.29), channel_id=1, source_target_pairs={{0,6},{1,7},{2,4},{3,5},{4,2},{5,3},{6,0},{7,1},{8,14},{9,15},{10,... | collective-permute-start | bytes 147464 | tf_op jit(solution)/shard_map/ppermute | solution.py:21
  36.5 2.8 %collective-permute-start.15 = (bf16[96,256]{1,0:T(8,128)(2,1)S(1)}, bf16[96,256]{1,0:T(8,128)(2,1)S(1)}, u32[]{:S(2)}, u32[]{:S(2)}) collective-permute-start(bf16[96,256]{1,0:T(8,128)(2,1)S(1)} %outward.3), channel_id=1, source_target_pairs={{0,8},{1,9},{2,10},{3,11},{4,12},{5,13},{6,14},{7,15},{8,0},{9,1},... | collective-permute-start | bytes 147464 | tf_op jit(solution)/shard_map/ppermute | solution.py:21
  39.3 1.0 %narrow.1 = f32[1,128]{1,0:T(1,128)} custom-call(f32[8,1024]{1,0:T(8,128)S(1)} %get-tuple-element.33.mism_ref, f32[96,256]{1,0:T(8,128)S(1)} %get-tuple-element.30.first_ref.after_ref), custom_call_target="tpu_custom_call" | custom-call | flops 10000000000 | tf_op jit(solution)/shard_map/narrow/pallas_call | solution.py:40
  40.4 1.2 %collective-permute-done.15 = bf16[96,256]{1,0:T(8,128)(2,1)S(1)} collective-permute-done((bf16[96,256]{1,0:T(8,128)(2,1)S(1)}, bf16[96,256]{1,0:T(8,128)(2,1)S(1)}, u32[]{:S(2)}, u32[]{:S(2)}) %collective-permute-start.15) | collective-permute-done | bytes 49184 | tf_op jit(solution)/shard_map/ppermute | solution.py:21
  41.6 0.7 %convert_add_fusion = f32[96,256]{1,0:T(8,128)} fusion(f32[96,256]{1,0:T(8,128)S(1)} %outward.2, bf16[96,256]{1,0:T(8,128)(2,1)S(1)} %collective-permute-done.15), kind=kLoop, calls=%fused_computation | loop fusion | flops 49152 | bytes 245760 | tf_op jit(solution)/shard_map/add | solution.py:494
  (29 shorter events, 0.6 us)
Async XLA Ops:
  1.5 4.6 %collective-permute-start = (bf16[8,256]{1,0:T(8,128)(2,1)S(1)}, bf16[8,256]{1,0:T(8,128)(2,1)S(1)}, u32[]{:S(2)}, u32[]{:S(2)}) collective-permute-start(bf16[8,256]{1,0:T(8,128)(2,1)S(1)} %edge.1.after_ref), channel_id=1, source_target_pairs={{0,16},{16,0},{1,17},{17,1},{2,18},{18,2},{3,19},{19,3},{4,20},{20... | collective-permute-start | bytes 12296 | tf_op jit(solution)/shard_map/ppermute | solution.py:26
  4.5 0.8 %copy-start = (s32[8,8,32]{2,1,0:T(8,128)S(1)}, s32[8,8,32]{2,1,0:T(8,128)}, u32[]{:S(2)}) copy-start(s32[8,8,32]{2,1,0:T(8,128)} %mask_ref.1) | copy-start | bytes 24580
  6.1 5.3 %collective-permute-start.1 = (bf16[112,256]{1,0:T(8,128)(2,1)S(1)}, bf16[112,256]{1,0:T(8,128)(2,1)S(1)}, u32[]{:S(2)}, u32[]{:S(2)}) collective-permute-start(bf16[112,256]{1,0:T(8,128)(2,1)S(1)} %block.1.after_ref.near_ref), channel_id=1, source_target_pairs={{0,8},{1,9},{2,10},{3,11},{4,12},{5,13},{6,14},{7,15},{8,0},{9,1},... | collective-permute-start | bytes 172040 | tf_op jit(solution)/shard_map/ppermute | solution.py:21
  11.5 6.2 %copy-start.1 = (s32[128]{0:T(128)S(1)}, s32[128]{0:T(128)}, u32[]{:S(2)}) copy-start(s32[128]{0:T(128)} %param.10) | copy-start | bytes 1540
  11.5 6.2 %copy-start.2 = (f32[128]{0:T(128)S(1)}, f32[128]{0:T(128)}, u32[]{:S(2)}) copy-start(f32[128]{0:T(128)} %param.11) | copy-start | bytes 1540
  11.5 6.2 %copy-start.3 = (f32[128]{0:T(128)S(1)}, f32[128]{0:T(128)}, u32[]{:S(2)}) copy-start(f32[128]{0:T(128)} %param.12) | copy-start | bytes 1540
  11.5 6.7 %collective-permute-start.4 = (bf16[208,256]{1,0:T(8,128)(2,1)S(1)}, bf16[208,256]{1,0:T(8,128)(2,1)S(1)}, u32[]{:S(2)}, u32[]{:S(2)}) collective-permute-start(bf16[208,256]{1,0:T(8,128)(2,1)S(1)} %window.1.after_ref.refs_0_), channel_id=1, source_target_pairs={{0,6},{1,7},{2,4},{3,5},{4,2},{5,3},{6,0},{7,1},{8,14},{9,15},{10,... | collective-permute-start | bytes 319496 | tf_op jit(solution)/shard_map/ppermute | solution.py:21
  14.4 4.7 %collective-permute-start.3 = (bf16[208,256]{1,0:T(8,128)(2,1)S(1)}, bf16[208,256]{1,0:T(8,128)(2,1)S(1)}, u32[]{:S(2)}, u32[]{:S(2)}) collective-permute-start(bf16[208,256]{1,0:T(8,128)(2,1)S(1)} %window.1.after_ref.refs_0_), channel_id=1, source_target_pairs={{0,4},{1,5},{2,6},{3,7},{4,0},{5,1},{6,2},{7,3},{8,12},{9,13},{10,... | collective-permute-start | bytes 319496 | tf_op jit(solution)/shard_map/ppermute | solution.py:21
  14.9 4.7 %collective-permute-start.2 = (bf16[208,256]{1,0:T(8,128)(2,1)S(1)}, bf16[208,256]{1,0:T(8,128)(2,1)S(1)}, u32[]{:S(2)}, u32[]{:S(2)}) collective-permute-start(bf16[208,256]{1,0:T(8,128)(2,1)S(1)} %window.1.after_ref.refs_0_), channel_id=1, source_target_pairs={{0,2},{1,3},{2,0},{3,1},{4,6},{5,7},{6,4},{7,5},{8,10},{9,11},{10,... | collective-permute-start | bytes 319496 | tf_op jit(solution)/shard_map/ppermute | solution.py:21
  19.6 1.8 %collective-permute-start.5 = (bf16[832,256]{1,0:T(8,128)(2,1)S(1)}, bf16[832,256]{1,0:T(8,128)(2,1)S(1)}, u32[]{:S(2)}, u32[]{:S(2)}) collective-permute-start(bf16[832,256]{1,0:T(8,128)(2,1)S(1)} %pack.1.rest_ref), channel_id=1, source_target_pairs={{0,1},{1,0},{2,3},{3,2},{4,5},{5,4},{6,7},{7,6},{8,9},{9,8},{10,11... | collective-permute-start | bytes 1277960 | tf_op jit(solution)/shard_map/ppermute | solution.py:21
  23.8 1.3 %collective-permute-start.6 = (bf16[64,256]{1,0:T(8,128)(2,1)S(1)}, bf16[64,256]{1,0:T(8,128)(2,1)S(1)}, u32[]{:S(2)}, u32[]{:S(2)}) collective-permute-start(bf16[64,256]{1,0:T(8,128)(2,1)S(1)} %get-tuple-element.24), channel_id=1, source_target_pairs={{0,1},{1,0},{2,3},{3,2},{4,5},{5,4},{6,7},{7,6},{8,9},{9,8},{10,11... | collective-permute-start | bytes 98312 | tf_op jit(solution)/shard_map/ppermute | solution.py:21
  25.1 1.8 %collective-permute-start.7 = (bf16[8,96,256]{2,1,0:T(8,128)(2,1)S(1)}, bf16[8,96,256]{2,1,0:T(8,128)(2,1)S(1)}, u32[]{:S(2)}, u32[]{:S(2)}) collective-permute-start(bf16[8,96,256]{2,1,0:T(8,128)(2,1)S(1)} %gate.1), channel_id=1, source_target_pairs={{0,1},{1,0},{2,3},{3,2},{4,5},{5,4},{6,7},{7,6},{8,9},{9,8},{10,11... | collective-permute-start | bytes 1179656 | tf_op jit(solution)/shard_map/ppermute | solution.py:21
  25.4 3.9 %collective-permute-start.8 = (bf16[64,256]{1,0:T(8,128)(2,1)S(1)}, bf16[64,256]{1,0:T(8,128)(2,1)S(1)}, u32[]{:S(2)}, u32[]{:S(2)}) collective-permute-start(bf16[64,256]{1,0:T(8,128)(2,1)S(1)} %rims.1.after_ref), channel_id=1, source_target_pairs={{0,16},{16,0},{1,17},{17,1},{2,18},{18,2},{3,19},{19,3},{4,20},{20... | collective-permute-start | bytes 98312 | tf_op jit(solution)/shard_map/ppermute | solution.py:26
  29.3 5.8 %collective-permute-start.13 = (bf16[96,256]{1,0:T(8,128)(2,1)S(1)}, bf16[96,256]{1,0:T(8,128)(2,1)S(1)}, u32[]{:S(2)}, u32[]{:S(2)}) collective-permute-start(bf16[96,256]{1,0:T(8,128)(2,1)S(1)} %get-tuple-element.31), channel_id=1, source_target_pairs={{0,4},{1,5},{2,6},{3,7},{4,0},{5,1},{6,2},{7,3},{8,12},{9,13},{10,... | collective-permute-start | bytes 147464 | tf_op jit(solution)/shard_map/ppermute | solution.py:21
  31.0 5.5 %collective-permute-start.14 = (bf16[96,256]{1,0:T(8,128)(2,1)S(1)}, bf16[96,256]{1,0:T(8,128)(2,1)S(1)}, u32[]{:S(2)}, u32[]{:S(2)}) collective-permute-start(bf16[96,256]{1,0:T(8,128)(2,1)S(1)} %get-tuple-element.32), channel_id=1, source_target_pairs={{0,6},{1,7},{2,4},{3,5},{4,2},{5,3},{6,0},{7,1},{8,14},{9,15},{10,... | collective-permute-start | bytes 147464 | tf_op jit(solution)/shard_map/ppermute | solution.py:21
  31.4 5.0 %collective-permute-start.12 = (bf16[96,256]{1,0:T(8,128)(2,1)S(1)}, bf16[96,256]{1,0:T(8,128)(2,1)S(1)}, u32[]{:S(2)}, u32[]{:S(2)}) collective-permute-start(bf16[96,256]{1,0:T(8,128)(2,1)S(1)} %get-tuple-element.25.after_ref), channel_id=1, source_target_pairs={{0,2},{1,3},{2,0},{3,1},{4,6},{5,7},{6,4},{7,5},{8,10},{9,11},{10,... | collective-permute-start | bytes 147464 | tf_op jit(solution)/shard_map/ppermute | solution.py:21
  32.9 7.4 %collective-permute-start.9 = (bf16[96,256]{1,0:T(8,128)(2,1)S(1)}, bf16[96,256]{1,0:T(8,128)(2,1)S(1)}, u32[]{:S(2)}, u32[]{:S(2)}) collective-permute-start(bf16[96,256]{1,0:T(8,128)(2,1)S(1)} %get-tuple-element.27), channel_id=1, source_target_pairs={{0,2},{1,3},{2,0},{3,1},{4,6},{5,7},{6,4},{7,5},{8,10},{9,11},{10,... | collective-permute-start | bytes 147464 | tf_op jit(solution)/shard_map/ppermute | solution.py:21
  33.5 6.8 %collective-permute-start.10 = (bf16[96,256]{1,0:T(8,128)(2,1)S(1)}, bf16[96,256]{1,0:T(8,128)(2,1)S(1)}, u32[]{:S(2)}, u32[]{:S(2)}) collective-permute-start(bf16[96,256]{1,0:T(8,128)(2,1)S(1)} %get-tuple-element.28), channel_id=1, source_target_pairs={{0,4},{1,5},{2,6},{3,7},{4,0},{5,1},{6,2},{7,3},{8,12},{9,13},{10,... | collective-permute-start | bytes 147464 | tf_op jit(solution)/shard_map/ppermute | solution.py:21
  35.1 5.2 %collective-permute-start.11 = (bf16[96,256]{1,0:T(8,128)(2,1)S(1)}, bf16[96,256]{1,0:T(8,128)(2,1)S(1)}, u32[]{:S(2)}, u32[]{:S(2)}) collective-permute-start(bf16[96,256]{1,0:T(8,128)(2,1)S(1)} %get-tuple-element.29), channel_id=1, source_target_pairs={{0,6},{1,7},{2,4},{3,5},{4,2},{5,3},{6,0},{7,1},{8,14},{9,15},{10,... | collective-permute-start | bytes 147464 | tf_op jit(solution)/shard_map/ppermute | solution.py:21
  36.5 5.1 %collective-permute-start.15 = (bf16[96,256]{1,0:T(8,128)(2,1)S(1)}, bf16[96,256]{1,0:T(8,128)(2,1)S(1)}, u32[]{:S(2)}, u32[]{:S(2)}) collective-permute-start(bf16[96,256]{1,0:T(8,128)(2,1)S(1)} %outward.3), channel_id=1, source_target_pairs={{0,8},{1,9},{2,10},{3,11},{4,12},{5,13},{6,14},{7,15},{8,0},{9,1},... | collective-permute-start | bytes 147464 | tf_op jit(solution)/shard_map/ppermute | solution.py:21
